TPU v7x, 32 devices: a whole 2x2x4 slice. The times are simulated.
32 devices in a mesh: fsdp: 4 (over y, x), seq: 8 (over z, core).
Axes of the slice: x: 2, y: 2, z: 4, core: 2. Of those that a mesh axis runs over, the one named last changes fastest.
Arguments:
- tokens: bfloat16 [4, 1024, 2048], P('fsdp', 'seq'), may hold values from -6 to 6
- teacher: bfloat16 [4, 1024, 2048], P('fsdp', 'seq'), may hold values from -6 to 6
- segments: int32 [4, 1024], P('fsdp', 'seq'), may hold values from 0 to 255, as said below
- valid: int32 [4, 1024], P('fsdp', 'seq'), may hold values from 0 to 1, as said below
- query_weight: bfloat16 [2048, 2048], P(('fsdp', 'seq')), may hold values from -0.125 to 0.125
- key_weight: bfloat16 [2048, 2048], P(('fsdp', 'seq')), may hold values from -0.125 to 0.125
- value_weight: bfloat16 [2048, 2048], P(('fsdp', 'seq')), may hold values from -0.125 to 0.125
- output_weight: bfloat16 [2048, 2048], P(('fsdp', 'seq')), may hold values from -0.5 to 0.5
- attention_gain: bfloat16 [2048], P(('fsdp', 'seq')), may hold values from 0.25 to 1.75
- gate_weight: bfloat16 [2048, 8192], P(('fsdp', 'seq')), may hold values from -0.125 to 0.125
- up_weight: bfloat16 [2048, 8192], P(('fsdp', 'seq')), may hold values from -0.125 to 0.125
- down_weight: bfloat16 [8192, 2048], P(('fsdp', 'seq')), may hold values from -0.125 to 0.125
- mlp_gain: bfloat16 [2048], P(('fsdp', 'seq')), may hold values from 0.25 to 1.75
Outputs:
- output: bfloat16 [4, 1024, 2048], P('fsdp', 'seq')
- loss: float32 [], replicated
- input_grad: float32 [4, 1024, 2048], P('fsdp', 'seq')
- query_weight_grad: float32 [2048, 2048], P(('fsdp', 'seq'))
- key_weight_grad: float32 [2048, 2048], P(('fsdp', 'seq'))
- value_weight_grad: float32 [2048, 2048], P(('fsdp', 'seq'))
- output_weight_grad: float32 [2048, 2048], P(('fsdp', 'seq'))
- attention_gain_grad: float32 [2048], P(('fsdp', 'seq'))
- gate_weight_grad: float32 [2048, 8192], P(('fsdp', 'seq'))
- up_weight_grad: float32 [2048, 8192], P(('fsdp', 'seq'))
- down_weight_grad: float32 [8192, 2048], P(('fsdp', 'seq'))
- mlp_gain_grad: float32 [2048], P(('fsdp', 'seq'))
Inputs may be any that keep to these rules, and one draw needn't show every extreme that they name: `segments`: within a sequence the document numbers start at 0 and never fall, and a document begins only at a place that is a multiple of 4; when an index of fsdp holds two or more sequences, one of them is a single document (with one sequence per index, as here, this does not occur). The first token of every sequence is valid.
All inputs are finite; a program needn't handle non-finite values.
Results may differ from a plain program's by a relative error of at most 0.012.
The roundings to bfloat16 on the way count: a program that leaves them out, or rounds other values in their place, can miss the bound.
Values may be sent and summed in bfloat16 or wider, within the bound.
No kernel may reach another device: no remote copies, remote signals or barrier semaphores. Data moves between devices by JAX's collectives and lax.ppermute only.
A program may use at most 640 MiB of HBM per device.

v0:
```python
import jax
import jax.numpy as jnp
from jax import lax
from jax.sharding import PartitionSpec as P

H = 32
HD = 64


EPSILON = 1e-05
ROPE_BASE = 130000.0
MASKED = -1e30


def rms_norm(values, gain_vector):
    return (
        values
        * lax.rsqrt(jnp.mean(values * values, axis=-1, keepdims=True) + EPSILON)
        * gain_vector
    )


def rotate(values, positions):
    half_width = values.shape[-1] // 2
    exponents = jnp.arange(half_width).astype(jnp.float32) * (2.0 / values.shape[-1])
    inverse = jnp.power(ROPE_BASE, -exponents)
    angles = positions[:, None] * inverse[None, :]
    cosine = jnp.cos(angles)[:, None, :]
    sine_part = jnp.sin(angles)[:, None, :]
    leading = values[..., :half_width]
    trailing = values[..., half_width:]
    return jnp.concatenate(
        [leading * cosine - trailing * sine_part, trailing * cosine + leading * sine_part], axis=-1
    )


def matmul(left_side, right_side):
    return jnp.dot(left_side, right_side, preferred_element_type=jnp.float32)


def transposed(left_side, right_side):
    return lax.dot_general(
        left_side, right_side, (((0,), (0,)), ((), ())), preferred_element_type=jnp.float32
    )


def against(left_side, right_side):
    return lax.dot_general(
        left_side, right_side, (((1,), (1,)), ((), ())), preferred_element_type=jnp.float32
    )


def gated(gate_value, up_value):
    return gate_value * jax.nn.sigmoid(gate_value) * up_value


def block_scores(query_block, key_heads, segment, first_row, score_scale):
    block_rows = query_block.shape[0]
    row_places = first_row + jnp.arange(block_rows, dtype=jnp.int32)
    key_places = jnp.arange(key_heads.shape[0], dtype=jnp.int32)
    segment_rows = lax.dynamic_slice_in_dim(segment, first_row, block_rows, 0)
    allowed = (segment_rows[:, None] == segment[None, :]) & (
        key_places[None, :] <= row_places[:, None]
    )
    scores = (
        jnp.einsum("qhd,khd->hqk", query_block, key_heads, preferred_element_type=jnp.float32)
        * score_scale
    )
    return jnp.where(allowed[None], scores, MASKED)


def body(
    tokens,
    teacher,
    segments,
    valid,
    query_weight,
    key_weight,
    value_weight,
    output_weight,
    attention_gain,
    gate_weight,
    up_weight,
    down_weight,
    mlp_gain,
):
    sequences, local_rows, model_width = tokens.shape
    groups = lax.axis_size("seq")
    local_heads = H // groups
    length = local_rows * groups
    block_rows = min(512, length)
    blocks = length // block_rows
    total_rows = sequences * local_rows
    score_scale = HD ** (-0.5)
    attention_full = (
        lax.all_gather(query_weight, ("fsdp", "seq"), axis=0, tiled=True),
        lax.all_gather(key_weight, ("fsdp", "seq"), axis=0, tiled=True),
        lax.all_gather(value_weight, ("fsdp", "seq"), axis=0, tiled=True),
        lax.all_gather(output_weight, ("fsdp", "seq"), axis=0, tiled=True),
        lax.all_gather(attention_gain, ("fsdp", "seq"), axis=0, tiled=True),
    )
    mlp_full = (
        lax.all_gather(gate_weight, ("fsdp", "seq"), axis=0, tiled=True),
        lax.all_gather(up_weight, ("fsdp", "seq"), axis=0, tiled=True),
        lax.all_gather(down_weight, ("fsdp", "seq"), axis=0, tiled=True),
        lax.all_gather(mlp_gain, ("fsdp", "seq"), axis=0, tiled=True),
    )
    inputs = tokens.reshape(total_rows, model_width).astype(jnp.float32)
    first_gain = attention_full[4].astype(jnp.float32)
    normed = rms_norm(inputs, first_gain).astype(jnp.bfloat16)
    positions = (
        lax.axis_index("seq") * local_rows + jnp.arange(local_rows, dtype=jnp.int32)
    ).astype(jnp.float32)
    head_shape = (sequences, local_rows, H, HD)
    query_pre = matmul(normed, attention_full[0]).reshape(head_shape)
    key_pre = matmul(normed, attention_full[1]).reshape(head_shape)
    value_heads = matmul(normed, attention_full[2]).astype(jnp.bfloat16).reshape(head_shape)

    def rotated(values):
        return rotate(values, positions)

    query_rot, query_pull = jax.vjp(rotated, query_pre)
    key_rot, key_pull = jax.vjp(rotated, key_pre)
    query_all, key_all, value_all = (
        lax.all_to_all(
            query_rot.astype(jnp.bfloat16), "seq", split_axis=2, concat_axis=1, tiled=True
        ),
        lax.all_to_all(
            key_rot.astype(jnp.bfloat16), "seq", split_axis=2, concat_axis=1, tiled=True
        ),
        lax.all_to_all(value_heads, "seq", split_axis=2, concat_axis=1, tiled=True),
    )
    segment_all = lax.all_gather(segments, "seq", axis=1, tiled=True)
    query_blocks = query_all.reshape(sequences * blocks, block_rows, local_heads, HD)
    block_index = jnp.arange(sequences * blocks, dtype=jnp.int32)

    def attend(item_pair):
        query_block, which = item_pair
        seq_id = which // blocks
        first_row = which % blocks * block_rows
        scores = block_scores(
            query_block, key_all[seq_id], segment_all[seq_id], first_row, score_scale
        )
        row_max = jnp.max(scores, axis=-1, keepdims=True)
        exponent = jnp.exp(scores - row_max)
        row_total = jnp.sum(exponent, axis=-1, keepdims=True)
        weights = (exponent / row_total).astype(jnp.bfloat16)
        mixed_block = jnp.einsum(
            "hqk,khd->qhd", weights, value_all[seq_id], preferred_element_type=jnp.float32
        )
        return (mixed_block.astype(jnp.bfloat16), (row_max + jnp.log(row_total))[..., 0])

    mixed_blocks, log_totals = lax.map(attend, (query_blocks, block_index))
    mixed_heads = mixed_blocks.reshape(sequences, length, local_heads, HD)
    mixed = lax.all_to_all(mixed_heads, "seq", split_axis=1, concat_axis=2, tiled=True).reshape(
        total_rows, model_width
    )
    after_attention = inputs + matmul(mixed, attention_full[3])
    second_gain = mlp_full[3].astype(jnp.float32)
    normed_two = rms_norm(after_attention, second_gain).astype(jnp.bfloat16)
    gate_value = matmul(normed_two, mlp_full[0])
    up_value = matmul(normed_two, mlp_full[1])
    hidden = gated(gate_value, up_value).astype(jnp.bfloat16)
    result = after_attention + matmul(hidden, mlp_full[2])
    keep_mask = valid.reshape(total_rows).astype(jnp.float32)
    difference = result - teacher.reshape(total_rows, model_width).astype(jnp.float32)
    count, error_sum = lax.psum(
        (jnp.sum(keep_mask), jnp.sum(keep_mask[:, None] * difference * difference)), ("fsdp", "seq")
    )
    loss = error_sum / count
    grad_result = 2.0 / count * keep_mask[:, None] * difference
    grad_branch = grad_result.astype(jnp.bfloat16)
    grad_hidden = against(grad_branch, mlp_full[2])
    unused, gate_pull = jax.vjp(gated, gate_value, up_value)
    grad_gate, grad_upward = gate_pull(grad_hidden)
    gate_up_grad = jnp.concatenate(
        [grad_gate.astype(jnp.bfloat16), grad_upward.astype(jnp.bfloat16)], axis=1
    )
    hidden_width = grad_gate.shape[1]
    grad_normed_two = against(gate_up_grad[:, :hidden_width], mlp_full[0]) + against(
        gate_up_grad[:, hidden_width:], mlp_full[1]
    )
    unused, second_pull = jax.vjp(rms_norm, after_attention, second_gain)
    grad_after, second_gain_grad = second_pull(grad_normed_two)
    grad_after = grad_after + grad_result
    gate_up_sum = lax.psum_scatter(
        transposed(normed_two, gate_up_grad), ("fsdp", "seq"), scatter_dimension=0, tiled=True
    )
    down_sum = lax.psum_scatter(
        transposed(hidden, grad_branch), ("fsdp", "seq"), scatter_dimension=0, tiled=True
    )
    grad_attention_out = grad_after.astype(jnp.bfloat16)
    grad_mixed = (
        against(grad_attention_out, attention_full[3]).astype(jnp.bfloat16).reshape(head_shape)
    )
    grad_mixed_all = lax.all_to_all(grad_mixed, "seq", split_axis=2, concat_axis=1, tiled=True)
    grad_blocks = grad_mixed_all.reshape(sequences * blocks, block_rows, local_heads, HD)

    def attend_back(running, item_tuple):
        query_block, grad_block, log_total, which = item_tuple
        seq_id = which // blocks
        first_row = which % blocks * block_rows
        key_heads = key_all[seq_id]
        scores = block_scores(query_block, key_heads, segment_all[seq_id], first_row, score_scale)
        probs = jnp.exp(scores - log_total[:, :, None])
        grad_probs = jnp.einsum(
            "qhd,khd->hqk", grad_block, value_all[seq_id], preferred_element_type=jnp.float32
        )
        inner = jnp.sum(probs * grad_probs, axis=-1, keepdims=True)
        grad_scores = (probs * (grad_probs - inner)).astype(jnp.bfloat16)
        grad_query = (
            jnp.einsum("hqk,khd->qhd", grad_scores, key_heads, preferred_element_type=jnp.float32)
            * score_scale
        )
        key_part = (
            jnp.einsum("hqk,qhd->khd", grad_scores, query_block, preferred_element_type=jnp.float32)
            * score_scale
        )
        value_part = jnp.einsum(
            "hqk,qhd->khd",
            probs.astype(jnp.bfloat16),
            grad_block,
            preferred_element_type=jnp.float32,
        )
        grad_keys, grad_values = running
        grad_keys = lax.dynamic_update_index_in_dim(
            grad_keys,
            lax.dynamic_index_in_dim(grad_keys, seq_id, 0, keepdims=False) + key_part,
            seq_id,
            0,
        )
        grad_values = lax.dynamic_update_index_in_dim(
            grad_values,
            lax.dynamic_index_in_dim(grad_values, seq_id, 0, keepdims=False) + value_part,
            seq_id,
            0,
        )
        return ((grad_keys, grad_values), grad_query)

    empty_heads = jnp.zeros((sequences, length, local_heads, HD), jnp.float32)
    (grad_keys, grad_values), grad_queries = lax.scan(
        attend_back,
        (empty_heads, empty_heads),
        (query_blocks, grad_blocks, log_totals, block_index),
    )
    grad_queries = grad_queries.reshape(sequences, length, local_heads, HD).astype(jnp.bfloat16)
    query_back, key_back, value_back = (
        lax.all_to_all(grad_queries, "seq", split_axis=1, concat_axis=2, tiled=True),
        lax.all_to_all(
            grad_keys.astype(jnp.bfloat16), "seq", split_axis=1, concat_axis=2, tiled=True
        ),
        lax.all_to_all(
            grad_values.astype(jnp.bfloat16), "seq", split_axis=1, concat_axis=2, tiled=True
        ),
    )
    grad_query_pre = (
        query_pull(query_back.astype(jnp.float32))[0]
        .astype(jnp.bfloat16)
        .reshape(total_rows, model_width)
    )
    grad_key_pre = (
        key_pull(key_back.astype(jnp.float32))[0]
        .astype(jnp.bfloat16)
        .reshape(total_rows, model_width)
    )
    grad_value_pre = value_back.reshape(total_rows, model_width)
    grad_normed = (
        against(grad_query_pre, attention_full[0])
        + against(grad_key_pre, attention_full[1])
        + against(grad_value_pre, attention_full[2])
    )
    unused, first_pull = jax.vjp(rms_norm, inputs, first_gain)
    grad_inputs, first_gain_grad = first_pull(grad_normed)
    grad_inputs = grad_inputs + grad_after
    projection_grads = jnp.concatenate([grad_query_pre, grad_key_pre, grad_value_pre], axis=1)
    attention_sum = lax.psum_scatter(
        jnp.concatenate(
            [transposed(normed, projection_grads), transposed(mixed, grad_attention_out)], axis=1
        ),
        ("fsdp", "seq"),
        scatter_dimension=0,
        tiled=True,
    )
    gain_first, gain_second = (
        lax.psum_scatter(first_gain_grad, ("fsdp", "seq"), scatter_dimension=0, tiled=True),
        lax.psum_scatter(second_gain_grad, ("fsdp", "seq"), scatter_dimension=0, tiled=True),
    )
    output_shape = (sequences, local_rows, model_width)
    return (
        result.reshape(output_shape).astype(jnp.bfloat16),
        loss,
        grad_inputs.reshape(output_shape),
        attention_sum[:, :model_width],
        attention_sum[:, model_width : 2 * model_width],
        attention_sum[:, 2 * model_width : 3 * model_width],
        attention_sum[:, 3 * model_width :],
        gain_first,
        gate_up_sum[:, :hidden_width],
        gate_up_sum[:, hidden_width:],
        down_sum,
        gain_second,
    )


def solution(mesh):
    placed = (
        P("fsdp", "seq", None),
        P("fsdp", "seq", None),
        P("fsdp", "seq"),
        P("fsdp", "seq"),
        P(("fsdp", "seq"), None),
        P(("fsdp", "seq"), None),
        P(("fsdp", "seq"), None),
        P(("fsdp", "seq"), None),
        P(("fsdp", "seq")),
        P(("fsdp", "seq"), None),
        P(("fsdp", "seq"), None),
        P(("fsdp", "seq"), None),
        P(("fsdp", "seq")),
    )
    return jax.shard_map(
        body,
        mesh=mesh,
        in_specs=placed,
        out_specs=(
            P("fsdp", "seq", None),
            P(),
            P("fsdp", "seq", None),
            P(("fsdp", "seq"), None),
            P(("fsdp", "seq"), None),
            P(("fsdp", "seq"), None),
            P(("fsdp", "seq"), None),
            P(("fsdp", "seq")),
            P(("fsdp", "seq"), None),
            P(("fsdp", "seq"), None),
            P(("fsdp", "seq"), None),
            P(("fsdp", "seq")),
        ),
        check_vma=False,
    )
```

profile of v0, /device:TPU:0, one launch (start us, length us, event | category | flops | bytes accessed | tf_op | source)
XLA Modules:
  0.0 4379.5 jit_solution(16597896884502710594)
XLA Ops:
  13.6 42.3 all-reduce.10
  57.4 33.8 all-gather.12.cloned.1.call-done
  100.6 73.9 %all-gather.10.cloned.1.call-done = bf16[2048,2048]{1,0:T(8,128)(2,1)} async-done(((bf16[64,2048]{1,0:T(8,128)(2,1)}), bf16[2048,2048]{1,0:T(8,128)(2,1)}) %all-gather.10.cloned.1.call-update) | async-done | bytes 8388624 | tf_op jit(solution)/shard_map/all_gather | solution.py:97
  174.4 12.4 copy.107
  186.8 66.6 %all-gather.8.cloned.1.call-done = bf16[2048,2048]{1,0:T(8,128)(2,1)} async-done(((bf16[64,2048]{1,0:T(8,128)(2,1)}), bf16[2048,2048]{1,0:T(8,128)(2,1)}) %all-gather.8.cloned.1.call-update) | async-done | bytes 8388624 | tf_op jit(solution)/shard_map/all_gather | solution.py:96
  253.4 12.4 copy.104
  279.9 25.1 all-to-all-done.1
  308.6 24.6 all_gather.30
  337.7 20.5 while.30
  370.2 46.6 %psum.15 = f32[]{:T(128)} all-reduce(f32[]{:T(128)} %convert_reduce_fusion), channel_id=1, replica_groups=mesh['fsdp'=4,'seq'=8] {'fsdp','seq'}, use_global_device_ids=true, to_apply=%region_9.10 | all-reduce | flops 1 | bytes 8 | tf_op jit(solution)/shard_map/psum | solution.py:167
  428.6 127.8 %all-gather.16.cloned.1.call-done = bf16[2048,8192]{1,0:T(8,128)(2,1)} async-done(((bf16[64,8192]{1,0:T(8,128)(2,1)}), bf16[2048,8192]{1,0:T(8,128)(2,1)}) %all-gather.16.cloned.1.call-update) | async-done | bytes 33554448 | tf_op jit(solution)/shard_map/all_gather | solution.py:103
  556.4 17.9 fusion.97
  574.3 177.9 %all-gather.18.cloned.1.call-done = bf16[2048,8192]{1,0:T(8,128)(2,1)} async-done(((bf16[64,8192]{1,0:T(8,128)(2,1)}), bf16[2048,8192]{1,0:T(8,128)(2,1)}) %all-gather.18.cloned.1.call-update) | async-done | bytes 33554448 | tf_op jit(solution)/shard_map/all_gather | solution.py:104
  752.2 20.8 multiply_convert_fusion.2
  773.1 175.1 %all-gather.20.cloned.1.call-done = bf16[8192,2048]{1,0:T(8,128)(2,1)} async-done(((bf16[256,2048]{1,0:T(8,128)(2,1)}), bf16[8192,2048]{1,0:T(8,128)(2,1)}) %all-gather.20.cloned.1.call-update) | async-done | bytes 33554448 | tf_op jit(solution)/shard_map/all_gather | solution.py:105
  948.2 16.8 multiply_convert_fusion.4
  965.0 19.9 multiply_convert_fusion.1
  984.9 45.5 %fusion.56 = f32[2048,16384]{1,0:T(8,128)} fusion(bf16[128,2048]{1,0:T(8,128)(2,1)S(1)} %multiply_convert_fusion.3, bf16[128,8192]{1,0:T(8,128)(2,1)} %get-tuple-element.389, bf16[128,8192]{1,0:T(8,128)(2,1)} %get-tuple-element.390), kind=kOutput, calls=%fused_computation.67 | convolution fusion | flops 8598323200 | bytes 138936320 | tf_op jit(solution)/shard_map/dot_general | solution.py:42
  1030.5 18.1 fusion.98
  1048.6 18.2 multiply_reduce_fusion.1
  1082.3 20.5 all-to-all-done.4
  1108.4 30.2 while.31
  1151.2 18.3 all-to-all-done.5
  1177.2 17.7 all-to-all-done.6
  1198.4 8.1 fusion.84
  1225.0 21.9 fusion.61
  1246.9 45.0 %pad_maximum_fusion = f32[2048,8192]{1,0:T(8,128)} fusion(f32[2048,2048]{1,0:T(8,128)} %fusion.84, f32[2048,6144]{1,0:T(8,128)} %fusion.61), kind=kLoop, calls=%fused_computation.62 | loop fusion | flops 16777216 | bytes 134217728 | tf_op jit(solution)/shard_map/concatenate | solution.py:277
  1292.0 26.8 fusion.100
  1336.9 41.1 all-reduce.9
  1383.0 1568.6 %all-reduce.13.cloned.1.call-done = f32[2048,16384]{1,0:T(8,128)} async-done(((f32[2048,16384]{1,0:T(8,128)}), f32[2048,16384]{1,0:T(8,128)}) %all-reduce.13.cloned.1.call-update) | async-done | bytes 134217744
  2956.5 706.2 %reduce-scatter.3.cloned.1.call-done = f32[64,8192]{1,0:T(8,128)} async-done(((f32[2048,8192]{1,0:T(8,128)}), f32[64,8192]{1,0:T(8,128)}) %reduce-scatter.3.cloned.1.call-update) | async-done | bytes 2097168 | tf_op jit(solution)/shard_map/reduce_scatter | solution.py:276
  3665.5 705.8 %reduce-scatter.5.cloned.1.call-done = f32[256,2048]{1,0:T(8,128)} async-done(((f32[8192,2048]{1,0:T(8,128)}), f32[256,2048]{1,0:T(8,128)}) %reduce-scatter.5.cloned.1.call-update) | async-done | bytes 2097168 | tf_op jit(solution)/shard_map/reduce_scatter | solution.py:189
  (240 shorter events, 197.2 us)
Async XLA Ops:
  7.2 84.0 %all-gather.12.cloned.1.call-start = ((), (), s32[]{:S(2)}) async-start(), calls=%async_computation.12 | async-start | bytes 8650752 | tf_op jit(solution)/shard_map/all_gather | solution.py:98
  7.9 166.5 %all-gather.10.cloned.1.call-start = ((), (), s32[]{:S(2)}) async-start(), calls=%async_computation.11 | async-start | bytes 8650752 | tf_op jit(solution)/shard_map/all_gather | solution.py:97
  8.7 244.8 %all-gather.8.cloned.1.call-start = ((), (), s32[]{:S(2)}) async-start(), calls=%async_computation.10 | async-start | bytes 8650752 | tf_op jit(solution)/shard_map/all_gather | solution.py:96
  9.4 413.6 %all-gather.14.cloned.1.call-start = ((), (), s32[]{:S(2)}) async-start(), calls=%async_computation.13 | async-start | bytes 8650752 | tf_op jit(solution)/shard_map/all_gather | solution.py:99
  10.0 546.4 %all-gather.16.cloned.1.call-start = ((), (), s32[]{:S(2)}) async-start(), calls=%async_computation.14 | async-start | bytes 34603008 | tf_op jit(solution)/shard_map/all_gather | solution.py:103
  10.6 741.7 %all-gather.18.cloned.1.call-start = ((), (), s32[]{:S(2)}) async-start(), calls=%async_computation.15 | async-start | bytes 34603008 | tf_op jit(solution)/shard_map/all_gather | solution.py:104
  11.1 937.1 %all-gather.20.cloned.1.call-start = ((), (), s32[]{:S(2)}) async-start(), calls=%async_computation.16 | async-start | bytes 34603008 | tf_op jit(solution)/shard_map/all_gather | solution.py:105
  55.9 215.9 %copy-start.18 = (f32[2048]{0:T(1024)}, f32[2048]{0:T(1024)S(1)}, u32[]{:S(2)}) copy-start(f32[2048]{0:T(1024)S(1)} %convert_element_type.201) | copy-start | bytes 24580
  57.2 39.9 copy-start.36
  57.2 214.7 %copy-start.31 = (f32[128]{0:T(128)}, f32[128]{0:T(128)S(1)}, u32[]{:S(2)}) copy-start(f32[128]{0:T(128)S(1)} %fusion.91) | copy-start | bytes 1540
  57.4 217.1 %copy-start.25 = (f32[128,32]{0,1:T(8,128)}, f32[128,32]{0,1:T(8,128)S(1)}, u32[]{:S(2)}) copy-start(f32[128,32]{0,1:T(8,128)S(1)} %get-tuple-element.410) | copy-start | bytes 49156
  57.4 217.1 %copy-start.27 = (f32[128,32]{0,1:T(8,128)}, f32[128,32]{0,1:T(8,128)S(1)}, u32[]{:S(2)}) copy-start(f32[128,32]{0,1:T(8,128)S(1)} %get-tuple-element.411) | copy-start | bytes 49156
  97.1 178.5 %all-to-all-start.2 = ((bf16[1,128,32,64]{1,3,0,2:T(8,128)(2,1)}), bf16[1,128,32,64]{1,3,0,2:T(8,128)(2,1)S(1)}, u32[]{:S(2)}, u32[]{:S(2)}) async-start(bf16[1,128,32,64]{1,3,0,2:T(8,128)(2,1)} %bitcast.41), calls=%async_computation.2 | async-start | bytes 1048576 | tf_op jit(solution)/shard_map/all_to_all | solution.py:131
  275.6 29.5 all-to-all-start.1
  305.0 32.1 all-to-all-start
  359.6 57.1 %copy-start.29 = (f32[2,4,512]{2,1,0:T(4,128)}, f32[2,4,512]{2,1,0:T(4,128)S(1)}, u32[]{:S(2)}) copy-start(f32[2,4,512]{2,1,0:T(4,128)S(1)} %get-tuple-element.593) | copy-start | bytes 49156
  359.6 63.4 %copy-start.7 = (bf16[1,1024,4,64]{1,3,2,0:T(8,128)(2,1)}, bf16[1,1024,4,64]{1,3,2,0:T(8,128)(2,1)S(1)}, u32[]{:S(2)}) copy-start(bf16[1,1024,4,64]{1,3,2,0:T(8,128)(2,1)S(1)} %get-tuple-element.652) | copy-start | bytes 1572868
  359.7 68.3 %copy-start = (bf16[1,1024,4,64]{1,3,2,0:T(8,128)(2,1)}, bf16[1,1024,4,64]{1,3,2,0:T(8,128)(2,1)S(1)}, u32[]{:S(2)}) copy-start(bf16[1,1024,4,64]{1,3,2,0:T(8,128)(2,1)S(1)} %get-tuple-element.644) | copy-start | bytes 1572868
  359.7 68.3 %copy-start.4 = (bf16[2,512,4,64]{1,3,2,0:T(8,128)(2,1)}, bf16[2,512,4,64]{1,3,2,0:T(8,128)(2,1)S(1)}, u32[]{:S(2)}) copy-start(bf16[2,512,4,64]{1,3,2,0:T(8,128)(2,1)S(1)} %get-tuple-element.649) | copy-start | bytes 1572868
  363.0 54.5 %all-to-all-start.3 = ((bf16[8,2,16384]{2,1,0:T(2,128)(2,1)}), bf16[8,2,16384]{2,1,0:T(2,128)(2,1)}, u32[]{:S(2)}, u32[]{:S(2)}) async-start(bf16[8,2,16384]{2,1,0:T(2,128)(2,1)} %reshape.506), calls=%async_computation.3 | async-start | bytes 1048576 | tf_op jit(solution)/shard_map/all_to_all | solution.py:155
  369.5 2582.0 %all-reduce.13.cloned.1.call-start = ((), (), s32[]{:S(2)}) async-start(), calls=%async_computation.19 | async-start | bytes 268435456
  574.3 373.9 %copy-start.17 = (bf16[1,128,2048]{2,1,0:T(8,128)(2,1)S(1)}, bf16[1,128,2048]{2,1,0:T(8,128)(2,1)}, u32[]{:S(2)}) copy-start(bf16[1,128,2048]{2,1,0:T(8,128)(2,1)} %param.18) | copy-start | bytes 1572868
  1070.8 37.5 copy-start.30
  1078.7 24.1 all-to-all-start.4
  1138.6 59.9 %copy-start.10 = (f32[128,2048]{1,0:T(8,128)S(1)}, f32[128,2048]{1,0:T(8,128)}, u32[]{:S(2)}) copy-start(f32[128,2048]{1,0:T(8,128)} %copy-done.9) | copy-start | bytes 3145732
  1138.6 59.8 %copy-start.13 = (bf16[1,128,8,4,64]{1,4,3,2,0:T(8,128)(2,1)S(1)}, bf16[1,128,8,4,64]{1,4,3,2,0:T(8,128)(2,1)}, u32[]{:S(2)}) copy-start(bf16[1,128,8,4,64]{1,4,3,2,0:T(8,128)(2,1)} %copy-done.12) | copy-start | bytes 1572868
  1144.7 24.8 all-to-all-start.5
  1169.5 25.4 all-to-all-start.6
  1194.9 24.8 all-to-all-start.7
  1198.4 2464.3 %reduce-scatter.3.cloned.1.call-start = ((), (), s32[]{:S(2)}) async-start(), calls=%async_computation.17 | async-start | bytes 69206016 | tf_op jit(solution)/shard_map/reduce_scatter | solution.py:276
  1291.9 3079.4 %reduce-scatter.5.cloned.1.call-start = ((), (), s32[]{:S(2)}) async-start(), calls=%async_computation.18 | async-start | bytes 69206016 | tf_op jit(solution)/shard_map/reduce_scatter | solution.py:189
  1332.9 47.6 %copy-start.37 = (f32[128]{0:T(128)S(1)}, f32[128]{0:T(128)}, u32[]{:S(2)}) copy-start(f32[128]{0:T(128)} %copy-done.36) | copy-start | bytes 1540
  (32 other events, 454.1 us)
Sparse Core Ops, SparseCore 0:
  11.0 80.1 all-gather.11
  94.2 80.2 all-gather.9
  177.4 75.9 all-gather.7
  256.3 92.2 all-gather.13
  351.4 204.9 all-gather.15
  559.2 192.9 all-gather.17
  755.2 192.9 all-gather.19
  1030.6 1920.9 all-reduce.12
  2953.9 708.6 reduce-scatter.2
  3665.4 705.8 reduce-scatter.4
where the time goes:
time: 4390 us; the launch traced here: 4380 us
  waiting for transfers between devices  3730 us (85%)
  matrix products  285 us (6%)
  blocking collectives  155 us (4%)
  local copies, waits for them, and re-layouts  79.9 us (2%)
  other arithmetic  71 us (2%)
    unnamed x11, waiting for transfers between devices  1570 us
    reduce_scatter x1, waiting for transfers between devices, body(): lax.psum_scatter(jnp.concatenate([transposed(normed, projection_grads), t...  706 us
    reduce_scatter x1, waiting for transfers between devices, body(): lax.psum_scatter(transposed(hidden, grad_branch), ('fsdp', 'seq'), scatte...  706 us
    all_gather x1, waiting for transfers between devices, body(): lax.all_gather(up_weight, ('fsdp', 'seq'), axis=0, tiled=True)  178 us
    all_gather x1, waiting for transfers between devices, body(): lax.all_gather(down_weight, ('fsdp', 'seq'), axis=0, tiled=True)  175 us
    all_gather x1, waiting for transfers between devices, body(): lax.all_gather(gate_weight, ('fsdp', 'seq'), axis=0, tiled=True)  128 us
    dot_general x4, matrix products, transposed(): lax.dot_general(left_side, right_side, (((0,), (0,)), ((), ())), preferre...  102 us
  transfers between devices with their start and end apart: 18, of which 15 were waited for; matrix products, arithmetic and copies ran while one was open for 8% of the time, Pallas kernels for 0%

commit v1 on v0

v1 whole, which is shorter than its diff:
```python
import jax
import jax.numpy as jnp
from jax import lax
from jax.sharding import PartitionSpec as P

H = 32
HD = 64
EPSILON = 1e-05
ROPE_BASE = 130000.0
MASKED = -1e30
BF = jnp.bfloat16
F32 = jnp.float32
ALL = ("fsdp", "seq")


def rms_norm(values, gain_vector):
    return (
        values
        * lax.rsqrt(jnp.mean(values * values, axis=-1, keepdims=True) + EPSILON)
        * gain_vector
    )


def rope_tables(length):
    exponents = jnp.arange(HD // 2).astype(F32) * (2.0 / HD)
    inverse = jnp.power(ROPE_BASE, -exponents)
    angles = jnp.arange(length, dtype=jnp.int32).astype(F32)[:, None] * inverse[None, :]
    return jnp.cos(angles), jnp.sin(angles)


def rotate(values, cosine, sine):
    half = HD // 2
    cosine, sine = cosine[:, None, :], sine[:, None, :]
    leading, trailing = values[..., :half], values[..., half:]
    return jnp.concatenate(
        [leading * cosine - trailing * sine, trailing * cosine + leading * sine], axis=-1
    )


def matmul(left_side, right_side):
    return jnp.dot(left_side, right_side, preferred_element_type=F32)


def transposed(left_side, right_side):
    return lax.dot_general(
        left_side, right_side, (((0,), (0,)), ((), ())), preferred_element_type=F32
    )


def against(left_side, right_side):
    return lax.dot_general(
        left_side, right_side, (((1,), (1,)), ((), ())), preferred_element_type=F32
    )


def gated(gate_value, up_value):
    return gate_value * jax.nn.sigmoid(gate_value) * up_value


def gather_rows(local):
    return lax.all_gather(local, "seq", axis=0, tiled=True)


def scatter_rows(partial):
    return lax.psum_scatter(
        partial.astype(BF), "seq", scatter_dimension=0, tiled=True
    ).astype(F32)


def columns_in(weight, blocks):
    groups = lax.axis_size("seq")
    rows, width = weight.shape
    part = width // (blocks * groups)
    swapped = lax.all_to_all(
        weight.reshape(rows, blocks, groups, part), "seq", split_axis=2, concat_axis=0, tiled=True
    ).reshape(groups * rows, blocks * part)
    return lax.all_gather(swapped, "fsdp", axis=0, tiled=True)


def columns_out(grad, blocks):
    groups = lax.axis_size("seq")
    part = grad.shape[1] // blocks
    summed = lax.psum_scatter(grad.astype(BF), "fsdp", scatter_dimension=0, tiled=True)
    rows = summed.shape[0] // groups
    swapped = lax.all_to_all(
        summed.reshape(groups * rows, blocks, 1, part),
        "seq",
        split_axis=0,
        concat_axis=2,
        tiled=True,
    )
    return swapped.reshape(rows, blocks * groups * part).astype(F32)


def rows_in(weight):
    return lax.all_gather(weight, "fsdp", axis=0, tiled=True)


def rows_out(grad):
    return lax.psum_scatter(
        grad.astype(BF), "fsdp", scatter_dimension=0, tiled=True
    ).astype(F32)


def body(
    tokens,
    teacher,
    segments,
    valid,
    query_weight,
    key_weight,
    value_weight,
    output_weight,
    attention_gain,
    gate_weight,
    up_weight,
    down_weight,
    mlp_gain,
):
    sequences, local_rows, width = tokens.shape
    groups = lax.axis_size("seq")
    shards = lax.axis_size("fsdp")
    heads = H // groups
    length = local_rows * groups
    scale = HD ** (-0.5)
    own = lax.axis_index("seq")
    aligned = H % (shards * groups) == 0
    head_blocks = shards if aligned else 1

    inputs = tokens.reshape(local_rows, width).astype(F32)
    tokens_all = gather_rows(tokens.reshape(local_rows, width)).astype(F32)
    segment = lax.all_gather(segments, "seq", axis=1, tiled=True).reshape(length)
    gains = lax.all_gather(
        jnp.stack([attention_gain, mlp_gain], axis=1), ALL, axis=0, tiled=True
    ).astype(F32)
    first_gain, second_gain = gains[:, 0], gains[:, 1]
    normed = rms_norm(tokens_all, first_gain).astype(BF)

    qkv_weight = jnp.concatenate(
        [columns_in(w, head_blocks) for w in (query_weight, key_weight, value_weight)], axis=1
    )
    if aligned:
        out_weight = rows_in(output_weight)
    else:
        out_weight = lax.dynamic_slice_in_dim(
            lax.all_gather(output_weight, ALL, axis=0, tiled=True),
            own * heads * HD,
            heads * HD,
            0,
        )
    gate_up_weight = jnp.concatenate(
        [columns_in(gate_weight, shards), columns_in(up_weight, shards)], axis=1
    )
    down_full = rows_in(down_weight)

    hw = heads * HD
    qkv = matmul(normed, qkv_weight)
    cosine, sine = rope_tables(length)

    def rotated(values):
        return rotate(values.reshape(length, heads, HD), cosine, sine)

    query = rotated(qkv[:, :hw]).astype(BF)
    key = rotated(qkv[:, hw : 2 * hw]).astype(BF)
    value = qkv[:, 2 * hw :].astype(BF).reshape(length, heads, HD)
    places = jnp.arange(length, dtype=jnp.int32)
    allowed = (segment[:, None] == segment[None, :]) & (places[None, :] <= places[:, None])
    scores = jnp.einsum("qhd,khd->hqk", query, key, preferred_element_type=F32) * scale
    scores = jnp.where(allowed[None], scores, MASKED)
    row_max = jnp.max(scores, axis=-1, keepdims=True)
    exponent = jnp.exp(scores - row_max)
    row_total = jnp.sum(exponent, axis=-1, keepdims=True)
    probs = exponent / row_total
    weights = probs.astype(BF)
    mixed = (
        jnp.einsum("hqk,khd->qhd", weights, value, preferred_element_type=F32)
        .astype(BF)
        .reshape(length, hw)
    )
    after_attention = inputs + scatter_rows(matmul(mixed, out_weight))
    normed_two_own = rms_norm(after_attention, second_gain).astype(BF)
    normed_two = gather_rows(normed_two_own)
    gate_up = matmul(normed_two, gate_up_weight)
    hidden_width = gate_up.shape[1] // 2
    gate_value, up_value = gate_up[:, :hidden_width], gate_up[:, hidden_width:]
    hidden = gated(gate_value, up_value).astype(BF)
    result = after_attention + scatter_rows(matmul(hidden, down_full))
    keep_mask = valid.reshape(local_rows).astype(F32)
    difference = result - teacher.reshape(local_rows, width).astype(F32)
    count, error_sum = lax.psum(
        (jnp.sum(keep_mask), jnp.sum(keep_mask[:, None] * difference * difference)), ALL
    )
    loss = error_sum / count
    grad_result = 2.0 / count * keep_mask[:, None] * difference
    grad_branch = gather_rows(grad_result.astype(BF))
    grad_hidden = against(grad_branch, down_full)
    unused, gate_pull = jax.vjp(gated, gate_value, up_value)
    grad_gate, grad_upward = gate_pull(grad_hidden)
    gate_up_grad = jnp.concatenate([grad_gate.astype(BF), grad_upward.astype(BF)], axis=1)
    grad_normed_two = scatter_rows(against(gate_up_grad, gate_up_weight))
    unused, second_pull = jax.vjp(rms_norm, after_attention, second_gain)
    grad_after, second_gain_grad = second_pull(grad_normed_two)
    grad_after = grad_after + grad_result
    down_sum = rows_out(transposed(hidden, grad_branch))
    gate_up_weight_grad = transposed(normed_two, gate_up_grad)
    gate_sum = columns_out(gate_up_weight_grad[:, :hidden_width], shards)
    up_sum = columns_out(gate_up_weight_grad[:, hidden_width:], shards)

    grad_out = gather_rows(grad_after.astype(BF))
    grad_mixed = against(grad_out, out_weight).astype(BF).reshape(length, heads, HD)
    output_grad = transposed(mixed, grad_out)
    if aligned:
        output_sum = rows_out(output_grad)
    else:
        output_sum = lax.psum_scatter(
            lax.dynamic_update_slice_in_dim(
                jnp.zeros((width, width), BF), output_grad.astype(BF), own * hw, 0
            ),
            ALL,
            scatter_dimension=0,
            tiled=True,
        ).astype(F32)
    grad_probs = jnp.einsum("qhd,khd->hqk", grad_mixed, value, preferred_element_type=F32)
    inner = jnp.sum(probs * grad_probs, axis=-1, keepdims=True)
    grad_scores = (probs * (grad_probs - inner)).astype(BF)
    grad_query = (
        jnp.einsum("hqk,khd->qhd", grad_scores, key, preferred_element_type=F32) * scale
    ).astype(BF)
    grad_key = (
        jnp.einsum("hqk,qhd->khd", grad_scores, query, preferred_element_type=F32) * scale
    ).astype(BF)
    grad_value = jnp.einsum("hqk,qhd->khd", weights, grad_mixed, preferred_element_type=F32)

    def rotated_back(values):
        return rotate(values.astype(F32), cosine, -sine).astype(BF).reshape(length, hw)

    qkv_grad = jnp.concatenate(
        [
            rotated_back(grad_query),
            rotated_back(grad_key),
            grad_value.astype(BF).reshape(length, hw),
        ],
        axis=1,
    )
    grad_normed = scatter_rows(against(qkv_grad, qkv_weight))
    unused, first_pull = jax.vjp(rms_norm, inputs, first_gain)
    grad_inputs, first_gain_grad = first_pull(grad_normed)
    grad_inputs = grad_inputs + grad_after
    qkv_weight_grad = transposed(normed, qkv_grad)
    query_sum, key_sum, value_sum = (
        columns_out(qkv_weight_grad[:, i * hw : (i + 1) * hw], head_blocks) for i in range(3)
    )
    gain_sums = lax.psum_scatter(
        jnp.stack([first_gain_grad, second_gain_grad], axis=1),
        ALL,
        scatter_dimension=0,
        tiled=True,
    )
    output_shape = (sequences, local_rows, width)
    return (
        result.reshape(output_shape).astype(BF),
        loss,
        grad_inputs.reshape(output_shape),
        query_sum,
        key_sum,
        value_sum,
        output_sum,
        gain_sums[:, 0],
        gate_sum,
        up_sum,
        down_sum,
        gain_sums[:, 1],
    )


def solution(mesh):
    rows = P("fsdp", "seq", None)
    places = P("fsdp", "seq")
    matrix = P(ALL, None)
    vector = P(ALL)
    return jax.shard_map(
        body,
        mesh=mesh,
        in_specs=(
            rows,
            rows,
            places,
            places,
            matrix,
            matrix,
            matrix,
            matrix,
            vector,
            matrix,
            matrix,
            matrix,
            vector,
        ),
        out_specs=(
            rows,
            P(),
            rows,
            matrix,
            matrix,
            matrix,
            matrix,
            vector,
            matrix,
            matrix,
            matrix,
            vector,
        ),
        check_vma=False,
    )
```

time: 4390 us -> 1230 us (0.28)
  waiting for transfers between devices: 3730 us -> 672 us
  matrix products: 285 us -> 139 us
  blocking collectives: 155 us -> 256 us
    unnamed x11 -> x24, waiting for transfers between devices: 1570 us -> 134 us
    reduce_scatter x2 -> x11, waiting for transfers between devices: 1410 us -> 228 us  [the longest x5 100 us: columns_out(): lax.psum_scatter(grad.astype(BF), 'fsdp', scatter_dimension=0, tiled=True)]
    all_gather x7 -> x11, waiting for transfers between devices: 655 us -> 301 us  [the longest x4 161 us: gather_rows(): return lax.all_gather(local, 'seq', axis=0, tiled=True)]
    all_to_all x0 -> x5, blocking collectives: none -> 126 us  [columns_in(): lax.all_to_all(weight.reshape(rows, blocks, groups, part), 'seq', split_a...]
    all_to_all x8 -> x5, waiting for transfers between devices: 89 us -> 8.5 us  [columns_out(): lax.all_to_all(summed.reshape(groups * rows, blocks, 1, part), 'seq', spl...]
    dot_general x4, matrix products: 102 us -> 31.7 us  [transposed(): lax.dot_general(left_side, right_side, (((0,), (0,)), ((), ())), preferre...]
    concatenate x3 -> x1, other arithmetic: 46.7 us -> 0.07 us  [rotate(): jnp.concatenate([leading * cosine - trailing * sine, trailing * cosine +...]
    dot_general x7 -> x4, matrix products: 81 us -> 35.4 us  [against(): lax.dot_general(left_side, right_side, (((1,), (1,)), ((), ())), preferre...]
  transfers between devices with their start and end apart: 18 -> 28, of which waited for: 15 -> 20; matrix products, arithmetic and copies ran while one was open for 8% -> 15% of each run, Pallas kernels for 0% -> 0%
where the time goes in v1:
time: 1230 us; the launch traced here: 1220 us
  waiting for transfers between devices  672 us (55%)
  blocking collectives  256 us (21%)
  matrix products  139 us (11%)
  local copies, waits for them, and re-layouts  76.5 us (6%)
  other arithmetic  37.4 us (3%)
  starting transfers between devices  23.7 us (2%)
  between operations  18.4 us (1%)
    all_gather x4, waiting for transfers between devices, gather_rows(): return lax.all_gather(local, 'seq', axis=0, tiled=True)  161 us
    unnamed x24, waiting for transfers between devices  134 us
    all_to_all x5, blocking collectives, columns_in(): lax.all_to_all(weight.reshape(rows, blocks, groups, part), 'seq', split_a...  126 us
    all_gather x5, waiting for transfers between devices, columns_in(): return lax.all_gather(swapped, 'fsdp', axis=0, tiled=True)  104 us
    reduce_scatter x5, waiting for transfers between devices, columns_out(): lax.psum_scatter(grad.astype(BF), 'fsdp', scatter_dimension=0, tiled=True)  100 us
    reduce_scatter x4, waiting for transfers between devices, scatter_rows(): lax.psum_scatter(partial.astype(BF), 'seq', scatter_dimension=0, tiled=True)  91.9 us
    psum x2, blocking collectives, body(): lax.psum((jnp.sum(keep_mask), jnp.sum(keep_mask[:, None] * difference * d...  81.7 us
    all_gather x1, blocking collectives, body(): lax.all_gather(jnp.stack([attention_gain, mlp_gain], axis=1), ALL, axis=0...  39.3 us
  transfers between devices with their start and end apart: 28, of which 20 were waited for; matrix products, arithmetic and copies ran while one was open for 15% of the time, Pallas kernels for 0%

profile of v1, /device:TPU:0, one launch (start us, length us, event | category | flops | bytes accessed | tf_op | source)
XLA Modules:
  0.0 1222.3 jit_solution(9955692637208750982)
XLA Ops:
  9.7 15.9 %all_to_all.120 = bf16[8,2,8192]{2,1,0:T(2,128)(2,1)S(1)} all-to-all(bf16[8,2,8192]{2,1,0:T(2,128)(2,1)S(1)} %reshape.371), channel_id=1, replica_groups=mesh['fsdp'=4,'seq'=8] {'seq'}, dimensions={0} | all-to-all | bytes 524288 | tf_op jit(solution)/shard_map/all_to_all | solution.py:74
  29.0 12.1 all_to_all.121
  44.6 12.1 all_to_all.122
  59.8 39.3 %all-gather.1 = bf16[32,64,2]{1,2,0:T(2,128)(2,1)S(1)} all-gather(bf16[1,64,2]{1,2,0:T(2,128)(2,1)S(1)} %maximum_bitcast_fusion), channel_id=1, replica_groups=mesh['fsdp'=4,'seq'=8] {'fsdp','seq'}, dimensions={0}, use_global_device_ids=true | all-gather | bytes 8448 | tf_op jit(solution)/shard_map/all_gather | solution.py:133
  99.2 8.8 all_gather.44
  116.9 42.6 %all-gather.34.cloned.1.call-done = bf16[1,1024,2048]{2,1,0:T(8,128)(2,1)} async-done(((bf16[1,128,2048]{2,1,0:T(8,128)(2,1)}), bf16[1,1024,2048]{2,1,0:T(8,128)(2,1)}) %all-gather.34.cloned.1.call-update) | async-done | bytes 4194320 | tf_op jit(solution)/shard_map/all_gather | solution.py:61
  169.1 10.0 fusion.71
  192.1 47.8 %all_to_all.123 = bf16[64,4,8,256]{3,1,0,2:T(4,128)(2,1)S(1)} all-to-all(bf16[64,4,8,256]{3,1,0,2:T(4,128)(2,1)S(1)} %copy.117), channel_id=1, replica_groups=mesh['fsdp'=4,'seq'=8] {'seq'}, dimensions={2} | all-to-all | bytes 2097152 | tf_op jit(solution)/shard_map/all_to_all | solution.py:74
  242.2 37.9 %all_to_all.124 = bf16[64,4,8,256]{3,1,0,2:T(4,128)(2,1)S(1)} all-to-all(bf16[64,4,8,256]{3,1,0,2:T(4,128)(2,1)S(1)} %copy.118), channel_id=1, replica_groups=mesh['fsdp'=4,'seq'=8] {'seq'}, dimensions={2} | all-to-all | bytes 2097152 | tf_op jit(solution)/shard_map/all_to_all | solution.py:74
  285.4 53.1 %all-gather.24.cloned.1.call-done = bf16[2048,1024]{1,0:T(8,128)(2,1)} async-done(((bf16[512,1024]{1,0:T(8,128)(2,1)}), bf16[2048,1024]{1,0:T(8,128)(2,1)}) %all-gather.24.cloned.1.call-update) | async-done | bytes 4194320 | tf_op jit(solution)/shard_map/all_gather | solution.py:77
  343.2 50.5 %all-gather.26.cloned.1.call-done = bf16[2048,1024]{1,0:T(8,128)(2,1)} async-done(((bf16[512,1024]{1,0:T(8,128)(2,1)}), bf16[2048,1024]{1,0:T(8,128)(2,1)}) %all-gather.26.cloned.1.call-update) | async-done | bytes 4194320 | tf_op jit(solution)/shard_map/all_gather | solution.py:77
  398.4 44.7 %all-gather.22.cloned.1.call-done = bf16[1024,2048]{1,0:T(8,128)(2,1)} async-done(((bf16[128,2048]{1,0:T(8,128)(2,1)}), bf16[1024,2048]{1,0:T(8,128)(2,1)}) %all-gather.22.cloned.1.call-update) | async-done | bytes 4194320 | tf_op jit(solution)/shard_map/all_gather | solution.py:61
  443.1 12.5 %fusion.72 = f32[1024,2048]{1,0:T(8,128)S(1)} fusion(bf16[1024,2048]{1,0:T(8,128)(2,1)} %all-gather.22.cloned.1.call-done, bf16[2048,2048]{1,0:T(8,128)(2,1)} %constant_dynamic-update-slice_fusion.3), kind=kOutput, calls=%fused_computation.145 | convolution fusion | flops 8589934592 | bytes 20971520 | tf_op jit(solution)/shard_map/dot_general | solution.py:41
  460.3 35.9 %all-gather.28.cloned.1.call-done = bf16[1024,2048]{1,0:T(8,128)(2,1)} async-done(((bf16[256,2048]{1,0:T(8,128)(2,1)}), bf16[1024,2048]{1,0:T(8,128)(2,1)}) %all-gather.28.cloned.1.call-update) | async-done | bytes 4194320 | tf_op jit(solution)/shard_map/all_gather | solution.py:96
  505.7 41.3 %psum.15 = f32[]{:T(128)} all-reduce(f32[]{:T(128)} %convert_reduce_fusion), channel_id=1, replica_groups=mesh['fsdp'=4,'seq'=8] {'fsdp','seq'}, use_global_device_ids=true, to_apply=%region_9.10 | all-reduce | flops 1 | bytes 8 | tf_op jit(solution)/shard_map/psum | solution.py:190
  558.1 45.2 %all-gather.30.cloned.1.call-done = bf16[1024,2048]{1,0:T(8,128)(2,1)} async-done(((bf16[128,2048]{1,0:T(8,128)(2,1)}), bf16[1024,2048]{1,0:T(8,128)(2,1)}) %all-gather.30.cloned.1.call-update) | async-done | bytes 4194320 | tf_op jit(solution)/shard_map/all_gather | solution.py:61
  603.4 11.7 fusion.10
  617.1 12.7 %convolution_convert_fusion.1 = bf16[1024,2048]{1,0:T(8,128)(2,1)} fusion(bf16[2048,2048]{1,0:T(8,128)(2,1)} %constant_dynamic-update-slice_fusion.3, bf16[1024,1024]{1,0:T(8,128)(2,1)S(1)} %get-tuple-element.21, bf16[1024,1024]{1,0:T(8,128)(2,1)S(1)} %get-tuple-element.20), kind=kOutput, calls=%fused_computation.31 | convolution fusion | flops 8600420352 | bytes 16777216 | tf_op jit(solution)/shard_map/dot_general | solution.py:51
  629.8 48.8 %reduce-scatter.19.cloned.1.call-done = bf16[128,2048]{1,0:T(8,128)(2,1)} async-done(((bf16[1024,2048]{1,0:T(8,128)(2,1)}), bf16[128,2048]{1,0:T(8,128)(2,1)}) %reduce-scatter.19.cloned.1.call-update) | async-done | bytes 524304 | tf_op jit(solution)/shard_map/reduce_scatter | solution.py:65
  684.3 12.1 convolution_convert_fusion
  700.9 28.6 %all-gather.32.cloned.1.call-done = bf16[1024,2048]{1,0:T(8,128)(2,1)} async-done(((bf16[128,2048]{1,0:T(8,128)(2,1)}), bf16[1024,2048]{1,0:T(8,128)(2,1)}) %all-gather.32.cloned.1.call-update) | async-done | bytes 4194320 | tf_op jit(solution)/shard_map/all_gather | solution.py:61
  733.1 15.6 %multiply_reduce_fusion = (f32[4,1024]{1,0:T(4,128)S(1)}, f32[4,1024,1024]{1,2,0:T(8,128)}) fusion(f32[4,1024,1024]{1,2,0:T(8,128)} %get-tuple-element.50, f32[4,1024]{1,0:T(4,128)S(1)} %get-tuple-element.49, bf16[1024,4,64]{0,2,1:T(8,128)(2,1)S(1)} %bitcast.253, bf16[1024,4,64]{0,2,1:T(8,128)(2,1)S(1)} %bitcast.232), kind=kOutput, calls=%fused_computation.2 | convolution fusion | flops 549449728 | bytes 34635776 | tf_op jit(solution)/shard_map/qhd,khd->hqk/dot_general | solution.py:223
  777.7 8.8 convolution_convert_fusion.4
  806.4 33.2 %reduce-scatter.33.cloned.1.call-done = bf16[512,1024]{1,0:T(8,128)(2,1)} async-done(((bf16[2048,1024]{1,0:T(8,128)(2,1)}), bf16[512,1024]{1,0:T(8,128)(2,1)}) %reduce-scatter.33.cloned.1.call-update) | async-done | bytes 1048592 | tf_op jit(solution)/shard_map/reduce_scatter | solution.py:83
  846.8 23.8 %reduce-scatter.23.cloned.1.call-done = bf16[512,256]{1,0:T(8,128)(2,1)} async-done(((bf16[2048,256]{1,0:T(8,128)(2,1)}), bf16[512,256]{1,0:T(8,128)(2,1)}) %reduce-scatter.23.cloned.1.call-update) | async-done | bytes 262160 | tf_op jit(solution)/shard_map/reduce_scatter | solution.py:83
  877.8 40.4 %psum.14 = f32[]{:T(128)} all-reduce(f32[]{:T(128)} %get-tuple-element.16), channel_id=1, replica_groups=mesh['fsdp'=4,'seq'=8] {'fsdp','seq'}, use_global_device_ids=true, to_apply=%region_7.8 | all-reduce | flops 1 | bytes 8 | tf_op jit(solution)/shard_map/psum | solution.py:190
  930.5 28.4 %reduce-scatter.25.cloned.1.call-done = bf16[512,256]{1,0:T(8,128)(2,1)} async-done(((bf16[2048,256]{1,0:T(8,128)(2,1)}), bf16[512,256]{1,0:T(8,128)(2,1)}) %reduce-scatter.25.cloned.1.call-update) | async-done | bytes 262160 | tf_op jit(solution)/shard_map/reduce_scatter | solution.py:83
  975.2 14.5 %reduce-scatter.27.cloned.1.call-done = bf16[512,256]{1,0:T(8,128)(2,1)} async-done(((bf16[2048,256]{1,0:T(8,128)(2,1)}), bf16[512,256]{1,0:T(8,128)(2,1)}) %reduce-scatter.27.cloned.1.call-update) | async-done | bytes 262160 | tf_op jit(solution)/shard_map/reduce_scatter | solution.py:83
  992.2 28.2 %reduce-scatter.29.cloned.1.call-done = bf16[64,2048]{1,0:T(8,128)(2,1)} async-done(((bf16[256,2048]{1,0:T(8,128)(2,1)}), bf16[64,2048]{1,0:T(8,128)(2,1)}) %reduce-scatter.29.cloned.1.call-update) | async-done | bytes 262160 | tf_op jit(solution)/shard_map/reduce_scatter | solution.py:100
  1031.2 8.2 all-to-all-done.7
  1041.7 35.1 %reduce-scatter.21.cloned.1.call-done = bf16[128,2048]{1,0:T(8,128)(2,1)} async-done(((bf16[1024,2048]{1,0:T(8,128)(2,1)}), bf16[128,2048]{1,0:T(8,128)(2,1)}) %reduce-scatter.21.cloned.1.call-update) | async-done | bytes 524304 | tf_op jit(solution)/shard_map/reduce_scatter | solution.py:65
  1082.2 130.2 %reduce-scatter.37.cloned.1.call-done = f32[64,2]{1,0:T(8,128)} async-done(((f32[2048,2]{1,0:T(8,128)}), f32[64,2]{1,0:T(8,128)}) %reduce-scatter.37.cloned.1.call-update) | async-done | bytes 528
  (270 shorter events, 213.7 us)
Async XLA Ops:
  7.2 102.7 %all-gather.14.cloned.1.call-start = ((), (), s32[]{:S(2)}) async-start(), calls=%async_computation.22 | async-start | bytes 1310720 | tf_op jit(solution)/shard_map/all_gather | solution.py:77
  27.4 84.8 %all-gather.16.cloned.1.call-start = ((), (), s32[]{:S(2)}) async-start(), calls=%async_computation.23 | async-start | bytes 1310720 | tf_op jit(solution)/shard_map/all_gather | solution.py:77
  43.0 56.2 %copy-start.34 = (s32[1,128]{1,0:T(1,128)S(1)}, s32[1,128]{1,0:T(1,128)}, u32[]{:S(2)}) copy-start(s32[1,128]{1,0:T(1,128)} %param.15) | copy-start | bytes 1540
  43.0 71.6 %all-gather.18.cloned.1.call-start = ((), (), s32[]{:S(2)}) async-start(), calls=%async_computation.24 | async-start | bytes 1310720 | tf_op jit(solution)/shard_map/all_gather | solution.py:77
  58.5 101.0 %all-gather.34.cloned.1.call-start = ((), (), s32[]{:S(2)}) async-start(), calls=%async_computation.43 | async-start | bytes 4718592 | tf_op jit(solution)/shard_map/all_gather | solution.py:61
  59.1 127.5 %all-gather.20.cloned.1.call-start = ((), (), s32[]{:S(2)}) async-start(), calls=%async_computation.25 | async-start | bytes 1310720 | tf_op jit(solution)/shard_map/all_gather | solution.py:96
  59.7 221.7 %reduce-scatter.15.cloned.1.call-start = ((), (), s32[]{:S(2)}) async-start(), calls=%async_computation.26 | async-start | bytes 4718592 | tf_op jit(solution)/shard_map/reduce_scatter | solution.py:65
  99.2 63.6 %copy-start.30 = (f32[2048,1]{0,1:T(1,128)}, f32[2048,1]{0,1:T(1,128)S(1)}, u32[]{:S(2)}) copy-start(f32[2048,1]{0,1:T(1,128)S(1)} %get-tuple-element.45) | copy-start | bytes 24580
  109.9 58.9 %copy-start.12 = (f32[1024,32]{0,1:T(8,128)}, f32[1024,32]{0,1:T(8,128)S(1)}, u32[]{:S(2)}) copy-start(f32[1024,32]{0,1:T(8,128)S(1)} %get-tuple-element.48) | copy-start | bytes 393220
  191.3 147.2 %all-gather.24.cloned.1.call-start = ((), (), s32[]{:S(2)}) async-start(), calls=%async_computation.28 | async-start | bytes 5242880 | tf_op jit(solution)/shard_map/all_gather | solution.py:77
  241.1 152.6 %all-gather.26.cloned.1.call-start = ((), (), s32[]{:S(2)}) async-start(), calls=%async_computation.29 | async-start | bytes 5242880 | tf_op jit(solution)/shard_map/all_gather | solution.py:77
  281.3 161.7 %all-gather.22.cloned.1.call-start = ((), (), s32[]{:S(2)}) async-start(), calls=%async_computation.27 | async-start | bytes 4718592 | tf_op jit(solution)/shard_map/all_gather | solution.py:61
  284.8 211.4 %all-gather.28.cloned.1.call-start = ((), (), s32[]{:S(2)}) async-start(), calls=%async_computation.30 | async-start | bytes 5242880 | tf_op jit(solution)/shard_map/all_gather | solution.py:96
  285.4 270.3 %reduce-scatter.17.cloned.1.call-start = ((), (), s32[]{:S(2)}) async-start(), calls=%async_computation.31 | async-start | bytes 4718592 | tf_op jit(solution)/shard_map/reduce_scatter | solution.py:65
  504.5 98.9 %all-gather.30.cloned.1.call-start = ((), (), s32[]{:S(2)}) async-start(), calls=%async_computation.32 | async-start | bytes 4718592 | tf_op jit(solution)/shard_map/all_gather | solution.py:61
  557.9 120.7 %reduce-scatter.19.cloned.1.call-start = ((), (), s32[]{:S(2)}) async-start(), calls=%async_computation.33 | async-start | bytes 4718592 | tf_op jit(solution)/shard_map/reduce_scatter | solution.py:65
  629.7 99.8 %all-gather.32.cloned.1.call-start = ((), (), s32[]{:S(2)}) async-start(), calls=%async_computation.34 | async-start | bytes 4718592 | tf_op jit(solution)/shard_map/all_gather | solution.py:61
  684.1 116.1 %reduce-scatter.31.cloned.1.call-start = ((), (), s32[]{:S(2)}) async-start(), calls=%async_computation.40 | async-start | bytes 5242880 | tf_op jit(solution)/shard_map/reduce_scatter | solution.py:83
  700.3 139.3 %reduce-scatter.33.cloned.1.call-start = ((), (), s32[]{:S(2)}) async-start(), calls=%async_computation.41 | async-start | bytes 5242880 | tf_op jit(solution)/shard_map/reduce_scatter | solution.py:83
  700.8 169.8 %reduce-scatter.23.cloned.1.call-start = ((), (), s32[]{:S(2)}) async-start(), calls=%async_computation.36 | async-start | bytes 1310720 | tf_op jit(solution)/shard_map/reduce_scatter | solution.py:83
  776.7 151.1 %reduce-scatter.35.cloned.1.call-start = ((), (), s32[]{:S(2)}) async-start(), calls=%async_computation.42 | async-start | bytes 5242880 | tf_op jit(solution)/shard_map/reduce_scatter | solution.py:100
  786.5 172.4 %reduce-scatter.25.cloned.1.call-start = ((), (), s32[]{:S(2)}) async-start(), calls=%async_computation.37 | async-start | bytes 1310720 | tf_op jit(solution)/shard_map/reduce_scatter | solution.py:83
  787.3 202.4 %reduce-scatter.27.cloned.1.call-start = ((), (), s32[]{:S(2)}) async-start(), calls=%async_computation.38 | async-start | bytes 1310720 | tf_op jit(solution)/shard_map/reduce_scatter | solution.py:83
  787.9 232.5 %reduce-scatter.29.cloned.1.call-start = ((), (), s32[]{:S(2)}) async-start(), calls=%async_computation.39 | async-start | bytes 1310720 | tf_op jit(solution)/shard_map/reduce_scatter | solution.py:100
  792.4 284.3 %reduce-scatter.21.cloned.1.call-start = ((), (), s32[]{:S(2)}) async-start(), calls=%async_computation.35 | async-start | bytes 4718592 | tf_op jit(solution)/shard_map/reduce_scatter | solution.py:65
  802.8 39.4 %all-to-all-start.8 = ((bf16[512,4,1,256]{3,1,2,0:T(4,128)(2,1)}), bf16[512,4,1,256]{3,1,2,0:T(4,128)(2,1)S(1)}, u32[]{:S(2)}, u32[]{:S(2)}) async-start(bf16[512,4,1,256]{3,1,2,0:T(4,128)(2,1)} %bitcast.49), calls=%async_computation.17 | async-start | bytes 2097152 | tf_op jit(solution)/shard_map/all_to_all | solution.py:85
  842.2 31.2 %all-to-all-start.9 = ((bf16[512,4,1,256]{3,1,2,0:T(4,128)(2,1)}), bf16[512,4,1,256]{3,1,2,0:T(4,128)(2,1)S(1)}, u32[]{:S(2)}, u32[]{:S(2)}) async-start(bf16[512,4,1,256]{3,1,2,0:T(4,128)(2,1)} %bitcast.208), calls=%async_computation.19 | async-start | bytes 2097152 | tf_op jit(solution)/shard_map/all_to_all | solution.py:85
  873.4 94.5 %copy-start.5 = (bf16[512,4,1,256]{3,1,2,0:T(4,128)(2,1)}, bf16[512,4,1,256]{3,1,2,0:T(4,128)(2,1)S(1)}, u32[]{:S(2)}) copy-start(bf16[512,4,1,256]{3,1,2,0:T(4,128)(2,1)S(1)} %all-to-all-done.9) | copy-start | bytes 3145732
  873.4 89.7 %all-to-all-start.5 = ((bf16[8,2,8192]{2,1,0:T(2,128)(2,1)}), bf16[8,2,8192]{2,1,0:T(2,128)(2,1)S(1)}, u32[]{:S(2)}, u32[]{:S(2)}) async-start(bf16[8,2,8192]{2,1,0:T(2,128)(2,1)} %reshape.377), calls=%async_computation.10 | async-start | bytes 524288 | tf_op jit(solution)/shard_map/all_to_all | solution.py:85
  963.1 59.4 %all-to-all-start.6 = ((bf16[8,2,8192]{2,1,0:T(2,128)(2,1)}), bf16[8,2,8192]{2,1,0:T(2,128)(2,1)S(1)}, u32[]{:S(2)}, u32[]{:S(2)}) async-start(bf16[8,2,8192]{2,1,0:T(2,128)(2,1)} %reshape.379), calls=%async_computation.12 | async-start | bytes 524288 | tf_op jit(solution)/shard_map/all_to_all | solution.py:85
  1022.5 17.0 %all-to-all-start.7 = ((bf16[8,2,8192]{2,1,0:T(2,128)(2,1)}), bf16[8,2,8192]{2,1,0:T(2,128)(2,1)S(1)}, u32[]{:S(2)}, u32[]{:S(2)}) async-start(bf16[8,2,8192]{2,1,0:T(2,128)(2,1)} %reshape.381), calls=%async_computation.14 | async-start | bytes 524288 | tf_op jit(solution)/shard_map/all_to_all | solution.py:85
  1027.1 185.2 %reduce-scatter.37.cloned.1.call-start = ((), (), s32[]{:S(2)}) async-start(), calls=%async_computation.44 | async-start | bytes 1081344
  (43 other events, 615.9 us)
Sparse Core Ops, SparseCore 0:
  27.6 25.3 all-gather.13
  55.4 26.5 all-gather.15
  84.3 26.4 all-gather.17
  112.3 47.1 all-gather.33
  161.2 25.3 all-gather.19
  191.4 79.5 reduce-scatter.14
  273.4 65.0 all-gather.23
  341.0 52.6 all-gather.25
  395.9 47.1 all-gather.21
  444.8 51.4 all-gather.27
  504.6 51.0 reduce-scatter.16
  558.0 45.2 all-gather.29
  629.9 48.7 reduce-scatter.18
  684.2 45.2 all-gather.31
  732.3 51.4 reduce-scatter.30
  786.9 52.6 reduce-scatter.32
  842.9 27.7 reduce-scatter.22
  873.8 53.9 reduce-scatter.34
  931.2 27.7 reduce-scatter.24
  962.0 27.7 reduce-scatter.26
  992.6 27.7 reduce-scatter.28
  1022.8 53.9 reduce-scatter.20
  1079.9 132.3 reduce-scatter.36

commit v2 on v1

--- a/solution.py
+++ b/solution.py
@@ -21,10 +21,10 @@
     )
 
 
-def rope_tables(length):
+def rope_tables(places):
     exponents = jnp.arange(HD // 2).astype(F32) * (2.0 / HD)
     inverse = jnp.power(ROPE_BASE, -exponents)
-    angles = jnp.arange(length, dtype=jnp.int32).astype(F32)[:, None] * inverse[None, :]
+    angles = places.astype(F32)[:, None] * inverse[None, :]
     return jnp.cos(angles), jnp.sin(angles)
 
 
@@ -57,39 +57,101 @@
     return gate_value * jax.nn.sigmoid(gate_value) * up_value
 
 
+def turn(value, steps):
+    size = lax.axis_size("seq")
+    return lax.ppermute(value, "seq", [(s, (s - 2 * steps) % size) for s in range(size)])
+
+
+def swap(value):
+    return lax.ppermute(value, "seq", [(s, s ^ 1) for s in range(lax.axis_size("seq"))])
+
+
+def place():
+    own = lax.axis_index("seq")
+    return own // 2, own % 2, lax.axis_size("seq") // 2
+
+
+def order(chips):
+    near = []
+    for step in range(1, chips // 2 + 1):
+        near += [step] if 2 * step == chips else [step, chips - step]
+    return near
+
+
 def gather_rows(local):
-    return lax.all_gather(local, "seq", axis=0, tiled=True)
-
-
-def scatter_rows(partial):
-    return lax.psum_scatter(
-        partial.astype(BF), "seq", scatter_dimension=0, tiled=True
-    ).astype(F32)
-
-
-def columns_in(weight, blocks):
-    groups = lax.axis_size("seq")
-    rows, width = weight.shape
-    part = width // (blocks * groups)
-    swapped = lax.all_to_all(
-        weight.reshape(rows, blocks, groups, part), "seq", split_axis=2, concat_axis=0, tiled=True
-    ).reshape(groups * rows, blocks * part)
-    return lax.all_gather(swapped, "fsdp", axis=0, tiled=True)
-
-
-def columns_out(grad, blocks):
-    groups = lax.axis_size("seq")
-    part = grad.shape[1] // blocks
+    chip, core, chips = place()
+    parts = {0: local}
+    for step in order(chips):
+        parts[step] = turn(local, step)
+    mine = [parts[step] for step in range(chips)]
+    return jnp.concatenate(mine + [swap(part) for part in mine], axis=0)
+
+
+def scatter_rows(left_side, weight, product):
+    chip, core, chips = place()
+    half = left_side.shape[0] // 2
+    rows = half // chips
+    other = swap(product(left_side[half:], weight).astype(BF))
+    total = product(left_side[:half], weight) + other.astype(F32)
+    parts = total.astype(BF)
+    result = total[:rows]
+    for step in order(chips):
+        result = result + turn(parts[step * rows : (step + 1) * rows], -step).astype(F32)
+    return result
+
+
+def unroll(parts):
+    chip, core, chips = place()
+    return lax.dynamic_slice_in_dim(
+        jnp.concatenate([parts, parts], axis=0), (chips - chip) % chips, chips, 0
+    )
+
+
+def by_core(mine, other, axis):
+    chip, core, chips = place()
+    return jnp.where(
+        core == 0, jnp.stack([mine, other], axis=axis), jnp.stack([other, mine], axis=axis)
+    )
+
+
+def columns_in(weight):
+    chip, core, chips = place()
+    rows, groups, cols = weight.shape
+    pairs = weight.reshape(rows, chips, 2 * cols)
+
+    def share(step):
+        return lax.dynamic_index_in_dim(pairs, (chip + step) % chips, 1, keepdims=False)
+
+    parts = {0: share(0)}
+    for step in order(chips):
+        parts[chips - step] = turn(share(step), -step)
+    stacked = unroll(jnp.stack([parts[step] for step in range(chips)])).reshape(
+        chips, rows, 2, cols
+    )
+    mine = lax.dynamic_index_in_dim(stacked, core, 2, keepdims=False)
+    other = swap(lax.dynamic_index_in_dim(stacked, 1 - core, 2, keepdims=False))
+    local = by_core(mine, other, 1).reshape(groups * rows, cols)
+    return lax.all_gather(local, "fsdp", axis=0, tiled=True)
+
+
+def columns_out(grad):
+    chip, core, chips = place()
+    cols = grad.shape[1]
     summed = lax.psum_scatter(grad.astype(BF), "fsdp", scatter_dimension=0, tiled=True)
-    rows = summed.shape[0] // groups
-    swapped = lax.all_to_all(
-        summed.reshape(groups * rows, blocks, 1, part),
-        "seq",
-        split_axis=0,
-        concat_axis=2,
-        tiled=True,
-    )
-    return swapped.reshape(rows, blocks * groups * part).astype(F32)
+    rows = summed.shape[0] // (2 * chips)
+    stacked = summed.reshape(chips, 2, rows, cols)
+    mine = lax.dynamic_index_in_dim(stacked, core, 1, keepdims=False)
+    other = swap(lax.dynamic_index_in_dim(stacked, 1 - core, 1, keepdims=False))
+    pairs = by_core(mine, other, 2)
+
+    def share(step):
+        return lax.dynamic_index_in_dim(pairs, (chip + step) % chips, 0, keepdims=False)
+
+    parts = {0: share(0)}
+    for step in order(chips):
+        parts[chips - step] = turn(share(step), -step)
+    natural = unroll(jnp.stack([parts[step] for step in range(chips)]))
+    return jnp.moveaxis(natural, 0, 1).reshape(rows, 2 * chips, cols)
 
 
 def rows_in(weight):
@@ -100,6 +162,37 @@
     return lax.psum_scatter(
         grad.astype(BF), "fsdp", scatter_dimension=0, tiled=True
     ).astype(F32)
+
+
+def sum_to_owners(values):
+    for axis in ALL:
+        size, own = lax.axis_size(axis), lax.axis_index(axis)
+        bit = size // 2
+        while bit:
+            halves = values.reshape(2, values.shape[0] // 2, values.shape[1])
+            mine = (own // bit) % 2
+            keep = lax.dynamic_index_in_dim(halves, mine, 0, keepdims=False)
+            give = lax.dynamic_index_in_dim(halves, 1 - mine, 0, keepdims=False)
+            values = keep + lax.ppermute(give, axis, [(s, s ^ bit) for s in range(size)])
+            bit //= 2
+    return values[0]
+
+
+def split_columns(weight, blocks):
+    groups = lax.axis_size("seq")
+    rows, width = weight.shape
+    return jnp.moveaxis(
+        weight.reshape(rows, blocks, groups, width // (blocks * groups)), 1, 2
+    ).reshape(rows, groups, width // groups)
+
+
+def join_columns(weight, blocks):
+    rows, groups, cols = weight.shape
+    return (
+        jnp.moveaxis(weight.reshape(rows, groups, blocks, cols // blocks), 2, 1)
+        .reshape(rows, groups * cols)
+        .astype(F32)
+    )
 
 
 def body(
@@ -124,38 +217,68 @@
     length = local_rows * groups
     scale = HD ** (-0.5)
     own = lax.axis_index("seq")
+    chip, core, chips = place()
+    weight_rows = query_weight.shape[0]
     aligned = H % (shards * groups) == 0
     head_blocks = shards if aligned else 1
+    hw = heads * HD
 
     inputs = tokens.reshape(local_rows, width).astype(F32)
+    keep_mask = valid.reshape(local_rows).astype(F32)
+    spread = local_rows // weight_rows
+    own_segments = segments.reshape(weight_rows, spread)
+    extra = jnp.concatenate(
+        [
+            attention_gain[:, None],
+            mlp_gain[:, None],
+            jnp.full((weight_rows, 1), jnp.sum(keep_mask)).astype(BF),
+            (own_segments // 256).astype(BF),
+            (own_segments % 256).astype(BF),
+        ],
+        axis=1,
+    )
+    extra = jnp.pad(extra, ((0, 0), (0, 128 - extra.shape[1])))
+    attention_in = columns_in(
+        jnp.concatenate(
+            [split_columns(w, head_blocks) for w in (query_weight, key_weight, value_weight)]
+            + [jnp.broadcast_to(extra[:, None], (weight_rows, groups, 128))],
+            axis=2,
+        )
+    )
+    qkv_weight = attention_in[:, : 3 * hw]
+    extras = attention_in[:, 3 * hw :].astype(F32)
+    first_gain, second_gain = extras[:, 0], extras[:, 1]
+    count = jnp.sum(extras[::weight_rows, 2])
+    table = lax.dynamic_slice_in_dim(
+        extras, lax.axis_index("fsdp") * groups * weight_rows, groups * weight_rows, 0
+    ).astype(jnp.int32)
+    segment_blocks = (table[:, 3 : 3 + spread] * 256 + table[:, 3 + spread : 3 + 2 * spread]).reshape(
+        groups, local_rows
+    )
+    relative = jnp.arange(groups, dtype=jnp.int32)
+    block_of = (chip + relative % chips) % chips * 2 + (core + relative // chips) % 2
+    segment = segment_blocks[block_of].reshape(length)
+    places = (
+        block_of[:, None] * local_rows + jnp.arange(local_rows, dtype=jnp.int32)[None, :]
+    ).reshape(length)
+
     tokens_all = gather_rows(tokens.reshape(local_rows, width)).astype(F32)
-    segment = lax.all_gather(segments, "seq", axis=1, tiled=True).reshape(length)
-    gains = lax.all_gather(
-        jnp.stack([attention_gain, mlp_gain], axis=1), ALL, axis=0, tiled=True
-    ).astype(F32)
-    first_gain, second_gain = gains[:, 0], gains[:, 1]
     normed = rms_norm(tokens_all, first_gain).astype(BF)
-
-    qkv_weight = jnp.concatenate(
-        [columns_in(w, head_blocks) for w in (query_weight, key_weight, value_weight)], axis=1
-    )
     if aligned:
         out_weight = rows_in(output_weight)
     else:
         out_weight = lax.dynamic_slice_in_dim(
-            lax.all_gather(output_weight, ALL, axis=0, tiled=True),
-            own * heads * HD,
-            heads * HD,
-            0,
+            lax.all_gather(output_weight, ALL, axis=0, tiled=True), own * hw, hw, 0
         )
-    gate_up_weight = jnp.concatenate(
-        [columns_in(gate_weight, shards), columns_in(up_weight, shards)], axis=1
+    gate_up_weight = columns_in(
+        jnp.concatenate(
+            [split_columns(gate_weight, shards), split_columns(up_weight, shards)], axis=2
+        )
     )
     down_full = rows_in(down_weight)
 
-    hw = heads * HD
     qkv = matmul(normed, qkv_weight)
-    cosine, sine = rope_tables(length)
+    cosine, sine = rope_tables(places)
 
     def rotated(values):
         return rotate(values.reshape(length, heads, HD), cosine, sine)
@@ -163,7 +286,6 @@
     query = rotated(qkv[:, :hw]).astype(BF)
     key = rotated(qkv[:, hw : 2 * hw]).astype(BF)
     value = qkv[:, 2 * hw :].astype(BF).reshape(length, heads, HD)
-    places = jnp.arange(length, dtype=jnp.int32)
     allowed = (segment[:, None] == segment[None, :]) & (places[None, :] <= places[:, None])
     scores = jnp.einsum("qhd,khd->hqk", query, key, preferred_element_type=F32) * scale
     scores = jnp.where(allowed[None], scores, MASKED)
@@ -177,34 +299,29 @@
         .astype(BF)
         .reshape(length, hw)
     )
-    after_attention = inputs + scatter_rows(matmul(mixed, out_weight))
-    normed_two_own = rms_norm(after_attention, second_gain).astype(BF)
-    normed_two = gather_rows(normed_two_own)
+    after_attention = inputs + scatter_rows(mixed, out_weight, matmul)
+    normed_two = gather_rows(rms_norm(after_attention, second_gain).astype(BF))
     gate_up = matmul(normed_two, gate_up_weight)
     hidden_width = gate_up.shape[1] // 2
     gate_value, up_value = gate_up[:, :hidden_width], gate_up[:, hidden_width:]
     hidden = gated(gate_value, up_value).astype(BF)
-    result = after_attention + scatter_rows(matmul(hidden, down_full))
-    keep_mask = valid.reshape(local_rows).astype(F32)
+    result = after_attention + scatter_rows(hidden, down_full, matmul)
     difference = result - teacher.reshape(local_rows, width).astype(F32)
-    count, error_sum = lax.psum(
-        (jnp.sum(keep_mask), jnp.sum(keep_mask[:, None] * difference * difference)), ALL
-    )
-    loss = error_sum / count
+    error_sum = jnp.sum(keep_mask[:, None] * difference * difference)
     grad_result = 2.0 / count * keep_mask[:, None] * difference
     grad_branch = gather_rows(grad_result.astype(BF))
     grad_hidden = against(grad_branch, down_full)
     unused, gate_pull = jax.vjp(gated, gate_value, up_value)
     grad_gate, grad_upward = gate_pull(grad_hidden)
     gate_up_grad = jnp.concatenate([grad_gate.astype(BF), grad_upward.astype(BF)], axis=1)
-    grad_normed_two = scatter_rows(against(gate_up_grad, gate_up_weight))
+    grad_normed_two = scatter_rows(gate_up_grad, gate_up_weight, against)
     unused, second_pull = jax.vjp(rms_norm, after_attention, second_gain)
     grad_after, second_gain_grad = second_pull(grad_normed_two)
     grad_after = grad_after + grad_result
     down_sum = rows_out(transposed(hidden, grad_branch))
-    gate_up_weight_grad = transposed(normed_two, gate_up_grad)
-    gate_sum = columns_out(gate_up_weight_grad[:, :hidden_width], shards)
-    up_sum = columns_out(gate_up_weight_grad[:, hidden_width:], shards)
+    gate_up_sum = columns_out(transposed(normed_two, gate_up_grad))
+    gate_sum = join_columns(gate_up_sum[:, :, :hidden_width], shards)
+    up_sum = join_columns(gate_up_sum[:, :, hidden_width:], shards)
 
     grad_out = gather_rows(grad_after.astype(BF))
     grad_mixed = against(grad_out, out_weight).astype(BF).reshape(length, heads, HD)
@@ -242,34 +359,39 @@
         ],
         axis=1,
     )
-    grad_normed = scatter_rows(against(qkv_grad, qkv_weight))
+    qkv_sum = columns_out(transposed(normed, qkv_grad))
+    query_sum, key_sum, value_sum = (
+        join_columns(qkv_sum[:, :, i * hw : (i + 1) * hw], head_blocks) for i in range(3)
+    )
+    grad_normed = scatter_rows(qkv_grad, qkv_weight, against)
     unused, first_pull = jax.vjp(rms_norm, inputs, first_gain)
     grad_inputs, first_gain_grad = first_pull(grad_normed)
     grad_inputs = grad_inputs + grad_after
-    qkv_weight_grad = transposed(normed, qkv_grad)
-    query_sum, key_sum, value_sum = (
-        columns_out(qkv_weight_grad[:, i * hw : (i + 1) * hw], head_blocks) for i in range(3)
-    )
-    gain_sums = lax.psum_scatter(
-        jnp.stack([first_gain_grad, second_gain_grad], axis=1),
-        ALL,
-        scatter_dimension=0,
-        tiled=True,
+    devices = shards * groups
+    sums = sum_to_owners(
+        jnp.concatenate(
+            [
+                first_gain_grad.reshape(devices, weight_rows),
+                second_gain_grad.reshape(devices, weight_rows),
+                jnp.full((devices, 128), error_sum),
+            ],
+            axis=1,
+        )
     )
     output_shape = (sequences, local_rows, width)
     return (
         result.reshape(output_shape).astype(BF),
-        loss,
+        sums[2 * weight_rows] / count,
         grad_inputs.reshape(output_shape),
         query_sum,
         key_sum,
         value_sum,
         output_sum,
-        gain_sums[:, 0],
+        sums[:weight_rows],
         gate_sum,
         up_sum,
         down_sum,
-        gain_sums[:, 1],
+        sums[weight_rows : 2 * weight_rows],
     )
 
 

time: 1230 us -> 958 us (0.78)
  blocking collectives: 256 us -> 0 us
  waiting for transfers between devices: 672 us -> 538 us
  local copies, waits for them, and re-layouts: 76.5 us -> 133 us
  starting transfers between devices: 23.7 us -> 56.9 us
    ppermute x0 -> x65, waiting for transfers between devices: none -> 456 us  [the longest x36 423 us: turn(): lax.ppermute(value, 'seq', [(s, (s - 2 * steps) % size) for s in range(si...]
    all_gather x9 -> x2, waiting for transfers between devices: 265 us -> 0.02 us  [columns_in(): return lax.all_gather(local, 'fsdp', axis=0, tiled=True)]
    unnamed x24 -> x8, waiting for transfers between devices: 134 us -> 0.13 us
    all_to_all x5 -> x0, blocking collectives: 126 us -> none  [columns_in(): lax.all_to_all(weight.reshape(rows, blocks, groups, part), 'seq', split_a...]
    reduce_scatter x4 -> x0, waiting for transfers between devices: 91.9 us -> none  [scatter_rows(): lax.psum_scatter(partial.astype(BF), 'seq', scatter_dimension=0, tiled=True)]
    psum x2 -> x0, blocking collectives: 81.7 us -> none  [body(): lax.psum((jnp.sum(keep_mask), jnp.sum(keep_mask[:, None] * difference * d...]
    ppermute x0 -> x65, starting transfers between devices: none -> 56.2 us  [the longest x36 48.7 us: turn(): lax.ppermute(value, 'seq', [(s, (s - 2 * steps) % size) for s in range(si...]
    all_gather x2 -> x0, blocking collectives: 48.1 us -> none  [the longest x1 39.3 us: body(): lax.all_gather(jnp.stack([attention_gain, mlp_gain], axis=1), ALL, axis=0...]
  transfers between devices with their start and end apart: 28 -> 73, of which waited for: 20 -> 40; matrix products, arithmetic and copies ran while one was open for 15% -> 21% of each run, Pallas kernels for 0% -> 0%
where the time goes in v2:
time: 958 us; the launch traced here: 943 us
  waiting for transfers between devices  538 us (56%)
  matrix products  148 us (15%)
  local copies, waits for them, and re-layouts  133 us (14%)
  starting transfers between devices  56.9 us (6%)
  other arithmetic  47.6 us (5%)
  between operations  19.1 us (2%)
    ppermute x36, waiting for transfers between devices, turn(): lax.ppermute(value, 'seq', [(s, (s - 2 * steps) % size) for s in range(si...  423 us
    reduce_scatter x2, waiting for transfers between devices, columns_out(): lax.psum_scatter(grad.astype(BF), 'fsdp', scatter_dimension=0, tiled=True)  81.9 us
    unnamed x161, local copies, waits for them, and re-layouts  49.8 us
    ppermute x36, starting transfers between devices, turn(): lax.ppermute(value, 'seq', [(s, (s - 2 * steps) % size) for s in range(si...  48.7 us
    dot_general x6, matrix products, against(): lax.dot_general(left_side, right_side, (((1,), (1,)), ((), ())), preferre...  37 us
    dot_general x6, matrix products, matmul(): return jnp.dot(left_side, right_side, preferred_element_type=F32)  33.8 us
    dot_general x4, matrix products, transposed(): lax.dot_general(left_side, right_side, (((0,), (0,)), ((), ())), preferre...  31.5 us
    convert_element_type x16, local copies, waits for them, and re-layouts, join_columns(): return jnp.moveaxis(weight.reshape(rows, groups, blocks, cols // blocks),...  30.8 us
  transfers between devices with their start and end apart: 73, of which 40 were waited for; matrix products, arithmetic and copies ran while one was open for 21% of the time, Pallas kernels for 0%

profile of v2, /device:TPU:0, one launch (start us, length us, event | category | flops | bytes accessed | tf_op | source)
XLA Modules:
  0.0 942.9 jit_solution(4669022301912787363)
XLA Ops:
  31.9 12.7 %collective-permute-done.8 = bf16[64,1792]{1,0:T(8,128)(2,1)S(1)} collective-permute-done((bf16[64,1792]{1,0:T(8,128)(2,1)S(1)}, bf16[64,1792]{1,0:T(8,128)(2,1)S(1)}, u32[]{:S(2)}, u32[]{:S(2)}) %collective-permute-start.8) | collective-permute-done | bytes 229408 | tf_op jit(solution)/shard_map/ppermute | solution.py:62
  81.9 34.1 %collective-permute-done.23 = bf16[64,4096]{1,0:T(8,128)(2,1)S(1)} collective-permute-done((bf16[64,4096]{1,0:T(8,128)(2,1)}, bf16[64,4096]{1,0:T(8,128)(2,1)S(1)}, u32[]{:S(2)}, u32[]{:S(2)}) %collective-permute-start.23) | collective-permute-done | bytes 524320 | tf_op jit(solution)/shard_map/ppermute | solution.py:62
  134.2 8.1 collective-permute-done
  143.1 30.6 %collective-permute-done.1 = bf16[128,2048]{1,0:T(8,128)(2,1)S(1)} collective-permute-done((bf16[128,2048]{1,0:T(8,128)(2,1)S(1)}, bf16[128,2048]{1,0:T(8,128)(2,1)S(1)}, u32[]{:S(2)}, u32[]{:S(2)}) %collective-permute-start.1) | collective-permute-done | bytes 524320 | tf_op jit(solution)/shard_map/ppermute | solution.py:62
  198.9 11.5 %fusion.124 = (f32[4,1024]{1,0:T(4,128)}, f32[4,1024,1024]{1,2,0:T(8,128)}) fusion(pred[1024,1024]{0,1:T(8,128)(4,1)S(1)} %compare_and_fusion, bf16[1024,4,32]{0,2,1:T(8,128)(2,1)S(1)} %get-tuple-element.91, bf16[1024,4,32]{0,2,1:T(8,128)(2,1)S(1)} %get-tuple-element.92, bf16[1024,4,32]{0,2,1:T(8,128)(2,1)} %get-tuple-element.68, ...), kind=kOutput, calls=%fused_computation.343 | convolution fusion | flops 555746304 | bytes 18890752 | tf_op jit(solution)/shard_map/sub | solution.py:293
  232.0 12.9 %collective-permute-done.12 = bf16[128,2048]{1,0:T(8,128)(2,1)S(1)} collective-permute-done((bf16[128,2048]{1,0:T(8,128)(2,1)}, bf16[128,2048]{1,0:T(8,128)(2,1)S(1)}, u32[]{:S(2)}, u32[]{:S(2)}) %collective-permute-start.12) | collective-permute-done | bytes 524320 | tf_op jit(solution)/shard_map/ppermute | solution.py:62
  245.0 8.6 collective-permute-done.13
  253.5 23.6 %collective-permute-done.14 = bf16[128,2048]{1,0:T(8,128)(2,1)} collective-permute-done((bf16[128,2048]{1,0:T(8,128)(2,1)}, bf16[128,2048]{1,0:T(8,128)(2,1)}, u32[]{:S(2)}, u32[]{:S(2)}) %collective-permute-start.14) | collective-permute-done | bytes 524320 | tf_op jit(solution)/shard_map/ppermute | solution.py:62
  282.8 12.8 %collective-permute-done.15 = bf16[128,2048]{1,0:T(8,128)(2,1)S(1)} collective-permute-done((bf16[128,2048]{1,0:T(8,128)(2,1)S(1)}, bf16[128,2048]{1,0:T(8,128)(2,1)S(1)}, u32[]{:S(2)}, u32[]{:S(2)}) %collective-permute-start.15) | collective-permute-done | bytes 524320 | tf_op jit(solution)/shard_map/ppermute | solution.py:62
  296.4 29.2 %collective-permute-done.16 = bf16[128,2048]{1,0:T(8,128)(2,1)S(1)} collective-permute-done((bf16[128,2048]{1,0:T(8,128)(2,1)S(1)}, bf16[128,2048]{1,0:T(8,128)(2,1)S(1)}, u32[]{:S(2)}, u32[]{:S(2)}) %collective-permute-start.16) | collective-permute-done | bytes 524320 | tf_op jit(solution)/shard_map/ppermute | solution.py:62
  331.3 12.6 %fusion.128 = f32[1024,2048]{1,0:T(8,128)S(1)} fusion(bf16[1024,2048]{1,0:T(8,128)(2,1)} %constant_dynamic-update-slice_fusion.10, bf16[2048,2048]{1,0:T(8,128)(2,1)} %all-gather.9.cloned.1.call-done), kind=kOutput, calls=%fused_computation.347 | convolution fusion | flops 8589934592 | bytes 20971520 | tf_op jit(solution)/shard_map/dot_general | solution.py:41
  370.3 11.2 %collective-permute-done.27 = bf16[128,2048]{1,0:T(8,128)(2,1)} collective-permute-done((bf16[128,2048]{1,0:T(8,128)(2,1)}, bf16[128,2048]{1,0:T(8,128)(2,1)}, u32[]{:S(2)}, u32[]{:S(2)}) %collective-permute-start.27) | collective-permute-done | bytes 524320 | tf_op jit(solution)/shard_map/ppermute | solution.py:62
  381.6 9.6 %collective-permute-done.28 = bf16[128,2048]{1,0:T(8,128)(2,1)} collective-permute-done((bf16[128,2048]{1,0:T(8,128)(2,1)}, bf16[128,2048]{1,0:T(8,128)(2,1)}, u32[]{:S(2)}, u32[]{:S(2)}) %collective-permute-start.28) | collective-permute-done | bytes 524320 | tf_op jit(solution)/shard_map/ppermute | solution.py:62
  391.2 23.3 %collective-permute-done.29 = bf16[128,2048]{1,0:T(8,128)(2,1)} collective-permute-done((bf16[128,2048]{1,0:T(8,128)(2,1)}, bf16[128,2048]{1,0:T(8,128)(2,1)}, u32[]{:S(2)}, u32[]{:S(2)}) %collective-permute-start.29) | collective-permute-done | bytes 524320 | tf_op jit(solution)/shard_map/ppermute | solution.py:62
  419.7 13.3 %collective-permute-done.30 = bf16[128,2048]{1,0:T(8,128)(2,1)S(1)} collective-permute-done((bf16[128,2048]{1,0:T(8,128)(2,1)S(1)}, bf16[128,2048]{1,0:T(8,128)(2,1)S(1)}, u32[]{:S(2)}, u32[]{:S(2)}) %collective-permute-start.30) | collective-permute-done | bytes 524320 | tf_op jit(solution)/shard_map/ppermute | solution.py:62
  433.1 29.8 %collective-permute-done.31 = bf16[128,2048]{1,0:T(8,128)(2,1)S(1)} collective-permute-done((bf16[128,2048]{1,0:T(8,128)(2,1)S(1)}, bf16[128,2048]{1,0:T(8,128)(2,1)S(1)}, u32[]{:S(2)}, u32[]{:S(2)}) %collective-permute-start.31) | collective-permute-done | bytes 524320 | tf_op jit(solution)/shard_map/ppermute | solution.py:62
  465.7 9.9 %multiply_convert_fusion.1 = (bf16[1024,1024]{1,0:T(8,128)(2,1)S(1)}, bf16[1024,1024]{1,0:T(8,128)(2,1)S(1)}) fusion(f32[1024,2048]{1,0:T(8,128)S(1)} %bitcast.266, bf16[1024,2048]{1,0:T(8,128)(2,1)S(1)} %constant_dynamic-update-slice_fusion.18, bf16[1024,2048]{1,0:T(8,128)(2,1)} %all-gather.11.cloned.1.call-done), kind=kOutput, calls=%fused_computation.28 | convolution fusion | flops 4309647360 | bytes 20971520 | tf_op jit(solution)/shard_map/dot_general | solution.py:51
  475.6 9.8 %convolution_convert_fusion.6 = bf16[512,2048]{1,0:T(8,128)(2,1)S(1)} fusion(bf16[2048,2048]{1,0:T(8,128)(2,1)} %all-gather.9.cloned.1.call-done, bf16[1024,1024]{1,0:T(8,128)(2,1)S(1)} %get-tuple-element.34, bf16[1024,1024]{1,0:T(8,128)(2,1)S(1)} %get-tuple-element.33), kind=kOutput, calls=%fused_computation.44 | convolution fusion | flops 4300210176 | bytes 14680064 | tf_op jit(solution)/shard_map/dot_general | solution.py:51
  502.2 11.6 %collective-permute-done.38 = bf16[128,2048]{1,0:T(8,128)(2,1)S(1)} collective-permute-done((bf16[128,2048]{1,0:T(8,128)(2,1)S(1)}, bf16[128,2048]{1,0:T(8,128)(2,1)S(1)}, u32[]{:S(2)}, u32[]{:S(2)}) %collective-permute-start.38) | collective-permute-done | bytes 524320 | tf_op jit(solution)/shard_map/ppermute | solution.py:62
  513.9 10.1 %collective-permute-done.39 = bf16[128,2048]{1,0:T(8,128)(2,1)S(1)} collective-permute-done((bf16[128,2048]{1,0:T(8,128)(2,1)S(1)}, bf16[128,2048]{1,0:T(8,128)(2,1)S(1)}, u32[]{:S(2)}, u32[]{:S(2)}) %collective-permute-start.39) | collective-permute-done | bytes 524320 | tf_op jit(solution)/shard_map/ppermute | solution.py:62
  523.9 22.8 %collective-permute-done.40 = bf16[128,2048]{1,0:T(8,128)(2,1)S(1)} collective-permute-done((bf16[128,2048]{1,0:T(8,128)(2,1)S(1)}, bf16[128,2048]{1,0:T(8,128)(2,1)S(1)}, u32[]{:S(2)}, u32[]{:S(2)}) %collective-permute-start.40) | collective-permute-done | bytes 524320 | tf_op jit(solution)/shard_map/ppermute | solution.py:62
  551.4 13.0 %collective-permute-done.41 = bf16[128,2048]{1,0:T(8,128)(2,1)S(1)} collective-permute-done((bf16[128,2048]{1,0:T(8,128)(2,1)S(1)}, bf16[128,2048]{1,0:T(8,128)(2,1)S(1)}, u32[]{:S(2)}, u32[]{:S(2)}) %collective-permute-start.41) | collective-permute-done | bytes 524320 | tf_op jit(solution)/shard_map/ppermute | solution.py:62
  564.4 29.9 %collective-permute-done.42 = bf16[128,2048]{1,0:T(8,128)(2,1)S(1)} collective-permute-done((bf16[128,2048]{1,0:T(8,128)(2,1)S(1)}, bf16[128,2048]{1,0:T(8,128)(2,1)S(1)}, u32[]{:S(2)}, u32[]{:S(2)}) %collective-permute-start.42) | collective-permute-done | bytes 524320 | tf_op jit(solution)/shard_map/ppermute | solution.py:62
  599.2 13.8 %multiply_reduce_fusion = (f32[4,1024]{1,0:T(4,128)S(1)}, f32[4,1024,1024]{1,2,0:T(8,128)}) fusion(f32[4,1024,1024]{1,2,0:T(8,128)} %get-tuple-element.103, f32[4,1024]{1,0:T(4,128)S(1)} %copy-done.31, bf16[1024,4,64]{0,2,1:T(8,128)(2,1)} %bitcast.322, bf16[1024,4,64]{0,2,1:T(8,128)(2,1)S(1)} %bitcast.308), kind=kOutput, calls=%fused_computation.3 | convolution fusion | flops 549449728 | bytes 34635776 | tf_op jit(solution)/shard_map/qhd,khd->hqk/dot_general | solution.py:340
  632.1 8.6 fusion.35
  646.4 9.5 %convolution_convert_fusion.1 = bf16[1024,2048]{1,0:T(8,128)(2,1)} fusion(bf16[1024,1024]{1,0:T(8,128)(2,1)} %multiply_convert_fusion.2, bf16[1024,2048]{1,0:T(8,128)(2,1)} %copy-done.30), kind=kOutput, calls=%fused_computation.39 | convolution fusion | flops 4297064448 | bytes 10485760 | tf_op jit(solution)/shard_map/dot_general | solution.py:45
  656.1 14.1 %convolution_convert_fusion = bf16[2048,2048]{1,0:T(8,128)(2,1)} fusion(bf16[1024,2048]{1,0:T(8,128)(2,1)} %constant_dynamic-update-slice_fusion.10, bf16[1024,1024]{1,0:T(8,128)(2,1)} %copy-done.39, bf16[1024,1024]{1,0:T(8,128)(2,1)} %copy-done.40), kind=kOutput, calls=%fused_computation.16 | convolution fusion | flops 8602517504 | bytes 16777216 | tf_op jit(solution)/shard_map/dot_general | solution.py:45
  689.2 11.2 %collective-permute-done.49 = bf16[128,2048]{1,0:T(8,128)(2,1)S(1)} collective-permute-done((bf16[128,2048]{1,0:T(8,128)(2,1)}, bf16[128,2048]{1,0:T(8,128)(2,1)S(1)}, u32[]{:S(2)}, u32[]{:S(2)}) %collective-permute-start.49) | collective-permute-done | bytes 524320 | tf_op jit(solution)/shard_map/ppermute | solution.py:62
  700.4 9.9 %collective-permute-done.50 = bf16[128,2048]{1,0:T(8,128)(2,1)S(1)} collective-permute-done((bf16[128,2048]{1,0:T(8,128)(2,1)}, bf16[128,2048]{1,0:T(8,128)(2,1)S(1)}, u32[]{:S(2)}, u32[]{:S(2)}) %collective-permute-start.50) | collective-permute-done | bytes 524320 | tf_op jit(solution)/shard_map/ppermute | solution.py:62
  710.3 22.9 %collective-permute-done.51 = bf16[128,2048]{1,0:T(8,128)(2,1)S(1)} collective-permute-done((bf16[128,2048]{1,0:T(8,128)(2,1)}, bf16[128,2048]{1,0:T(8,128)(2,1)S(1)}, u32[]{:S(2)}, u32[]{:S(2)}) %collective-permute-start.51) | collective-permute-done | bytes 524320 | tf_op jit(solution)/shard_map/ppermute | solution.py:62
  770.2 81.9 %reduce-scatter.9.cloned.1.call-done = bf16[512,2048]{1,0:T(8,128)(2,1)} async-done(((bf16[2048,2048]{1,0:T(8,128)(2,1)}), bf16[512,2048]{1,0:T(8,128)(2,1)}) %reduce-scatter.9.cloned.1.call-update) | async-done | bytes 2097168 | tf_op jit(solution)/shard_map/reduce_scatter | solution.py:140
  886.0 21.2 %collective-permute-done.63 = bf16[64,2,2048]{2,0,1:T(8,128)(2,1)} collective-permute-done((bf16[64,2,2048]{2,0,1:T(8,128)(2,1)}, bf16[64,2,2048]{2,0,1:T(8,128)(2,1)}, u32[]{:S(2)}, u32[]{:S(2)}) %collective-permute-start.63) | collective-permute-done | bytes 524320 | tf_op jit(solution)/shard_map/ppermute | solution.py:62
  (444 shorter events, 339.6 us)
Async XLA Ops:
  7.2 175.2 %all-gather.5.cloned.1.call-start = ((), (), s32[]{:S(2)}) async-start(), calls=%async_computation.4 | async-start | bytes 4587520 | tf_op jit(solution)/shard_map/all_gather | solution.py:134
  55.4 162.5 %all-gather.7.cloned.1.call-start = ((), (), s32[]{:S(2)}) async-start(), calls=%async_computation.5 | async-start | bytes 1310720 | tf_op jit(solution)/shard_map/all_gather | solution.py:158
  69.3 46.7 %collective-permute-start.23 = (bf16[64,4096]{1,0:T(8,128)(2,1)}, bf16[64,4096]{1,0:T(8,128)(2,1)S(1)}, u32[]{:S(2)}, u32[]{:S(2)}) collective-permute-start(bf16[64,4096]{1,0:T(8,128)(2,1)} %bitcast.253), channel_id=1, source_target_pairs={{0,4},{1,5},{2,6},{3,7},{4,0},{5,1},{6,2},{7,3},{8,12},{9,13},{10,... | collective-permute-start | bytes 1572872 | tf_op jit(solution)/shard_map/ppermute | solution.py:62
  72.9 43.2 %collective-permute-start.24 = (bf16[64,4096]{1,0:T(8,128)(2,1)}, bf16[64,4096]{1,0:T(8,128)(2,1)S(1)}, u32[]{:S(2)}, u32[]{:S(2)}) collective-permute-start(bf16[64,4096]{1,0:T(8,128)(2,1)} %bitcast.252), channel_id=1, source_target_pairs={{0,2},{1,3},{2,4},{3,5},{4,6},{5,7},{6,0},{7,1},{8,10},{9,11},{10,... | collective-permute-start | bytes 1572872 | tf_op jit(solution)/shard_map/ppermute | solution.py:62
  74.9 256.4 %all-gather.9.cloned.1.call-start = ((), (), s32[]{:S(2)}) async-start(), calls=%async_computation.6 | async-start | bytes 10485760 | tf_op jit(solution)/shard_map/all_gather | solution.py:134
  126.7 46.9 %collective-permute-start.1 = (bf16[128,2048]{1,0:T(8,128)(2,1)S(1)}, bf16[128,2048]{1,0:T(8,128)(2,1)S(1)}, u32[]{:S(2)}, u32[]{:S(2)}) collective-permute-start(bf16[128,2048]{1,0:T(8,128)(2,1)S(1)} %bitcast.269), channel_id=1, source_target_pairs={{0,4},{1,5},{2,6},{3,7},{4,0},{5,1},{6,2},{7,3},{8,12},{9,13},{10,... | collective-permute-start | bytes 1572872 | tf_op jit(solution)/shard_map/ppermute | solution.py:62
  127.5 47.0 %collective-permute-start.2 = (bf16[128,2048]{1,0:T(8,128)(2,1)S(1)}, bf16[128,2048]{1,0:T(8,128)(2,1)S(1)}, u32[]{:S(2)}, u32[]{:S(2)}) collective-permute-start(bf16[128,2048]{1,0:T(8,128)(2,1)S(1)} %bitcast.270), channel_id=1, source_target_pairs={{0,2},{1,3},{2,4},{3,5},{4,6},{5,7},{6,0},{7,1},{8,10},{9,11},{10,... | collective-permute-start | bytes 1572872 | tf_op jit(solution)/shard_map/ppermute | solution.py:62
  129.5 46.4 %collective-permute-start.3 = (bf16[128,2048]{1,0:T(8,128)(2,1)S(1)}, bf16[128,2048]{1,0:T(8,128)(2,1)S(1)}, u32[]{:S(2)}, u32[]{:S(2)}) collective-permute-start(bf16[128,2048]{1,0:T(8,128)(2,1)S(1)} %bitcast.271), channel_id=1, source_target_pairs={{0,1},{1,0},{2,3},{3,2},{4,5},{5,4},{6,7},{7,6},{8,9},{9,8},{10,11... | collective-permute-start | bytes 1572872 | tf_op jit(solution)/shard_map/ppermute | solution.py:66
  132.0 217.9 %all-gather.11.cloned.1.call-start = ((), (), s32[]{:S(2)}) async-start(), calls=%async_computation.7 | async-start | bytes 5242880 | tf_op jit(solution)/shard_map/all_gather | solution.py:158
  142.3 34.5 %collective-permute-start.4 = (bf16[128,2048]{1,0:T(8,128)(2,1)S(1)}, bf16[128,2048]{1,0:T(8,128)(2,1)S(1)}, u32[]{:S(2)}, u32[]{:S(2)}) collective-permute-start(bf16[128,2048]{1,0:T(8,128)(2,1)S(1)} %collective-permute-done), channel_id=1, source_target_pairs={{0,1},{1,0},{2,3},{3,2},{4,5},{5,4},{6,7},{7,6},{8,9},{9,8},{10,11... | collective-permute-start | bytes 1572872 | tf_op jit(solution)/shard_map/ppermute | solution.py:66
  232.0 45.1 %collective-permute-start.14 = (bf16[128,2048]{1,0:T(8,128)(2,1)}, bf16[128,2048]{1,0:T(8,128)(2,1)}, u32[]{:S(2)}, u32[]{:S(2)}) collective-permute-start(bf16[128,2048]{1,0:T(8,128)(2,1)} %get-tuple-element.61), channel_id=1, source_target_pairs={{0,4},{1,5},{2,6},{3,7},{4,0},{5,1},{6,2},{7,3},{8,12},{9,13},{10,... | collective-permute-start | bytes 1572872 | tf_op jit(solution)/shard_map/ppermute | solution.py:62
  232.0 513.7 %reduce-scatter.7.cloned.1.call-start = ((), (), s32[]{:S(2)}) async-start(), calls=%async_computation.9 | async-start | bytes 1310720 | tf_op jit(solution)/shard_map/reduce_scatter | solution.py:162
  282.0 43.7 %collective-permute-start.16 = (bf16[128,2048]{1,0:T(8,128)(2,1)S(1)}, bf16[128,2048]{1,0:T(8,128)(2,1)S(1)}, u32[]{:S(2)}, u32[]{:S(2)}) collective-permute-start(bf16[128,2048]{1,0:T(8,128)(2,1)S(1)} %get-tuple-element.28), channel_id=1, source_target_pairs={{0,4},{1,5},{2,6},{3,7},{4,0},{5,1},{6,2},{7,3},{8,12},{9,13},{10,... | collective-permute-start | bytes 1572872 | tf_op jit(solution)/shard_map/ppermute | solution.py:62
  282.0 44.6 %collective-permute-start.17 = (bf16[128,2048]{1,0:T(8,128)(2,1)S(1)}, bf16[128,2048]{1,0:T(8,128)(2,1)S(1)}, u32[]{:S(2)}, u32[]{:S(2)}) collective-permute-start(bf16[128,2048]{1,0:T(8,128)(2,1)S(1)} %get-tuple-element.28), channel_id=1, source_target_pairs={{0,2},{1,3},{2,4},{3,5},{4,6},{5,7},{6,0},{7,1},{8,10},{9,11},{10,... | collective-permute-start | bytes 1572872 | tf_op jit(solution)/shard_map/ppermute | solution.py:62
  282.8 45.1 %collective-permute-start.18 = (bf16[128,2048]{1,0:T(8,128)(2,1)S(1)}, bf16[128,2048]{1,0:T(8,128)(2,1)S(1)}, u32[]{:S(2)}, u32[]{:S(2)}) collective-permute-start(bf16[128,2048]{1,0:T(8,128)(2,1)S(1)} %get-tuple-element.28), channel_id=1, source_target_pairs={{0,1},{1,0},{2,3},{3,2},{4,5},{5,4},{6,7},{7,6},{8,9},{9,8},{10,11... | collective-permute-start | bytes 1572872 | tf_op jit(solution)/shard_map/ppermute | solution.py:66
  295.6 33.1 %collective-permute-start.19 = (bf16[128,2048]{1,0:T(8,128)(2,1)S(1)}, bf16[128,2048]{1,0:T(8,128)(2,1)S(1)}, u32[]{:S(2)}, u32[]{:S(2)}) collective-permute-start(bf16[128,2048]{1,0:T(8,128)(2,1)S(1)} %collective-permute-done.15), channel_id=1, source_target_pairs={{0,1},{1,0},{2,3},{3,2},{4,5},{5,4},{6,7},{7,6},{8,9},{9,8},{10,11... | collective-permute-start | bytes 1572872 | tf_op jit(solution)/shard_map/ppermute | solution.py:66
  368.5 46.0 %collective-permute-start.29 = (bf16[128,2048]{1,0:T(8,128)(2,1)}, bf16[128,2048]{1,0:T(8,128)(2,1)}, u32[]{:S(2)}, u32[]{:S(2)}) collective-permute-start(bf16[128,2048]{1,0:T(8,128)(2,1)} %get-tuple-element.52), channel_id=1, source_target_pairs={{0,4},{1,5},{2,6},{3,7},{4,0},{5,1},{6,2},{7,3},{8,12},{9,13},{10,... | collective-permute-start | bytes 1572872 | tf_op jit(solution)/shard_map/ppermute | solution.py:62
  419.1 43.8 %collective-permute-start.31 = (bf16[128,2048]{1,0:T(8,128)(2,1)S(1)}, bf16[128,2048]{1,0:T(8,128)(2,1)S(1)}, u32[]{:S(2)}, u32[]{:S(2)}) collective-permute-start(bf16[128,2048]{1,0:T(8,128)(2,1)S(1)} %get-tuple-element.26), channel_id=1, source_target_pairs={{0,4},{1,5},{2,6},{3,7},{4,0},{5,1},{6,2},{7,3},{8,12},{9,13},{10,... | collective-permute-start | bytes 1572872 | tf_op jit(solution)/shard_map/ppermute | solution.py:62
  419.1 43.9 %collective-permute-start.32 = (bf16[128,2048]{1,0:T(8,128)(2,1)S(1)}, bf16[128,2048]{1,0:T(8,128)(2,1)S(1)}, u32[]{:S(2)}, u32[]{:S(2)}) collective-permute-start(bf16[128,2048]{1,0:T(8,128)(2,1)S(1)} %get-tuple-element.26), channel_id=1, source_target_pairs={{0,2},{1,3},{2,4},{3,5},{4,6},{5,7},{6,0},{7,1},{8,10},{9,11},{10,... | collective-permute-start | bytes 1572872 | tf_op jit(solution)/shard_map/ppermute | solution.py:62
  419.7 43.9 %collective-permute-start.33 = (bf16[128,2048]{1,0:T(8,128)(2,1)S(1)}, bf16[128,2048]{1,0:T(8,128)(2,1)S(1)}, u32[]{:S(2)}, u32[]{:S(2)}) collective-permute-start(bf16[128,2048]{1,0:T(8,128)(2,1)S(1)} %get-tuple-element.26), channel_id=1, source_target_pairs={{0,1},{1,0},{2,3},{3,2},{4,5},{5,4},{6,7},{7,6},{8,9},{9,8},{10,11... | collective-permute-start | bytes 1572872 | tf_op jit(solution)/shard_map/ppermute | solution.py:66
  501.1 45.6 %collective-permute-start.40 = (bf16[128,2048]{1,0:T(8,128)(2,1)S(1)}, bf16[128,2048]{1,0:T(8,128)(2,1)S(1)}, u32[]{:S(2)}, u32[]{:S(2)}) collective-permute-start(bf16[128,2048]{1,0:T(8,128)(2,1)S(1)} %get-tuple-element.49), channel_id=1, source_target_pairs={{0,4},{1,5},{2,6},{3,7},{4,0},{5,1},{6,2},{7,3},{8,12},{9,13},{10,... | collective-permute-start | bytes 1572872 | tf_op jit(solution)/shard_map/ppermute | solution.py:62
  550.8 43.5 %collective-permute-start.42 = (bf16[128,2048]{1,0:T(8,128)(2,1)S(1)}, bf16[128,2048]{1,0:T(8,128)(2,1)S(1)}, u32[]{:S(2)}, u32[]{:S(2)}) collective-permute-start(bf16[128,2048]{1,0:T(8,128)(2,1)S(1)} %get-tuple-element.22), channel_id=1, source_target_pairs={{0,4},{1,5},{2,6},{3,7},{4,0},{5,1},{6,2},{7,3},{8,12},{9,13},{10,... | collective-permute-start | bytes 1572872 | tf_op jit(solution)/shard_map/ppermute | solution.py:62
  550.8 43.5 %collective-permute-start.43 = (bf16[128,2048]{1,0:T(8,128)(2,1)S(1)}, bf16[128,2048]{1,0:T(8,128)(2,1)S(1)}, u32[]{:S(2)}, u32[]{:S(2)}) collective-permute-start(bf16[128,2048]{1,0:T(8,128)(2,1)S(1)} %get-tuple-element.22), channel_id=1, source_target_pairs={{0,2},{1,3},{2,4},{3,5},{4,6},{5,7},{6,0},{7,1},{8,10},{9,11},{10,... | collective-permute-start | bytes 1572872 | tf_op jit(solution)/shard_map/ppermute | solution.py:62
  551.4 43.6 %collective-permute-start.44 = (bf16[128,2048]{1,0:T(8,128)(2,1)S(1)}, bf16[128,2048]{1,0:T(8,128)(2,1)S(1)}, u32[]{:S(2)}, u32[]{:S(2)}) collective-permute-start(bf16[128,2048]{1,0:T(8,128)(2,1)S(1)} %get-tuple-element.22), channel_id=1, source_target_pairs={{0,1},{1,0},{2,3},{3,2},{4,5},{5,4},{6,7},{7,6},{8,9},{9,8},{10,11... | collective-permute-start | bytes 1572872 | tf_op jit(solution)/shard_map/ppermute | solution.py:66
  564.3 30.7 %collective-permute-start.45 = (bf16[128,2048]{1,0:T(8,128)(2,1)S(1)}, bf16[128,2048]{1,0:T(8,128)(2,1)S(1)}, u32[]{:S(2)}, u32[]{:S(2)}) collective-permute-start(bf16[128,2048]{1,0:T(8,128)(2,1)S(1)} %collective-permute-done.41), channel_id=1, source_target_pairs={{0,1},{1,0},{2,3},{3,2},{4,5},{5,4},{6,7},{7,6},{8,9},{9,8},{10,11... | collective-permute-start | bytes 1572872 | tf_op jit(solution)/shard_map/ppermute | solution.py:66
  631.0 122.1 %reduce-scatter.5.cloned.1.call-start = ((), (), s32[]{:S(2)}) async-start(), calls=%async_computation.8 | async-start | bytes 3932160 | tf_op jit(solution)/shard_map/reduce_scatter | solution.py:140
  646.3 116.6 %reduce-scatter.11.cloned.1.call-start = ((), (), s32[]{:S(2)}) async-start(), calls=%async_computation.11 | async-start | bytes 5242880 | tf_op jit(solution)/shard_map/reduce_scatter | solution.py:162
  655.9 196.2 %reduce-scatter.9.cloned.1.call-start = ((), (), s32[]{:S(2)}) async-start(), calls=%async_computation.10 | async-start | bytes 10485760 | tf_op jit(solution)/shard_map/reduce_scatter | solution.py:140
  687.4 45.9 %collective-permute-start.51 = (bf16[128,2048]{1,0:T(8,128)(2,1)}, bf16[128,2048]{1,0:T(8,128)(2,1)S(1)}, u32[]{:S(2)}, u32[]{:S(2)}) collective-permute-start(bf16[128,2048]{1,0:T(8,128)(2,1)} %get-tuple-element.46), channel_id=1, source_target_pairs={{0,4},{1,5},{2,6},{3,7},{4,0},{5,1},{6,2},{7,3},{8,12},{9,13},{10,... | collective-permute-start | bytes 1572872 | tf_op jit(solution)/shard_map/ppermute | solution.py:62
  765.7 88.4 %collective-permute-start.59 = (bf16[64,2,768]{2,0,1:T(8,128)(2,1)S(1)}, bf16[64,2,768]{2,0,1:T(8,128)(2,1)S(1)}, u32[]{:S(2)}, u32[]{:S(2)}) collective-permute-start(bf16[64,2,768]{2,0,1:T(8,128)(2,1)S(1)} %get-tuple-element.82), channel_id=1, source_target_pairs={{0,4},{1,5},{2,6},{3,7},{4,0},{5,1},{6,2},{7,3},{8,12},{9,13},{10,... | collective-permute-start | bytes 589832 | tf_op jit(solution)/shard_map/ppermute | solution.py:62
  767.8 86.4 %collective-permute-start.60 = (bf16[64,2,768]{2,0,1:T(8,128)(2,1)S(1)}, bf16[64,2,768]{2,0,1:T(8,128)(2,1)S(1)}, u32[]{:S(2)}, u32[]{:S(2)}) collective-permute-start(bf16[64,2,768]{2,0,1:T(8,128)(2,1)S(1)} %get-tuple-element.80), channel_id=1, source_target_pairs={{0,2},{1,3},{2,4},{3,5},{4,6},{5,7},{6,0},{7,1},{8,10},{9,11},{10,... | collective-permute-start | bytes 589832 | tf_op jit(solution)/shard_map/ppermute | solution.py:62
  861.7 45.5 %collective-permute-start.63 = (bf16[64,2,2048]{2,0,1:T(8,128)(2,1)}, bf16[64,2,2048]{2,0,1:T(8,128)(2,1)}, u32[]{:S(2)}, u32[]{:S(2)}) collective-permute-start(bf16[64,2,2048]{2,0,1:T(8,128)(2,1)} %get-tuple-element.41), channel_id=1, source_target_pairs={{0,4},{1,5},{2,6},{3,7},{4,0},{5,1},{6,2},{7,3},{8,12},{9,13},{10,... | collective-permute-start | bytes 1572872 | tf_op jit(solution)/shard_map/ppermute | solution.py:62
  (88 other events, 1104.5 us)
Sparse Core Ops, SparseCore 0:
  55.6 48.1 all-gather.4
  105.6 26.6 all-gather.6
  134.7 87.5 all-gather.8
  232.1 53.2 all-gather.10
  631.2 28.1 reduce-scatter.6
  662.4 43.9 reduce-scatter.4
  709.7 52.9 reduce-scatter.10
  765.7 86.3 reduce-scatter.8

commit v3 on v1

v3 whole, which is shorter than its diff:
```python
import jax
import jax.numpy as jnp
from jax import lax
from jax.experimental import pallas as pl
from jax.experimental.pallas import tpu as pltpu
from jax.sharding import PartitionSpec as P

H = 32
HD = 64
EPSILON = 1e-05
ROPE_BASE = 130000.0
MASKED = -1e30
BF = jnp.bfloat16
F32 = jnp.float32
ALL = ("fsdp", "seq")


def rms_norm(values, gain_vector):
    return (
        values
        * lax.rsqrt(jnp.mean(values * values, axis=-1, keepdims=True) + EPSILON)
        * gain_vector
    )


def rope_tables(length):
    exponents = jnp.arange(HD // 2).astype(F32) * (2.0 / HD)
    inverse = jnp.power(ROPE_BASE, -exponents)
    angles = inverse[:, None] * jnp.arange(length, dtype=jnp.int32).astype(F32)[None, :]
    return jnp.cos(angles), jnp.sin(angles)


def matmul(left_side, right_side):
    return jnp.dot(left_side, right_side, preferred_element_type=F32)


def transposed(left_side, right_side):
    return lax.dot_general(
        left_side, right_side, (((0,), (0,)), ((), ())), preferred_element_type=F32
    )


def against(left_side, right_side):
    return lax.dot_general(
        left_side, right_side, (((1,), (1,)), ((), ())), preferred_element_type=F32
    )


def gated(gate_value, up_value):
    return gate_value * jax.nn.sigmoid(gate_value) * up_value


def turn(value, steps):
    size = lax.axis_size("seq")
    return lax.ppermute(value, "seq", [(s, (s - 2 * steps) % size) for s in range(size)])


def swap(value):
    return lax.ppermute(value, "seq", [(s, s ^ 1) for s in range(lax.axis_size("seq"))])


def beside(value, bit):
    return lax.ppermute(value, "fsdp", [(f, f ^ bit) for f in range(lax.axis_size("fsdp"))])


def place():
    own = lax.axis_index("seq")
    return own // 2, own % 2, lax.axis_size("seq") // 2


def tie(value, *others):
    anywhere = pl.BlockSpec(memory_space=pl.ANY)
    return pl.pallas_call(
        lambda *refs: None,
        out_shape=jax.ShapeDtypeStruct(value.shape, value.dtype),
        in_specs=[anywhere] * (1 + len(others)),
        out_specs=anywhere,
        input_output_aliases={0: 0},
        cost_estimate=pl.CostEstimate(flops=0, bytes_accessed=0, transcendentals=0),
    )(value, *others)


def order(chips):
    near = []
    for step in range(1, chips // 2 + 1):
        near += [step] if 2 * step == chips else [step, chips - step]
    return near


def gather_rows(local):
    return lax.all_gather(local, "seq", axis=0, tiled=True)


def scatter_rows(partial):
    return lax.psum_scatter(
        partial.astype(BF), "seq", scatter_dimension=0, tiled=True
    ).astype(F32)


def move(kernel, out_shapes, *operands, first=()):
    given = len(operands)
    whole = pl.BlockSpec(memory_space=pltpu.VMEM)
    many = isinstance(out_shapes, tuple)
    moved = sum(x.size * x.dtype.itemsize for x in operands)
    return pl.pallas_call(
        lambda *refs: kernel(*refs[:given], *refs[given + len(first) :]),
        out_shape=out_shapes,
        in_specs=[
            pl.BlockSpec(memory_space=pltpu.SMEM if x.ndim == 1 else pltpu.VMEM)
            for x in operands
        ]
        + [pl.BlockSpec(memory_space=pl.ANY)] * len(first),
        out_specs=tuple([whole] * len(out_shapes)) if many else whole,
        compiler_params=pltpu.CompilerParams(vmem_limit_bytes=48 * 2**20),
        cost_estimate=pl.CostEstimate(flops=0, bytes_accessed=3 * moved, transcendentals=0),
    )(*operands, *first)


def here():
    chip, core, chips = place()
    return jnp.stack([chip, core]).astype(jnp.int32)


def columns_of(weights, blocks, rows_of_extra=()):
    chip, core, chips = place()
    rows = weights[0].shape[0]
    parts = [w.shape[1] // (blocks * 2 * chips) for w in weights]
    cols = blocks * sum(parts) + (128 if rows_of_extra else 0)

    def kernel(at, *refs):
        out = refs[-1]
        chip, core = at[0], at[1]
        extra = []
        if rows_of_extra:
            filled = jnp.zeros((rows, 128), F32)
            which = lax.broadcasted_iota(jnp.int32, (rows, 128), 0)
            for i, ref in enumerate(refs[len(parts) : -1]):
                filled = jnp.where(which == i, ref[...], filled)
            extra = [filled.astype(BF)]
        for z in range(chips):
            for c in range(2):
                runs = []
                for ref, part in zip(refs, parts):
                    for b in range(blocks):
                        start = ((b * chips + z) * 2 + c) * part
                        runs.append(ref[:, start : start + part])
                out[(c + core) % 2, (z - chip + chips) % chips] = jnp.concatenate(
                    runs + extra, axis=1
                )

    return move(
        kernel,
        jax.ShapeDtypeStruct((2, chips, rows, cols), weights[0].dtype),
        here(),
        *weights,
        *rows_of_extra,
    )


def exchange(pieces, first=()):
    chip, core, chips = place()
    other = swap(pieces[1])
    shares = [jnp.stack([pieces[0, step], other[step]]) for step in range(chips)]
    if first:
        shares = [tie(share, *first) for share in shares]
    arrived = {0: shares[0]}
    for step in order(chips):
        arrived[chips - step] = turn(shares[step], -step)
    return [arrived[step] for step in range(chips)]


def rows_of(arrived, first=()):
    chip, core, chips = place()
    pair, rows, cols = arrived[0].shape

    def kernel(at, *refs):
        chip, core = at[0], at[1]
        for step in range(chips):
            for k in range(2):
                refs[-1][(chip + step) % chips, (core + k) % 2] = refs[step][k]

    return move(
        kernel,
        jax.ShapeDtypeStruct((chips, 2, rows, cols), arrived[0].dtype),
        here(),
        *arrived,
        first=first,
    ).reshape(chips * 2 * rows, cols)


def rows_to(summed):
    chip, core, chips = place()
    cols = summed.shape[1]
    rows = summed.shape[0] // (2 * chips)

    def kernel(at, ref, out):
        chip, core = at[0], at[1]
        for step in range(chips):
            for k in range(2):
                out[k, step] = ref[(chip + step) % chips, (core + k) % 2]

    return move(
        kernel,
        jax.ShapeDtypeStruct((2, chips, rows, cols), summed.dtype),
        here(),
        summed.reshape(chips, 2, rows, cols),
    )


def columns_to(arrived, blocks, widths):
    chip, core, chips = place()
    pair, rows, cols = arrived[0].shape
    parts = [w // blocks for w in widths]

    def kernel(at, *refs):
        chip, core = at[0], at[1]
        outs = refs[chips:]
        for step in range(chips):
            z = (chip + step) % chips
            at_col = 0
            for out, part in zip(outs, parts):
                for b in range(blocks):
                    one = refs[step][0, :, at_col : at_col + part].astype(F32)
                    two = refs[step][1, :, at_col : at_col + part].astype(F32)
                    both = jnp.concatenate(
                        [jnp.where(core == 0, one, two), jnp.where(core == 0, two, one)], axis=1
                    )
                    start = pl.multiple_of((b * chips + z) * 2 * part, 2 * part)
                    out[:, pl.ds(start, 2 * part)] = both
                    at_col += part

    return move(
        kernel,
        tuple(jax.ShapeDtypeStruct((rows, 2 * chips * w), F32) for w in widths),
        here(),
        *arrived,
    )


def square():
    return lax.axis_size("fsdp") == 4


def flipped(blocks):
    own = lax.axis_index("fsdp")
    odd, high = own % 2 == 1, own // 2 == 1
    a, b, c, d = blocks
    a, b, c, d = (
        jnp.where(odd, b, a),
        jnp.where(odd, a, b),
        jnp.where(odd, d, c),
        jnp.where(odd, c, d),
    )
    return [
        jnp.where(high, c, a),
        jnp.where(high, d, b),
        jnp.where(high, a, c),
        jnp.where(high, b, d),
    ]


def relative_blocks(values):
    if not square():
        return values
    return jnp.concatenate(flipped(jnp.split(values, 4, axis=-1)), axis=-1)


def gather_square(local, ordered=False):
    if not square():
        return lax.all_gather(local, "fsdp", axis=0, tiled=True), ((), ())
    half = local.shape[0] // 2
    one = beside(local, 1)
    two = beside(local, 2)
    three = beside(two[:half], 1)
    four = beside(one[half:], 2)
    steps = ((one, two), (three, four))
    if ordered:
        last = jnp.concatenate([three, four], axis=0)
        return jnp.concatenate(flipped([local, one, two, last]), axis=0), steps
    return jnp.concatenate([local, one, two, three, four], axis=0), steps


def begin_square(grad, ordered=False):
    grad = grad.astype(BF)
    if not square():
        return (lax.psum_scatter(grad, "fsdp", scatter_dimension=0, tiled=True),)
    rows, cols = grad.shape
    g = grad.reshape(4, 2, rows // 8, cols)
    if ordered:
        own = lax.axis_index("fsdp")
        g = [lax.dynamic_index_in_dim(g, own ^ i, 0, keepdims=False) for i in range(4)]
        g = {(i, j): g[i][j] for i in range(4) for j in range(2)}
    return (
        g,
        beside(jnp.stack([g[1, 0], g[3, 0]]), 1),
        beside(jnp.stack([g[2, 1], g[3, 1]]), 2),
    )


def second_square(g, one=None, two=None):
    if one is None:
        return (g,)
    def kernel(a, b, c, d, first, second):
        first[...] = (a[...].astype(F32) + b[1].astype(F32)).astype(BF)
        second[...] = (c[...].astype(F32) + d[1].astype(F32)).astype(BF)

    part = jax.ShapeDtypeStruct(g[2, 0].shape, BF)
    first, second = move(kernel, (part, part), g[2, 0], one, g[1, 1], two)
    return g, one, two, beside(first, 2), beside(second, 1)


def finish_square(g, one=None, two=None, one_last=None, two_last=None):
    if one is None:
        return g
    return jnp.concatenate(
        [
            g[0, 0].astype(F32) + one[0].astype(F32) + one_last.astype(F32),
            g[0, 1].astype(F32) + two[0].astype(F32) + two_last.astype(F32),
        ],
        axis=0,
    ).astype(BF)


def turned(values, cosine, sine):
    half = values.shape[0] // 2
    lead, trail = values[:half], values[half:]
    return jnp.concatenate([lead * cosine - trail * sine, trail * cosine + lead * sine], axis=0)


def dot(left_side, right_side):
    return jnp.dot(left_side, right_side, preferred_element_type=F32)


def seen_bias(column_ref, row_ref, bias_ref, block):
    length = row_ref.shape[1]
    for first in range(0, length, block):
        keys = first + block
        ahead = lax.broadcasted_iota(jnp.int32, (keys, block), 0) <= (
            lax.broadcasted_iota(jnp.int32, (keys, block), 1) + first
        )
        same = column_ref[:keys] == row_ref[:, first:keys]
        bias_ref[:keys, first:keys] = jnp.where(same & ahead, 0.0, MASKED)


def attend(qkv, cosine, sine, segment, block, heads):
    length = qkv.shape[1]
    scale = HD ** (-0.5)

    def kernel(q_ref, k_ref, v_ref, cos_ref, sin_ref, column_ref, row_ref, *refs):
        mixed_ref, query_ref, key_ref, value_ref, log_ref, bias_ref = refs

        @pl.when(pl.program_id(0) == 0)
        def _():
            seen_bias(column_ref, row_ref, bias_ref, block)

        cos, sin = cos_ref[...], sin_ref[...]
        query = turned(q_ref[...], cos, sin).astype(BF) * scale
        key_t = turned(k_ref[...], cos, sin).astype(BF)
        value_t = v_ref[...].astype(BF)
        query_ref[...] = query
        key_ref[...] = key_t
        value_ref[...] = value_t
        key = key_t.T
        for first in range(0, length, block):
            keys = first + block
            scores = dot(key[:keys], query[:, first:keys]) + bias_ref[:keys, first:keys]
            top = jnp.max(scores, axis=0, keepdims=True)
            exponent = jnp.exp(scores - top)
            total = jnp.sum(exponent, axis=0, keepdims=True)
            weights = (exponent * (1.0 / total)).astype(BF)
            mixed_ref[:, first:keys] = dot(value_t[:, :keys], weights).astype(BF)
            log_ref[0, :, first:keys] = top + jnp.log(total)

    head = lambda offset: pl.BlockSpec((HD, length), lambda h: (h + offset, 0))
    whole = pl.BlockSpec(memory_space=pltpu.VMEM)
    tall = jax.ShapeDtypeStruct((heads * HD, length), BF)
    return pl.pallas_call(
        kernel,
        grid=(heads,),
        out_shape=(tall, tall, tall, tall, jax.ShapeDtypeStruct((heads, 1, length), F32)),
        in_specs=[
            head(0),
            head(heads),
            head(2 * heads),
            whole,
            whole,
            whole,
            whole,
        ],
        out_specs=(
            head(0),
            head(0),
            head(0),
            head(0),
            pl.BlockSpec((1, 1, length), lambda h: (h, 0, 0)),
        ),
        scratch_shapes=[pltpu.VMEM((length, length), F32)],
        compiler_params=pltpu.CompilerParams(vmem_limit_bytes=56 * 2**20),
        cost_estimate=pl.CostEstimate(
            flops=4 * heads * HD * length * length,
            bytes_accessed=24 * heads * HD * length,
            transcendentals=heads * length * length,
        ),
    )(qkv, qkv, qkv, cosine, sine, segment[:, None], segment[None, :])


def attend_back(grad, query, key, value, logs, cosine, sine, segment, block, heads):
    length = grad.shape[1]
    scale = HD ** (-0.5)

    def kernel(grad_ref, query_ref, key_ref, value_ref, log_ref, *refs):
        cos_ref, sin_ref, column_ref, row_ref, dq_ref, dk_ref, dv_ref, bias_ref = refs[:8]
        key_sum, value_sum = refs[8:]

        @pl.when(pl.program_id(0) == 0)
        def _():
            seen_bias(column_ref, row_ref, bias_ref, block)

        cos, sin = cos_ref[...], sin_ref[...]
        grad_t = grad_ref[...]
        query_t, key_t = query_ref[...], key_ref[...]
        grads, queries, key, value = grad_t.T, query_t.T, key_t.T, value_ref[...].T
        for first in reversed(range(0, length, block)):
            keys = first + block
            here_q = slice(first, keys)
            scores = dot(key[:keys], query_t[:, here_q]) + bias_ref[:keys, here_q]
            probs = jnp.exp(scores - log_ref[0, :, here_q])
            grad_probs = dot(value[:keys], grad_t[:, here_q])
            inner = jnp.sum(probs * grad_probs, axis=0, keepdims=True)
            grad_scores = (probs * (grad_probs - inner)).astype(BF)
            key_part = dot(grad_scores, queries[here_q])
            value_part = dot(probs.astype(BF), grads[here_q])
            if keys == length:
                key_sum[...] = key_part
                value_sum[...] = value_part
            else:
                key_sum[:keys] += key_part
                value_sum[:keys] += value_part
            dq = (dot(key_t[:, :keys], grad_scores) * scale).astype(BF).astype(F32)
            dq_ref[:, here_q] = turned(dq, cos[:, here_q], -sin[:, here_q]).astype(BF)
        dk = key_sum[...].astype(BF).astype(F32).T
        dk_ref[...] = turned(dk, cos, -sin).astype(BF)
        dv_ref[...] = value_sum[...].T.astype(BF)

    head = pl.BlockSpec((HD, length), lambda h: (h, 0))
    whole = pl.BlockSpec(memory_space=pltpu.VMEM)
    tall = jax.ShapeDtypeStruct((heads * HD, length), BF)
    return pl.pallas_call(
        kernel,
        grid=(heads,),
        out_shape=(tall, tall, tall),
        in_specs=[
            head,
            head,
            head,
            head,
            pl.BlockSpec((1, 1, length), lambda h: (h, 0, 0)),
            whole,
            whole,
            whole,
            whole,
        ],
        out_specs=(head, head, head),
        scratch_shapes=[
            pltpu.VMEM((length, length), F32),
            pltpu.VMEM((length, HD), F32),
            pltpu.VMEM((length, HD), F32),
        ],
        compiler_params=pltpu.CompilerParams(vmem_limit_bytes=56 * 2**20),
        cost_estimate=pl.CostEstimate(
            flops=10 * heads * HD * length * length,
            bytes_accessed=24 * heads * HD * length,
            transcendentals=heads * length * length,
        ),
    )(grad, query, key, value, logs, cosine, sine, segment[:, None], segment[None, :])


def sum_to_owners(values):
    for axis in ALL:
        size, own = lax.axis_size(axis), lax.axis_index(axis)
        bit = size // 2
        while bit:
            halves = values.reshape(2, values.shape[0] // 2, values.shape[1])
            mine = (own // bit) % 2
            keep = lax.dynamic_index_in_dim(halves, mine, 0, keepdims=False)
            give = lax.dynamic_index_in_dim(halves, 1 - mine, 0, keepdims=False)
            values = keep + lax.ppermute(give, axis, [(s, s ^ bit) for s in range(size)])
            bit //= 2
    return values[0]


def body(
    tokens,
    teacher,
    segments,
    valid,
    query_weight,
    key_weight,
    value_weight,
    output_weight,
    attention_gain,
    gate_weight,
    up_weight,
    down_weight,
    mlp_gain,
):
    sequences, local_rows, width = tokens.shape
    groups = lax.axis_size("seq")
    shards = lax.axis_size("fsdp")
    heads = H // groups
    length = local_rows * groups
    own = lax.axis_index("seq")
    chip, core, chips = place()
    weight_rows = query_weight.shape[0]
    aligned = H % (shards * groups) == 0
    head_blocks = shards if aligned else 1
    hw = heads * HD

    inputs = tokens.reshape(local_rows, width).astype(F32)
    keep_mask = valid.reshape(local_rows).astype(F32)
    lane_pad = lambda row: jnp.pad(row, ((0, 0), (0, 128 - row.shape[1])))
    own_gains = jnp.concatenate([attention_gain, mlp_gain])[None, :]
    extra_rows = (
        lane_pad(own_gains.astype(F32)),
        lane_pad((segments // 256).astype(F32)),
        lane_pad((segments % 256).astype(F32)),
        jnp.broadcast_to(jnp.sum(keep_mask), (1, 128)),
    )
    attention_shares = exchange(
        columns_of([query_weight, key_weight, value_weight], head_blocks, extra_rows)
    )
    if aligned:
        out_weight, out_steps = gather_square(output_weight, ordered=True)
    else:
        out_weight = lax.dynamic_slice_in_dim(
            lax.all_gather(output_weight, ALL, axis=0, tiled=True), own * hw, hw, 0
        )
        out_steps = ((), ())
    down_full, down_steps = gather_square(down_weight, ordered=True)
    tokens_all = gather_rows(relative_blocks(tokens.reshape(local_rows, width)))
    attention_in, unused = gather_square(
        rows_of(attention_shares, first=down_steps[0])
    )
    gate_up_shares = exchange(
        columns_of([gate_weight, up_weight], shards), (attention_shares[chips // 2],)
    )
    gate_up_weight, gate_up_steps = gather_square(rows_of(gate_up_shares))

    qkv_weight = attention_in[:, : 3 * hw]
    extras = attention_in[:, 3 * hw :].reshape(shards * groups, weight_rows, 128).astype(F32)
    normed_gain = extras[:, 0, :weight_rows].reshape(width)
    gains = relative_blocks(
        jnp.stack([normed_gain, extras[:, 0, weight_rows : 2 * weight_rows].reshape(width)])
    )
    first_gain, second_gain = gains[0], gains[1]
    count = jnp.sum(extras[:, 3, 0])
    table = lax.dynamic_slice_in_dim(
        extras, 0 if square() else lax.axis_index("fsdp") * groups, groups, 0
    ).astype(jnp.int32)
    segment = (table[:, 1, :local_rows] * 256 + table[:, 2, :local_rows]).reshape(length)
    cosine, sine = rope_tables(length)

    normed = rms_norm(
        tokens_all.astype(F32), normed_gain
    ).astype(BF)
    qkv = lax.dot_general(
        qkv_weight, normed, (((0,), (1,)), ((), ())), preferred_element_type=F32
    )
    mixed, query, key, value, logs = attend(
        qkv, cosine, sine, segment, 2 * local_rows, heads
    )
    mixed = tie(mixed, *gate_up_shares[1:], *out_steps[1], *down_steps[1])
    after_attention = inputs + tie(
        scatter_rows(transposed(mixed, out_weight)), *gate_up_steps[0]
    )
    normed_two = gather_rows(
        relative_blocks(rms_norm(after_attention, second_gain).astype(BF))
    )
    gate_up = matmul(normed_two, gate_up_weight)
    hidden_width = gate_up.shape[1] // 2
    gate_value, up_value = gate_up[:, :hidden_width], gate_up[:, hidden_width:]
    hidden = gated(gate_value, up_value).astype(BF)
    result = after_attention + scatter_rows(matmul(hidden, down_full))
    difference = result - teacher.reshape(local_rows, width).astype(F32)
    error_sum = jnp.sum(keep_mask[:, None] * difference * difference)
    grad_result = 2.0 / count * keep_mask[:, None] * difference
    grad_branch = gather_rows(grad_result.astype(BF))
    unused, gate_pull = jax.vjp(gated, gate_value, up_value)
    grad_gate, grad_upward = gate_pull(against(grad_branch, down_full))
    gate_up_grad = jnp.concatenate([grad_gate.astype(BF), grad_upward.astype(BF)], axis=1)
    grad_normed_sum = against(gate_up_grad, gate_up_weight).astype(BF)
    grad_normed_two = scatter_rows(grad_normed_sum)
    gate_up_weight_grad = transposed(normed_two, tie(gate_up_grad, grad_normed_sum)).astype(BF)
    gate_up_back = begin_square(gate_up_weight_grad)
    down_grad = transposed(hidden, tie(grad_branch, gate_up_weight_grad)).astype(BF)
    grad_normed_two = relative_blocks(tie(grad_normed_two, down_grad))
    unused, second_pull = jax.vjp(rms_norm, after_attention, second_gain)
    grad_after, second_gain_grad = second_pull(grad_normed_two)
    grad_after = grad_after + grad_result

    grad_out = tie(gather_rows(grad_after.astype(BF)), *gate_up_back[1:])
    gate_up_back = second_square(*gate_up_back)
    grad_mixed = against(out_weight, grad_out).astype(BF)
    output_grad = matmul(mixed, grad_out)
    qkv_grad = jnp.concatenate(
        attend_back(
            grad_mixed, query, key, value, logs, cosine, sine, segment, 2 * local_rows, heads
        ),
        axis=0,
    )
    gate_up_back = finish_square(*gate_up_back[:-1], tie(gate_up_back[-1], qkv_grad))
    gate_up_shares = exchange(rows_to(gate_up_back))
    gate_sum, up_sum = columns_to(gate_up_shares, shards, [hidden_width, hidden_width])
    down_back = second_square(*begin_square(tie(down_grad, grad_mixed), ordered=True))
    down_sum = finish_square(*down_back).astype(F32)
    if aligned:
        output_back = second_square(*begin_square(output_grad, ordered=True))
        output_sum = finish_square(*output_back).astype(F32)
    else:
        output_sum = lax.psum_scatter(
            lax.dynamic_update_slice_in_dim(
                jnp.zeros((width, width), BF), output_grad.astype(BF), own * hw, 0
            ),
            ALL,
            scatter_dimension=0,
            tiled=True,
        ).astype(F32)
    qkv_back = begin_square(
        lax.dot_general(normed, qkv_grad, (((0,), (1,)), ((), ())), preferred_element_type=F32)
    )
    qkv_back = finish_square(*second_square(*qkv_back))
    query_sum, key_sum, value_sum = columns_to(
        exchange(rows_to(qkv_back)), head_blocks, [hw, hw, hw]
    )

    grad_normed = relative_blocks(
        scatter_rows(
            lax.dot_general(
                qkv_grad, qkv_weight, (((0,), (1,)), ((), ())), preferred_element_type=F32
            )
        )
    )
    unused, first_pull = jax.vjp(rms_norm, inputs, first_gain)
    grad_inputs, first_gain_grad = first_pull(grad_normed)
    grad_inputs = grad_inputs + grad_after
    devices = shards * groups
    sums = sum_to_owners(
        jnp.concatenate(
            [
                first_gain_grad.reshape(devices, weight_rows),
                second_gain_grad.reshape(devices, weight_rows),
                jnp.full((devices, 128), error_sum),
            ],
            axis=1,
        )
    )
    output_shape = (sequences, local_rows, width)
    return (
        result.reshape(output_shape).astype(BF),
        sums[2 * weight_rows] / count,
        grad_inputs.reshape(output_shape),
        query_sum,
        key_sum,
        value_sum,
        output_sum,
        sums[:weight_rows],
        gate_sum,
        up_sum,
        down_sum,
        sums[weight_rows : 2 * weight_rows],
    )


def solution(mesh):
    rows = P("fsdp", "seq", None)
    places = P("fsdp", "seq")
    matrix = P(ALL, None)
    vector = P(ALL)
    return jax.shard_map(
        body,
        mesh=mesh,
        in_specs=(
            rows,
            rows,
            places,
            places,
            matrix,
            matrix,
            matrix,
            matrix,
            vector,
            matrix,
            matrix,
            matrix,
            vector,
        ),
        out_specs=(
            rows,
            P(),
            rows,
            matrix,
            matrix,
            matrix,
            matrix,
            vector,
            matrix,
            matrix,
            matrix,
            vector,
        ),
        check_vma=False,
    )
```

time: 1230 us -> 696 us (0.57)
  waiting for transfers between devices: 672 us -> 325 us
  blocking collectives: 256 us -> 0 us
  matrix products: 139 us -> 92.2 us
  starting transfers between devices: 23.7 us -> 69.5 us
  Pallas kernels: 0 us -> 41.7 us
  other arithmetic: 37.4 us -> 70.3 us
    ppermute x0 -> x53, waiting for transfers between devices: none -> 158 us  [the longest x32 108 us: beside(): lax.ppermute(value, 'fsdp', [(f, f ^ bit) for f in range(lax.axis_size('f...]
    all_gather x7 -> x0, waiting for transfers between devices: 140 us -> none  [the longest x5 104 us: columns_in(): return lax.all_gather(swapped, 'fsdp', axis=0, tiled=True)]
    reduce_scatter x7 -> x0, waiting for transfers between devices: 136 us -> none  [the longest x5 100 us: columns_out(): lax.psum_scatter(grad.astype(BF), 'fsdp', scatter_dimension=0, tiled=True)]
    unnamed x24 -> x8, waiting for transfers between devices: 134 us -> 0.13 us
    all_to_all x5 -> x0, blocking collectives: 126 us -> none  [columns_in(): lax.all_to_all(weight.reshape(rows, blocks, groups, part), 'seq', split_a...]
    all_gather x4, waiting for transfers between devices: 161 us -> 57.4 us  [gather_rows(): return lax.all_gather(local, 'seq', axis=0, tiled=True)]
    psum x2 -> x0, blocking collectives: 81.7 us -> none  [body(): lax.psum((jnp.sum(keep_mask), jnp.sum(keep_mask[:, None] * difference * d...]
    ppermute x0 -> x53, starting transfers between devices: none -> 68.3 us  [the longest x32 37.4 us: beside(): lax.ppermute(value, 'fsdp', [(f, f ^ bit) for f in range(lax.axis_size('f...]
  transfers between devices with their start and end apart: 28 -> 61, of which waited for: 20 -> 29; matrix products, arithmetic and copies ran while one was open for 15% -> 22% of each run, Pallas kernels for 0% -> 6%
where the time goes in v3:
time: 696 us; the launch traced here: 690 us
  waiting for transfers between devices  325 us (47%)
  matrix products  92.2 us (13%)
  local copies, waits for them, and re-layouts  72.9 us (10%)
  other arithmetic  70.3 us (10%)
  starting transfers between devices  69.5 us (10%)
  Pallas kernels  41.7 us (6%)
  between operations  18.7 us (3%)
    reduce_scatter x4, waiting for transfers between devices, scatter_rows(): lax.psum_scatter(partial.astype(BF), 'seq', scatter_dimension=0, tiled=True)  109 us
    ppermute x32, waiting for transfers between devices, beside(): lax.ppermute(value, 'fsdp', [(f, f ^ bit) for f in range(lax.axis_size('f...  108 us
    all_gather x4, waiting for transfers between devices, gather_rows(): return lax.all_gather(local, 'seq', axis=0, tiled=True)  57.4 us
    unnamed x140, local copies, waits for them, and re-layouts  43.3 us
    ppermute x12, waiting for transfers between devices, turn(): lax.ppermute(value, 'seq', [(s, (s - 2 * steps) % size) for s in range(si...  42.5 us
    ppermute x32, starting transfers between devices, beside(): lax.ppermute(value, 'fsdp', [(f, f ^ bit) for f in range(lax.axis_size('f...  37.4 us
    dot_general x3, matrix products, transposed(): lax.dot_general(left_side, right_side, (((0,), (0,)), ((), ())), preferre...  28.2 us
    dot_general x3, matrix products, against(): lax.dot_general(left_side, right_side, (((1,), (1,)), ((), ())), preferre...  27.6 us
  transfers between devices with their start and end apart: 61, of which 29 were waited for; matrix products, arithmetic and copies ran while one was open for 22% of the time, Pallas kernels for 6%

profile of v3, /device:TPU:0, one launch (start us, length us, event | category | flops | bytes accessed | tf_op | source)
XLA Modules:
  0.0 690.2 jit_solution(12825454268667362923)
XLA Ops:
  25.9 14.8 %collective-permute-done.14 = bf16[64,2048]{1,0:T(8,128)(2,1)S(1)} collective-permute-done((bf16[64,2048]{1,0:T(8,128)(2,1)}, bf16[64,2048]{1,0:T(8,128)(2,1)S(1)}, u32[]{:S(2)}, u32[]{:S(2)}) %collective-permute-start.14) | collective-permute-done | bytes 262176 | tf_op jit(solution)/shard_map/ppermute | solution.py:63
  55.1 21.5 %collective-permute-done.2.refs_3_.refs_1_ = bf16[2,64,896]{2,1,0:T(8,128)(2,1)S(1)} collective-permute-done((bf16[2,64,896]{2,1,0:T(8,128)(2,1)S(1)}, bf16[2,64,896]{2,1,0:T(8,128)(2,1)S(1)}, u32[]{:S(2)}, u32[]{:S(2)}) %collective-permute-start.2) | collective-permute-done | bytes 229408 | tf_op jit(solution)/shard_map/ppermute | solution.py:55
  77.8 5.7 collective-permute-done.1.refs_2_
  95.8 11.4 %collective-permute-done.7 = bf16[512,896]{1,0:T(8,128)(2,1)} collective-permute-done((bf16[512,896]{1,0:T(8,128)(2,1)}, bf16[512,896]{1,0:T(8,128)(2,1)}, u32[]{:S(2)}, u32[]{:S(2)}) %collective-permute-start.7) | collective-permute-done | bytes 917536 | tf_op jit(solution)/shard_map/ppermute | solution.py:63
  136.7 7.2 %fusion.8.q_ref.k_ref.v_ref = f32[768,1024]{1,0:T(8,128)} fusion(bf16[2048,896]{1,0:T(8,128)(2,1)} %constant_dynamic-update-slice_fusion, bf16[1024,2048]{1,0:T(8,128)(2,1)S(1)} %copy-done.22, f32[2048]{0:T(1024)S(1)} %mul.257, f32[1024]{0:T(1024)S(1)} %add_rsqrt_fusion), kind=kOutput, calls=%fused_computation.23 | convolution fusion | flops 3229614080 | bytes 10498048 | tf_op jit(solution)/shard_map/dot_general | solution.py:566
  143.9 12.2 %shard_map.222 = (bf16[256,1024]{1,0:T(8,128)(2,1)}, bf16[256,1024]{1,0:T(8,128)(2,1)}, bf16[256,1024]{1,0:T(8,128)(2,1)}, bf16[256,1024]{1,0:T(8,128)(2,1)}, f32[4,1,1024]{2,1,0:T(1,128)}) custom-call(f32[768,1024]{1,0:T(8,128)} %fusion.8.q_ref.k_ref.v_ref, f32[768,1024]{1,0:T(8,128)} %fusion.8.q_ref.k_ref.v_ref, f32[768,1024]{1,0:T(8,128)} %fusion.8.q_ref.k_ref.v_ref, ...), custom_call_target="tpu_custom_call" | custom-call | flops 1073741824 | bytes 6291456 | tf_op jit(solution)/shard_map/pallas_call | solution.py:377
  157.4 4.6 convolution_convert_fusion.2
  170.3 42.5 %reduce-scatter.5.cloned.1.call-done = bf16[128,2048]{1,0:T(8,128)(2,1)} async-done(((bf16[1024,2048]{1,0:T(8,128)(2,1)}), bf16[128,2048]{1,0:T(8,128)(2,1)}) %reduce-scatter.5.cloned.1.call-update) | async-done | bytes 524304 | tf_op jit(solution)/shard_map/reduce_scatter | solution.py:95
  237.4 8.0 %collective-permute-done.22 = bf16[256,2048]{1,0:T(8,128)(2,1)S(1)} collective-permute-done((bf16[256,2048]{1,0:T(8,128)(2,1)S(1)}, bf16[256,2048]{1,0:T(8,128)(2,1)S(1)}, u32[]{:S(2)}, u32[]{:S(2)}) %collective-permute-start.22) | collective-permute-done | bytes 1048608 | tf_op jit(solution)/shard_map/ppermute | solution.py:63
  246.5 4.2 collective-permute-done.23
  251.7 12.4 %all-gather.7.cloned.1.call-done = bf16[1024,2048]{1,0:T(8,128)(2,1)} async-done(((bf16[128,2048]{1,0:T(8,128)(2,1)}), bf16[1024,2048]{1,0:T(8,128)(2,1)}) %all-gather.7.cloned.1.call-update) | async-done | bytes 4194320 | tf_op jit(solution)/shard_map/all_gather | solution.py:91
  264.1 12.5 %fusion.65 = f32[1024,2048]{1,0:T(8,128)S(1)} fusion(bf16[1024,2048]{1,0:T(8,128)(2,1)} %all-gather.7.cloned.1.call-done, bf16[2048,2048]{1,0:T(8,128)(2,1)} %constant_dynamic-update-slice_fusion.7), kind=kOutput, calls=%fused_computation.315 | convolution fusion | flops 8589934592 | bytes 20971520 | tf_op jit(solution)/shard_map/dot_general | solution.py:34
  282.1 6.1 convolution_convert_fusion.5
  290.7 46.5 %reduce-scatter.7.cloned.1.call-done = bf16[128,2048]{1,0:T(8,128)(2,1)} async-done(((bf16[1024,2048]{1,0:T(8,128)(2,1)}), bf16[128,2048]{1,0:T(8,128)(2,1)}) %reduce-scatter.7.cloned.1.call-update) | async-done | bytes 524304 | tf_op jit(solution)/shard_map/reduce_scatter | solution.py:95
  339.7 45.0 %all-gather.9.cloned.1.call-done.refs_0_ = bf16[1024,2048]{1,0:T(8,128)(2,1)} async-done(((bf16[128,2048]{1,0:T(8,128)(2,1)}), bf16[1024,2048]{1,0:T(8,128)(2,1)}) %all-gather.9.cloned.1.call-update) | async-done | bytes 4194320 | tf_op jit(solution)/shard_map/all_gather | solution.py:91
  384.7 10.6 %fusion.5 = (bf16[1024,1024]{1,0:T(8,128)(2,1)S(1)}, bf16[1024,1024]{1,0:T(8,128)(2,1)S(1)}) fusion(f32[1024,2048]{1,0:T(8,128)} %copy-done.17, bf16[1024,2048]{1,0:T(8,128)(2,1)} %all-gather.9.cloned.1.call-done.refs_0_, bf16[256,2048]{1,0:T(8,128)(2,1)} %get-tuple-element.88, bf16[256,2048]{1,0:T(8,128)(2,1)} %get-tuple-element.87, ...), kind=kOutput, calls=%fused_computation.9 | convolution fusion | flops 4326424576 | bytes 20971520 | tf_op jit(solution)/shard_map/dot_general | solution.py:44
  397.4 12.6 %convolution_convert_fusion.1.refs_1_ = bf16[1024,2048]{1,0:T(8,128)(2,1)} fusion(bf16[2048,2048]{1,0:T(8,128)(2,1)} %constant_dynamic-update-slice_fusion.7, bf16[1024,1024]{1,0:T(8,128)(2,1)S(1)} %get-tuple-element.68, bf16[1024,1024]{1,0:T(8,128)(2,1)S(1)} %get-tuple-element.67), kind=kOutput, calls=%fused_computation.16 | convolution fusion | flops 8600420352 | bytes 16777216 | tf_op jit(solution)/shard_map/dot_general | solution.py:44
  410.2 4.7 pad_maximum_fusion.1.refs_0_
  415.0 14.1 %convolution_convert_fusion.refs_1_ = bf16[2048,2048]{1,0:T(8,128)(2,1)} fusion(bf16[1024,2048]{1,0:T(8,128)(2,1)} %all-gather.7.cloned.1.call-done, bf16[1024,2048]{1,0:T(8,128)(2,1)} %shard_map.231), kind=kOutput, calls=%fused_computation.5 | convolution fusion | flops 8594128896 | bytes 16777216 | tf_op jit(solution)/shard_map/dot_general | solution.py:38
  429.0 9.5 %convolution_convert_fusion.4.refs_1_.refs_0_ = bf16[1024,2048]{1,0:T(8,128)(2,1)} fusion(bf16[1024,1024]{1,0:T(8,128)(2,1)} %copy-done.29, bf16[1024,2048]{1,0:T(8,128)(2,1)} %shard_map.232), kind=kOutput, calls=%fused_computation.19 | convolution fusion | flops 4297064448 | bytes 10485760 | tf_op jit(solution)/shard_map/dot_general | solution.py:38
  438.5 20.4 %reduce-scatter.9.cloned.1.call-done = bf16[128,2048]{1,0:T(8,128)(2,1)} async-done(((bf16[1024,2048]{1,0:T(8,128)(2,1)}), bf16[128,2048]{1,0:T(8,128)(2,1)}) %reduce-scatter.9.cloned.1.call-update) | async-done | bytes 524304 | tf_op jit(solution)/shard_map/reduce_scatter | solution.py:95
  475.3 40.6 %collective-permute-done.25.refs_2_.refs_3_ = bf16[2,256,2048]{2,1,0:T(8,128)(2,1)} collective-permute-done((bf16[2,256,2048]{2,1,0:T(8,128)(2,1)}, bf16[2,256,2048]{2,1,0:T(8,128)(2,1)}, u32[]{:S(2)}, u32[]{:S(2)}) %collective-permute-start.25) | collective-permute-done | bytes 2097184 | tf_op jit(solution)/shard_map/ppermute | solution.py:63
  518.5 3.8 shard_map.240
  526.8 4.4 convolution_convert_fusion.8.grad_ref.refs_1_
  537.4 14.2 %shard_map.235 = (bf16[256,1024]{1,0:T(8,128)(2,1)}, bf16[256,1024]{1,0:T(8,128)(2,1)}, bf16[256,1024]{1,0:T(8,128)(2,1)}) custom-call(bf16[256,1024]{1,0:T(8,128)(2,1)} %convolution_convert_fusion.8.grad_ref.refs_1_, bf16[256,1024]{1,0:T(8,128)(2,1)} %get-tuple-element.34.query_ref, bf16[256,1024]{1,0:T(8,128)(2,1)} %get-tuple-element.35.key_ref, ...), custom_call_target="tpu_custom_call" | custom-call | flops 2684354560 | bytes 6291456 | tf_op jit(solution)/shard_map/pallas_call | solution.py:448
  556.0 5.2 convolution_convert_fusion.3
  561.2 4.2 fusion.13
  572.3 4.2 convolution_convert_fusion.6
  588.2 12.7 %collective-permute-done.32.refs_3_ = bf16[2,256,768]{2,1,0:T(8,128)(2,1)S(1)} collective-permute-done((bf16[2,256,768]{2,1,0:T(8,128)(2,1)S(1)}, bf16[2,256,768]{2,1,0:T(8,128)(2,1)S(1)}, u32[]{:S(2)}, u32[]{:S(2)}) %collective-permute-start.32) | collective-permute-done | bytes 786464 | tf_op jit(solution)/shard_map/ppermute | solution.py:63
  639.7 8.3 %collective-permute-done.47.refs_3_ = bf16[2,64,2048]{2,1,0:T(8,128)(2,1)} collective-permute-done((bf16[2,64,2048]{2,1,0:T(8,128)(2,1)}, bf16[2,64,2048]{2,1,0:T(8,128)(2,1)}, u32[]{:S(2)}, u32[]{:S(2)}) %collective-permute-start.47) | collective-permute-done | bytes 524320 | tf_op jit(solution)/shard_map/ppermute | solution.py:55
  648.0 9.2 %collective-permute-start.28 = (f32[4,256]{1,0:T(4,128)S(1)}, f32[4,256]{1,0:T(4,128)S(1)}, u32[]{:S(2)}, u32[]{:S(2)}) collective-permute-start(f32[4,256]{1,0:T(4,128)S(1)} %fusion.45), channel_id=1, source_target_pairs={{0,4},{1,5},{2,6},{3,7},{4,0},{5,1},{6,2},{7,3},{8,12},{9,13},{10,... | collective-permute-start | bytes 12296 | tf_op jit(solution)/shard_map/ppermute | solution.py:487
  660.8 6.9 %collective-permute-done.37.refs_3_ = bf16[2,64,768]{2,1,0:T(8,128)(2,1)S(1)} collective-permute-done((bf16[2,64,768]{2,1,0:T(8,128)(2,1)}, bf16[2,64,768]{2,1,0:T(8,128)(2,1)S(1)}, u32[]{:S(2)}, u32[]{:S(2)}) %collective-permute-start.37) | collective-permute-done | bytes 196640 | tf_op jit(solution)/shard_map/ppermute | solution.py:55
  (406 shorter events, 231.4 us)
Async XLA Ops:
  7.2 126.1 %all-gather.5.cloned.1.call-start = ((), (), s32[]{:S(2)}) async-start(), calls=%async_computation.4 | async-start | bytes 4718592 | tf_op jit(solution)/shard_map/all_gather | solution.py:91
  7.2 76.3 %collective-permute-start.4 = (bf16[256,2048]{1,0:T(8,128)(2,1)}, bf16[256,2048]{1,0:T(8,128)(2,1)S(1)}, u32[]{:S(2)}, u32[]{:S(2)}) collective-permute-start(bf16[256,2048]{1,0:T(8,128)(2,1)} %param.24), channel_id=1, source_target_pairs={{0,8},{8,0},{16,24},{24,16},{1,9},{9,1},{17,25},{25,17},{2,10},{10... | collective-permute-start | bytes 3145736 | tf_op jit(solution)/shard_map/ppermute | solution.py:63
  10.2 73.3 %collective-permute-start.5 = (bf16[256,2048]{1,0:T(8,128)(2,1)}, bf16[256,2048]{1,0:T(8,128)(2,1)S(1)}, u32[]{:S(2)}, u32[]{:S(2)}) collective-permute-start(bf16[256,2048]{1,0:T(8,128)(2,1)} %param.24), channel_id=1, source_target_pairs={{0,16},{8,24},{16,0},{24,8},{1,17},{9,25},{17,1},{25,9},{2,18},{10... | collective-permute-start | bytes 3145736 | tf_op jit(solution)/shard_map/ppermute | solution.py:63
  12.3 30.1 %collective-permute-start.16 = (bf16[64,2048]{1,0:T(8,128)(2,1)}, bf16[64,2048]{1,0:T(8,128)(2,1)S(1)}, u32[]{:S(2)}, u32[]{:S(2)}) collective-permute-start(bf16[64,2048]{1,0:T(8,128)(2,1)} %param.20), channel_id=1, source_target_pairs={{0,8},{8,0},{16,24},{24,16},{1,9},{9,1},{17,25},{25,17},{2,10},{10... | collective-permute-start | bytes 786440 | tf_op jit(solution)/shard_map/ppermute | solution.py:63
  14.4 198.4 %reduce-scatter.5.cloned.1.call-start = ((), (), s32[]{:S(2)}) async-start(), calls=%async_computation.5 | async-start | bytes 4718592 | tf_op jit(solution)/shard_map/reduce_scatter | solution.py:95
  21.5 29.2 %collective-permute-start = (bf16[4,64,896]{2,1,0:T(8,128)(2,1)S(1)}, bf16[4,64,896]{2,1,0:T(8,128)(2,1)S(1)}, u32[]{:S(2)}, u32[]{:S(2)}) collective-permute-start(bf16[4,64,896]{2,1,0:T(8,128)(2,1)S(1)} %slice_bitcast_fusion.14), channel_id=1, source_target_pairs={{0,1},{1,0},{2,3},{3,2},{4,5},{5,4},{6,7},{7,6},{8,9},{9,8},{10,11... | collective-permute-start | bytes 1376264 | tf_op jit(solution)/shard_map/ppermute | solution.py:59
  42.4 45.6 %collective-permute-start.10 = (bf16[4,64,2048]{2,1,0:T(8,128)(2,1)S(1)}, bf16[4,64,2048]{2,1,0:T(8,128)(2,1)S(1)}, u32[]{:S(2)}, u32[]{:S(2)}) collective-permute-start(bf16[4,64,2048]{2,1,0:T(8,128)(2,1)S(1)} %slice_bitcast_fusion.11), channel_id=1, source_target_pairs={{0,1},{1,0},{2,3},{3,2},{4,5},{5,4},{6,7},{7,6},{8,9},{9,8},{10,11... | collective-permute-start | bytes 3145736 | tf_op jit(solution)/shard_map/ppermute | solution.py:59
  89.7 66.4 %collective-permute-start.11 = (bf16[2,64,2048]{2,1,0:T(8,128)(2,1)}, bf16[2,64,2048]{2,1,0:T(8,128)(2,1)S(1)}, u32[]{:S(2)}, u32[]{:S(2)}) collective-permute-start(bf16[2,64,2048]{2,1,0:T(8,128)(2,1)} %shard_map.224), channel_id=1, source_target_pairs={{0,6},{1,7},{2,0},{3,1},{4,2},{5,3},{6,4},{7,5},{8,14},{9,15},{10,... | collective-permute-start | bytes 1572872 | tf_op jit(solution)/shard_map/ppermute | solution.py:55
  93.6 62.5 %collective-permute-start.12 = (bf16[2,64,2048]{2,1,0:T(8,128)(2,1)}, bf16[2,64,2048]{2,1,0:T(8,128)(2,1)S(1)}, u32[]{:S(2)}, u32[]{:S(2)}) collective-permute-start(bf16[2,64,2048]{2,1,0:T(8,128)(2,1)} %shard_map.225), channel_id=1, source_target_pairs={{0,4},{1,5},{2,6},{3,7},{4,0},{5,1},{6,2},{7,3},{8,12},{9,13},{10,... | collective-permute-start | bytes 1572872 | tf_op jit(solution)/shard_map/ppermute | solution.py:55
  114.8 41.3 %collective-permute-start.13 = (bf16[2,64,2048]{2,1,0:T(8,128)(2,1)}, bf16[2,64,2048]{2,1,0:T(8,128)(2,1)}, u32[]{:S(2)}, u32[]{:S(2)}) collective-permute-start(bf16[2,64,2048]{2,1,0:T(8,128)(2,1)} %shard_map.226), channel_id=1, source_target_pairs={{0,2},{1,3},{2,4},{3,5},{4,6},{5,7},{6,0},{7,1},{8,10},{9,11},{10,... | collective-permute-start | bytes 1572872 | tf_op jit(solution)/shard_map/ppermute | solution.py:55
  121.2 35.0 %collective-permute-start.18 = (bf16[128,2048]{1,0:T(8,128)(2,1)}, bf16[128,2048]{1,0:T(8,128)(2,1)S(1)}, u32[]{:S(2)}, u32[]{:S(2)}) collective-permute-start(bf16[128,2048]{1,0:T(8,128)(2,1)} %slice.467), channel_id=1, source_target_pairs={{0,8},{8,0},{16,24},{24,16},{1,9},{9,1},{17,25},{25,17},{2,10},{10... | collective-permute-start | bytes 1572872 | tf_op jit(solution)/shard_map/ppermute | solution.py:63
  124.4 31.8 %collective-permute-start.19 = (bf16[128,2048]{1,0:T(8,128)(2,1)}, bf16[128,2048]{1,0:T(8,128)(2,1)S(1)}, u32[]{:S(2)}, u32[]{:S(2)}) collective-permute-start(bf16[128,2048]{1,0:T(8,128)(2,1)} %slice.468), channel_id=1, source_target_pairs={{0,16},{8,24},{16,0},{24,8},{1,17},{9,25},{17,1},{25,9},{2,18},{10... | collective-permute-start | bytes 1572872 | tf_op jit(solution)/shard_map/ppermute | solution.py:63
  162.1 102.0 %all-gather.7.cloned.1.call-start = ((), (), s32[]{:S(2)}) async-start(), calls=%async_computation.6 | async-start | bytes 4718592 | tf_op jit(solution)/shard_map/all_gather | solution.py:91
  167.3 47.6 %collective-permute-start.20 = (bf16[512,2048]{1,0:T(8,128)(2,1)S(1)}, bf16[512,2048]{1,0:T(8,128)(2,1)}, u32[]{:S(2)}, u32[]{:S(2)}) collective-permute-start(bf16[512,2048]{1,0:T(8,128)(2,1)S(1)} %bitcast.258), channel_id=1, source_target_pairs={{0,8},{8,0},{16,24},{24,16},{1,9},{9,1},{17,25},{25,17},{2,10},{10... | collective-permute-start | bytes 6291464 | tf_op jit(solution)/shard_map/ppermute | solution.py:63
  168.0 46.9 %collective-permute-start.21 = (bf16[512,2048]{1,0:T(8,128)(2,1)S(1)}, bf16[512,2048]{1,0:T(8,128)(2,1)}, u32[]{:S(2)}, u32[]{:S(2)}) collective-permute-start(bf16[512,2048]{1,0:T(8,128)(2,1)S(1)} %bitcast.259), channel_id=1, source_target_pairs={{0,16},{8,24},{16,0},{24,8},{1,17},{9,25},{17,1},{25,9},{2,18},{10... | collective-permute-start | bytes 6291464 | tf_op jit(solution)/shard_map/ppermute | solution.py:63
  218.6 118.6 %reduce-scatter.7.cloned.1.call-start = ((), (), s32[]{:S(2)}) async-start(), calls=%async_computation.7 | async-start | bytes 4718592 | tf_op jit(solution)/shard_map/reduce_scatter | solution.py:95
  288.3 96.4 %all-gather.9.cloned.1.call-start = ((), (), s32[]{:S(2)}) async-start(), calls=%async_computation.8 | async-start | bytes 4718592 | tf_op jit(solution)/shard_map/all_gather | solution.py:91
  339.3 119.6 %reduce-scatter.9.cloned.1.call-start = ((), (), s32[]{:S(2)}) async-start(), calls=%async_computation.9 | async-start | bytes 4718592 | tf_op jit(solution)/shard_map/reduce_scatter | solution.py:95
  410.0 115.6 %all-gather.11.cloned.1.call-start = ((), (), s32[]{:S(2)}) async-start(), calls=%async_computation.10 | async-start | bytes 4718592 | tf_op jit(solution)/shard_map/all_gather | solution.py:91
  465.4 160.7 %reduce-scatter.11.cloned.1.call-start = ((), (), s32[]{:S(2)}) async-start(), calls=%async_computation.11 | async-start | bytes 4718592 | tf_op jit(solution)/shard_map/reduce_scatter | solution.py:95
  470.3 45.5 %collective-permute-start.25 = (bf16[2,256,2048]{2,1,0:T(8,128)(2,1)}, bf16[2,256,2048]{2,1,0:T(8,128)(2,1)}, u32[]{:S(2)}, u32[]{:S(2)}) collective-permute-start(bf16[2,256,2048]{2,1,0:T(8,128)(2,1)} %pad_maximum_fusion.3), channel_id=1, source_target_pairs={{0,16},{8,24},{16,0},{24,8},{1,17},{9,25},{17,1},{25,9},{2,18},{10... | collective-permute-start | bytes 6291464 | tf_op jit(solution)/shard_map/ppermute | solution.py:63
  473.3 45.3 %collective-permute-start.24 = (bf16[2,256,2048]{2,1,0:T(8,128)(2,1)}, bf16[2,256,2048]{2,1,0:T(8,128)(2,1)}, u32[]{:S(2)}, u32[]{:S(2)}) collective-permute-start(bf16[2,256,2048]{2,1,0:T(8,128)(2,1)} %pad_maximum_fusion.2), channel_id=1, source_target_pairs={{0,8},{8,0},{16,24},{24,16},{1,9},{9,1},{17,25},{25,17},{2,10},{10... | collective-permute-start | bytes 6291464 | tf_op jit(solution)/shard_map/ppermute | solution.py:63
  522.3 38.9 %collective-permute-start.44 = (bf16[256,2048]{1,0:T(8,128)(2,1)}, bf16[256,2048]{1,0:T(8,128)(2,1)}, u32[]{:S(2)}, u32[]{:S(2)}) collective-permute-start(bf16[256,2048]{1,0:T(8,128)(2,1)} %get-tuple-element.49), channel_id=1, source_target_pairs={{0,8},{8,0},{16,24},{24,16},{1,9},{9,1},{17,25},{25,17},{2,10},{10... | collective-permute-start | bytes 3145736 | tf_op jit(solution)/shard_map/ppermute | solution.py:63
  523.8 37.4 %collective-permute-start.43 = (bf16[256,2048]{1,0:T(8,128)(2,1)}, bf16[256,2048]{1,0:T(8,128)(2,1)}, u32[]{:S(2)}, u32[]{:S(2)}) collective-permute-start(bf16[256,2048]{1,0:T(8,128)(2,1)} %get-tuple-element.48), channel_id=1, source_target_pairs={{0,16},{8,24},{16,0},{24,8},{1,17},{9,25},{17,1},{25,9},{2,18},{10... | collective-permute-start | bytes 3145736 | tf_op jit(solution)/shard_map/ppermute | solution.py:63
  534.3 70.2 %collective-permute-start.50 = (bf16[2,128,2048]{2,1,0:T(8,128)(2,1)}, bf16[2,128,2048]{2,1,0:T(8,128)(2,1)S(1)}, u32[]{:S(2)}, u32[]{:S(2)}) collective-permute-start(bf16[2,128,2048]{2,1,0:T(8,128)(2,1)} %pad_maximum_fusion.9), channel_id=1, source_target_pairs={{0,16},{8,24},{16,0},{24,8},{1,17},{9,25},{17,1},{25,9},{2,18},{10... | collective-permute-start | bytes 3145736 | tf_op jit(solution)/shard_map/ppermute | solution.py:63
  536.8 67.6 %collective-permute-start.49 = (bf16[2,128,2048]{2,1,0:T(8,128)(2,1)}, bf16[2,128,2048]{2,1,0:T(8,128)(2,1)S(1)}, u32[]{:S(2)}, u32[]{:S(2)}) collective-permute-start(bf16[2,128,2048]{2,1,0:T(8,128)(2,1)} %pad_maximum_fusion.8), channel_id=1, source_target_pairs={{0,8},{8,0},{16,24},{24,16},{1,9},{9,1},{17,25},{25,17},{2,10},{10... | collective-permute-start | bytes 3145736 | tf_op jit(solution)/shard_map/ppermute | solution.py:63
  567.5 38.7 %collective-permute-start.45 = (bf16[4,64,2048]{2,1,0:T(8,128)(2,1)}, bf16[4,64,2048]{2,1,0:T(8,128)(2,1)}, u32[]{:S(2)}, u32[]{:S(2)}) collective-permute-start(bf16[4,64,2048]{2,1,0:T(8,128)(2,1)} %slice_bitcast_fusion), channel_id=1, source_target_pairs={{0,1},{1,0},{2,3},{3,2},{4,5},{5,4},{6,7},{7,6},{8,9},{9,8},{10,11... | collective-permute-start | bytes 3145736 | tf_op jit(solution)/shard_map/ppermute | solution.py:59
  613.8 34.2 %collective-permute-start.47 = (bf16[2,64,2048]{2,1,0:T(8,128)(2,1)}, bf16[2,64,2048]{2,1,0:T(8,128)(2,1)}, u32[]{:S(2)}, u32[]{:S(2)}) collective-permute-start(bf16[2,64,2048]{2,1,0:T(8,128)(2,1)} %pad_maximum_fusion.23), channel_id=1, source_target_pairs={{0,4},{1,5},{2,6},{3,7},{4,0},{5,1},{6,2},{7,3},{8,12},{9,13},{10,... | collective-permute-start | bytes 1572872 | tf_op jit(solution)/shard_map/ppermute | solution.py:55
  619.2 38.0 %collective-permute-start.46 = (bf16[2,64,2048]{2,1,0:T(8,128)(2,1)}, bf16[2,64,2048]{2,1,0:T(8,128)(2,1)}, u32[]{:S(2)}, u32[]{:S(2)}) collective-permute-start(bf16[2,64,2048]{2,1,0:T(8,128)(2,1)} %pad_maximum_fusion.22), channel_id=1, source_target_pairs={{0,6},{1,7},{2,0},{3,1},{4,2},{5,3},{6,4},{7,5},{8,14},{9,15},{10,... | collective-permute-start | bytes 1572872 | tf_op jit(solution)/shard_map/ppermute | solution.py:55
  622.2 38.6 %collective-permute-start.38 = (bf16[2,64,768]{2,1,0:T(8,128)(2,1)}, bf16[2,64,768]{2,1,0:T(8,128)(2,1)S(1)}, u32[]{:S(2)}, u32[]{:S(2)}) collective-permute-start(bf16[2,64,768]{2,1,0:T(8,128)(2,1)} %pad_maximum_fusion.34), channel_id=1, source_target_pairs={{0,2},{1,3},{2,4},{3,5},{4,6},{5,7},{6,0},{7,1},{8,10},{9,11},{10,... | collective-permute-start | bytes 589832 | tf_op jit(solution)/shard_map/ppermute | solution.py:55
  635.9 31.8 %collective-permute-start.37 = (bf16[2,64,768]{2,1,0:T(8,128)(2,1)}, bf16[2,64,768]{2,1,0:T(8,128)(2,1)S(1)}, u32[]{:S(2)}, u32[]{:S(2)}) collective-permute-start(bf16[2,64,768]{2,1,0:T(8,128)(2,1)} %pad_maximum_fusion.33), channel_id=1, source_target_pairs={{0,4},{1,5},{2,6},{3,7},{4,0},{5,1},{6,2},{7,3},{8,12},{9,13},{10,... | collective-permute-start | bytes 589832 | tf_op jit(solution)/shard_map/ppermute | solution.py:55
  637.4 30.3 %collective-permute-start.36 = (bf16[2,64,768]{2,1,0:T(8,128)(2,1)}, bf16[2,64,768]{2,1,0:T(8,128)(2,1)S(1)}, u32[]{:S(2)}, u32[]{:S(2)}) collective-permute-start(bf16[2,64,768]{2,1,0:T(8,128)(2,1)} %pad_maximum_fusion.32), channel_id=1, source_target_pairs={{0,6},{1,7},{2,0},{3,1},{4,2},{5,3},{6,4},{7,5},{8,14},{9,15},{10,... | collective-permute-start | bytes 589832 | tf_op jit(solution)/shard_map/ppermute | solution.py:55
  (93 other events, 1782.4 us)
Sparse Core Ops, SparseCore 0:
  14.5 63.3 all-gather.4
  162.2 50.5 reduce-scatter.4
  218.7 45.2 all-gather.6
  288.4 48.7 reduce-scatter.6
  339.4 45.2 all-gather.8
  410.1 48.7 reduce-scatter.8
  465.5 45.2 all-gather.10
  561.3 50.1 reduce-scatter.10

commit v4 on v3

--- a/solution.py
+++ b/solution.py
@@ -69,6 +69,8 @@
 
 
 def tie(value, *others):
+    if not others:
+        return value
     anywhere = pl.BlockSpec(memory_space=pl.ANY)
     return pl.pallas_call(
         lambda *refs: None,
@@ -92,9 +94,7 @@
 
 
 def scatter_rows(partial):
-    return lax.psum_scatter(
-        partial.astype(BF), "seq", scatter_dimension=0, tiled=True
-    ).astype(F32)
+    return lax.psum_scatter(partial, "seq", scatter_dimension=0, tiled=True)
 
 
 def move(kernel, out_shapes, *operands, first=()):
@@ -128,41 +128,51 @@
     cols = blocks * sum(parts) + (128 if rows_of_extra else 0)
 
     def kernel(at, *refs):
-        out = refs[-1]
         chip, core = at[0], at[1]
         extra = []
         if rows_of_extra:
             filled = jnp.zeros((rows, 128), F32)
             which = lax.broadcasted_iota(jnp.int32, (rows, 128), 0)
-            for i, ref in enumerate(refs[len(parts) : -1]):
+            for i, ref in enumerate(refs[len(parts) : -2]):
                 filled = jnp.where(which == i, ref[...], filled)
             extra = [filled.astype(BF)]
         for z in range(chips):
+            sides = []
             for c in range(2):
                 runs = []
                 for ref, part in zip(refs, parts):
                     for b in range(blocks):
                         start = ((b * chips + z) * 2 + c) * part
                         runs.append(ref[:, start : start + part])
-                out[(c + core) % 2, (z - chip + chips) % chips] = jnp.concatenate(
-                    runs + extra, axis=1
-                )
-
+                sides.append(jnp.concatenate(runs + extra, axis=1))
+            step = (z - chip + chips) % chips
+            refs[-2][step] = jnp.where(core == 0, sides[0], sides[1])
+            refs[-1][step] = jnp.where(core == 0, sides[1], sides[0])
+
+    side = jax.ShapeDtypeStruct((chips, rows, cols), weights[0].dtype)
     return move(
         kernel,
-        jax.ShapeDtypeStruct((2, chips, rows, cols), weights[0].dtype),
+        (side, side),
         here(),
         *weights,
         *rows_of_extra,
     )
 
 
-def exchange(pieces, first=()):
-    chip, core, chips = place()
-    other = swap(pieces[1])
-    shares = [jnp.stack([pieces[0, step], other[step]]) for step in range(chips)]
-    if first:
-        shares = [tie(share, *first) for share in shares]
+def pairs_of(mine, given, first=()):
+    chips = mine.shape[0]
+
+    def kernel(one, two, *outs):
+        for step, out in enumerate(outs):
+            out[0] = one[step]
+            out[1] = two[step]
+
+    pair = jax.ShapeDtypeStruct((2, *mine.shape[1:]), mine.dtype)
+    return move(kernel, (pair,) * chips, mine, swap(given), first=first)
+
+
+def exchange(shares):
+    chips = len(shares)
     arrived = {0: shares[0]}
     for step in order(chips):
         arrived[chips - step] = turn(shares[step], -step)
@@ -193,21 +203,22 @@
     cols = summed.shape[1]
     rows = summed.shape[0] // (2 * chips)
 
-    def kernel(at, ref, out):
+    def kernel(at, ref, mine, given):
         chip, core = at[0], at[1]
         for step in range(chips):
-            for k in range(2):
-                out[k, step] = ref[(chip + step) % chips, (core + k) % 2]
-
+            mine[step] = ref[(chip + step) % chips, core]
+            given[step] = ref[(chip + step) % chips, 1 - core]
+
+    side = jax.ShapeDtypeStruct((chips, rows, cols), summed.dtype)
     return move(
         kernel,
-        jax.ShapeDtypeStruct((2, chips, rows, cols), summed.dtype),
+        (side, side),
         here(),
         summed.reshape(chips, 2, rows, cols),
     )
 
 
-def columns_to(arrived, blocks, widths):
+def columns_to(arrived, blocks, widths, first=()):
     chip, core, chips = place()
     pair, rows, cols = arrived[0].shape
     parts = [w // blocks for w in widths]
@@ -234,6 +245,7 @@
         tuple(jax.ShapeDtypeStruct((rows, 2 * chips * w), F32) for w in widths),
         here(),
         *arrived,
+        first=first,
     )
 
 
@@ -265,60 +277,149 @@
     return jnp.concatenate(flipped(jnp.split(values, 4, axis=-1)), axis=-1)
 
 
-def gather_square(local, ordered=False):
+def gather_square(local, ordered=False, first=()):
     if not square():
         return lax.all_gather(local, "fsdp", axis=0, tiled=True), ((), ())
-    half = local.shape[0] // 2
+    rows, cols = local.shape
+    half = rows // 2
     one = beside(local, 1)
     two = beside(local, 2)
     three = beside(two[:half], 1)
     four = beside(one[half:], 2)
-    steps = ((one, two), (three, four))
-    if ordered:
-        last = jnp.concatenate([three, four], axis=0)
-        return jnp.concatenate(flipped([local, one, two, last]), axis=0), steps
-    return jnp.concatenate([local, one, two, three, four], axis=0), steps
-
-
-def begin_square(grad, ordered=False):
-    grad = grad.astype(BF)
+
+    flip = lax.axis_index("fsdp") if ordered else jnp.int32(0)
+
+    def kernel(at, *refs):
+        for i, ref in enumerate(refs[:3]):
+            refs[-1][i ^ at[0]] = ref[...]
+        refs[-1][3 ^ at[0], :half] = refs[3][...]
+        refs[-1][3 ^ at[0], half:] = refs[4][...]
+
+    whole = move(
+        kernel,
+        jax.ShapeDtypeStruct((4, rows, cols), local.dtype),
+        flip.astype(jnp.int32)[None],
+        local,
+        one,
+        two,
+        three,
+        four,
+        first=first,
+    )
+    return whole.reshape(4 * rows, cols), ((one, two), (three, four))
+
+
+def weight_terms(rows, grads, blocks, out_rows, turned=(False, False), first=()):
+    length = rows.shape[1 if turned[0] else 0]
+    cols = grads.shape[0 if turned[1] else 1]
+
+    def kernel(at, rows_ref, grads_ref, *refs):
+        contract = (((1,), (1 if turned[1] else 0,)), ((), ()))
+        left = rows_ref[...] if turned[0] else rows_ref[...].T
+        refs[-1][0] = lax.dot_general(
+            left, grads_ref[...], contract, preferred_element_type=F32
+        ).astype(BF)
+
+    return pl.pallas_call(
+        kernel,
+        grid_spec=pltpu.PrefetchScalarGridSpec(
+            num_scalar_prefetch=1,
+            grid=(blocks.shape[0],),
+            in_specs=[
+                pl.BlockSpec((out_rows, length), lambda i, at: (at[i], 0))
+                if turned[0]
+                else pl.BlockSpec((length, out_rows), lambda i, at: (0, at[i])),
+                pl.BlockSpec(grads.shape, lambda i, at: (0, 0)),
+            ]
+            + [pl.BlockSpec(memory_space=pl.ANY)] * len(first),
+            out_specs=pl.BlockSpec((1, out_rows, cols), lambda i, at: (i, 0, 0)),
+        ),
+        out_shape=jax.ShapeDtypeStruct((blocks.shape[0], out_rows, cols), BF),
+        compiler_params=pltpu.CompilerParams(vmem_limit_bytes=48 * 2**20),
+        cost_estimate=pl.CostEstimate(
+            flops=2 * length * out_rows * cols * blocks.shape[0],
+            bytes_accessed=2 * (length * (cols + out_rows * blocks.shape[0])),
+            transcendentals=0,
+        ),
+    )(blocks, rows, grads, *first)
+
+
+def begin_square(rows, grads, ordered=False, turned=(False, False), first=(), last=()):
     if not square():
-        return (lax.psum_scatter(grad, "fsdp", scatter_dimension=0, tiled=True),)
-    rows, cols = grad.shape
-    g = grad.reshape(4, 2, rows // 8, cols)
-    if ordered:
-        own = lax.axis_index("fsdp")
-        g = [lax.dynamic_index_in_dim(g, own ^ i, 0, keepdims=False) for i in range(4)]
-        g = {(i, j): g[i][j] for i in range(4) for j in range(2)}
-    return (
-        g,
-        beside(jnp.stack([g[1, 0], g[3, 0]]), 1),
-        beside(jnp.stack([g[2, 1], g[3, 1]]), 2),
-    )
-
-
-def second_square(g, one=None, two=None):
+        rows, grads = rows.T if turned[0] else rows, grads.T if turned[1] else grads
+        terms = transposed(rows, grads).astype(BF)
+        return (lax.psum_scatter(terms, "fsdp", scatter_dimension=0, tiled=True),), ()
+    half = rows.shape[0 if turned[0] else 1] // 8
+    flip = lax.axis_index("fsdp") if ordered else 0
+
+    def terms(which, first):
+        at = jnp.stack([2 * (jnp.int32(r) ^ flip) + h for r, h in which]).astype(jnp.int32)
+        return weight_terms(rows, grads, at, half, turned, first)
+
+    one = terms([(1, 0), (3, 0)], first)
+    two = terms([(2, 1), (3, 1)], first)
+    kept = terms([(2, 0), (1, 1), (0, 0), (0, 1)], (one, two, *last))
+    return (kept, beside(one, 1), beside(two, 2)), (one, two)
+
+
+def begin_square_of(terms, first=()):
+    rows, cols = terms.shape
+    half = rows // 8
+
+    def kernel(at, g, one, two, kept):
+        f = at[0]
+        one[0], one[1] = g[1 ^ f, 0], g[3 ^ f, 0]
+        two[0], two[1] = g[2 ^ f, 1], g[3 ^ f, 1]
+        kept[0], kept[1] = g[2 ^ f, 0], g[1 ^ f, 1]
+        kept[2], kept[3] = g[0 ^ f, 0], g[0 ^ f, 1]
+
+    pair = jax.ShapeDtypeStruct((2, half, cols), BF)
+    one, two, kept = move(
+        kernel,
+        (pair, pair, jax.ShapeDtypeStruct((4, half, cols), BF)),
+        flip(),
+        terms.reshape(4, 2, half, cols),
+        first=first,
+    )
+    return kept, beside(one, 1), beside(two, 2)
+
+
+def second_square(kept, one=None, two=None, first=()):
     if one is None:
-        return (g,)
-    def kernel(a, b, c, d, first, second):
-        first[...] = (a[...].astype(F32) + b[1].astype(F32)).astype(BF)
-        second[...] = (c[...].astype(F32) + d[1].astype(F32)).astype(BF)
-
-    part = jax.ShapeDtypeStruct(g[2, 0].shape, BF)
-    first, second = move(kernel, (part, part), g[2, 0], one, g[1, 1], two)
-    return g, one, two, beside(first, 2), beside(second, 1)
-
-
-def finish_square(g, one=None, two=None, one_last=None, two_last=None):
+        return (kept,)
+    before = first
+
+    def kernel(kept, one, two, first, second):
+        first[...] = (kept[0].astype(F32) + one[1].astype(F32)).astype(BF)
+        second[...] = (kept[1].astype(F32) + two[1].astype(F32)).astype(BF)
+
+    part = jax.ShapeDtypeStruct(kept.shape[1:], BF)
+    first, second = move(kernel, (part, part), kept, one, two, first=before)
+    return kept, one, two, beside(first, 2), beside(second, 1)
+
+
+def finish_square(
+    kept, one=None, two=None, one_last=None, two_last=None, kind=BF, first=()
+):
     if one is None:
-        return g
-    return jnp.concatenate(
-        [
-            g[0, 0].astype(F32) + one[0].astype(F32) + one_last.astype(F32),
-            g[0, 1].astype(F32) + two[0].astype(F32) + two_last.astype(F32),
-        ],
-        axis=0,
-    ).astype(BF)
+        return kept.astype(kind)
+
+    def kernel(kept, one, two, one_last, two_last, out):
+        wide = lambda x: x.astype(F32)
+        out[0] = (wide(kept[2]) + wide(one[0]) + wide(one_last[...])).astype(kind)
+        out[1] = (wide(kept[3]) + wide(two[0]) + wide(two_last[...])).astype(kind)
+
+    half, cols = kept.shape[1:]
+    return move(
+        kernel,
+        jax.ShapeDtypeStruct((2, half, cols), kind),
+        kept,
+        one,
+        two,
+        one_last,
+        two_last,
+        first=first,
+    ).reshape(2 * half, cols)
 
 
 def turned(values, cosine, sine):
@@ -342,7 +443,7 @@
         bias_ref[:keys, first:keys] = jnp.where(same & ahead, 0.0, MASKED)
 
 
-def attend(qkv, cosine, sine, segment, block, heads):
+def attend(qkv, cosine, sine, segment, block, heads, first=()):
     length = qkv.shape[1]
     scale = HD ** (-0.5)
 
@@ -374,19 +475,14 @@
     head = lambda offset: pl.BlockSpec((HD, length), lambda h: (h + offset, 0))
     whole = pl.BlockSpec(memory_space=pltpu.VMEM)
     tall = jax.ShapeDtypeStruct((heads * HD, length), BF)
+    anywhere = pl.BlockSpec(memory_space=pl.ANY)
     return pl.pallas_call(
-        kernel,
+        lambda *refs: kernel(*refs[:7], *refs[7 + len(first) :]),
         grid=(heads,),
         out_shape=(tall, tall, tall, tall, jax.ShapeDtypeStruct((heads, 1, length), F32)),
-        in_specs=[
-            head(0),
-            head(heads),
-            head(2 * heads),
-            whole,
-            whole,
-            whole,
-            whole,
-        ],
+        in_specs=[head(0), head(heads), head(2 * heads)]
+        + [whole] * 4
+        + [anywhere] * len(first),
         out_specs=(
             head(0),
             head(0),
@@ -401,16 +497,17 @@
             bytes_accessed=24 * heads * HD * length,
             transcendentals=heads * length * length,
         ),
-    )(qkv, qkv, qkv, cosine, sine, segment[:, None], segment[None, :])
-
-
-def attend_back(grad, query, key, value, logs, cosine, sine, segment, block, heads):
+    )(qkv, qkv, qkv, cosine, sine, segment[:, None], segment[None, :], *first)
+
+
+def attend_back(
+    grad, query, key, value, logs, cosine, sine, segment, block, heads, first=()
+):
     length = grad.shape[1]
     scale = HD ** (-0.5)
 
     def kernel(grad_ref, query_ref, key_ref, value_ref, log_ref, *refs):
-        cos_ref, sin_ref, column_ref, row_ref, dq_ref, dk_ref, dv_ref, bias_ref = refs[:8]
-        key_sum, value_sum = refs[8:]
+        cos_ref, sin_ref, column_ref, row_ref, out_ref, bias_ref, key_sum, value_sum = refs
 
         @pl.when(pl.program_id(0) == 0)
         def _():
@@ -437,18 +534,18 @@
                 key_sum[:keys] += key_part
                 value_sum[:keys] += value_part
             dq = (dot(key_t[:, :keys], grad_scores) * scale).astype(BF).astype(F32)
-            dq_ref[:, here_q] = turned(dq, cos[:, here_q], -sin[:, here_q]).astype(BF)
+            out_ref[0, :, here_q] = turned(dq, cos[:, here_q], -sin[:, here_q]).astype(BF)
         dk = key_sum[...].astype(BF).astype(F32).T
-        dk_ref[...] = turned(dk, cos, -sin).astype(BF)
-        dv_ref[...] = value_sum[...].T.astype(BF)
+        out_ref[1] = turned(dk, cos, -sin).astype(BF)
+        out_ref[2] = value_sum[...].T.astype(BF)
 
     head = pl.BlockSpec((HD, length), lambda h: (h, 0))
     whole = pl.BlockSpec(memory_space=pltpu.VMEM)
-    tall = jax.ShapeDtypeStruct((heads * HD, length), BF)
+    tall = jax.ShapeDtypeStruct((3, heads * HD, length), BF)
     return pl.pallas_call(
-        kernel,
+        lambda *refs: kernel(*refs[:9], *refs[9 + len(first) :]),
         grid=(heads,),
-        out_shape=(tall, tall, tall),
+        out_shape=tall,
         in_specs=[
             head,
             head,
@@ -459,8 +556,9 @@
             whole,
             whole,
             whole,
-        ],
-        out_specs=(head, head, head),
+        ]
+        + [pl.BlockSpec(memory_space=pl.ANY)] * len(first),
+        out_specs=pl.BlockSpec((3, HD, length), lambda h: (0, h, 0)),
         scratch_shapes=[
             pltpu.VMEM((length, length), F32),
             pltpu.VMEM((length, HD), F32),
@@ -472,21 +570,278 @@
             bytes_accessed=24 * heads * HD * length,
             transcendentals=heads * length * length,
         ),
-    )(grad, query, key, value, logs, cosine, sine, segment[:, None], segment[None, :])
-
-
-def sum_to_owners(values):
-    for axis in ALL:
-        size, own = lax.axis_size(axis), lax.axis_index(axis)
-        bit = size // 2
-        while bit:
-            halves = values.reshape(2, values.shape[0] // 2, values.shape[1])
-            mine = (own // bit) % 2
-            keep = lax.dynamic_index_in_dim(halves, mine, 0, keepdims=False)
-            give = lax.dynamic_index_in_dim(halves, 1 - mine, 0, keepdims=False)
-            values = keep + lax.ppermute(give, axis, [(s, s ^ bit) for s in range(size)])
-            bit //= 2
-    return values[0]
+    )(grad, query, key, value, logs, cosine, sine, segment[:, None], segment[None, :], *first)
+
+
+def gain_terms(grads, rows, scales, first=()):
+    length, width = rows.shape
+    block = 256
+
+    def kernel(grad_ref, row_ref, scale_ref, *refs):
+        total = jnp.zeros((1, block), F32)
+        step = 256
+        for at in range(0, length, step):
+            terms = grad_ref[at : at + step].astype(F32) * row_ref[at : at + step].astype(F32)
+            total += jnp.sum(terms * scale_ref[at : at + step], axis=0, keepdims=True)
+        refs[-1][...] = total
+
+    column = pl.BlockSpec((length, block), lambda i: (0, i))
+    return pl.pallas_call(
+        kernel,
+        grid=(width // block,),
+        out_shape=jax.ShapeDtypeStruct((1, width), F32),
+        in_specs=[
+            column,
+            column,
+            pl.BlockSpec((length, 1), lambda i: (0, 0)),
+        ]
+        + [pl.BlockSpec(memory_space=pl.ANY)] * len(first),
+        out_specs=pl.BlockSpec((1, block), lambda i: (0, i)),
+        cost_estimate=pl.CostEstimate(
+            flops=4 * length * width, bytes_accessed=4 * length * width, transcendentals=0
+        ),
+    )(grads, rows, scales, *first).reshape(width)
+
+
+def mlp(rows, gate_up_weight, down_full):
+    length, width = rows.shape
+    hidden_width = down_full.shape[0]
+    tall, block = min(1024, length), min(256, hidden_width)
+    steps = hidden_width // block
+
+    def kernel(x_ref, gate_w, up_w, down_w, gate_ref, up_ref, hidden_ref, out_ref, total):
+        x = x_ref[...]
+        gate, up = dot(x, gate_w[...]), dot(x, up_w[...])
+        hidden = gated(gate, up).astype(BF)
+        gate_ref[...], up_ref[...], hidden_ref[...] = gate, up, hidden
+        terms = dot(hidden, down_w[...])
+        step = pl.program_id(1)
+
+        @pl.when(step == 0)
+        def _():
+            total[...] = terms
+
+        @pl.when((step > 0) & (step < steps - 1))
+        def _():
+            total[...] += terms
+
+        @pl.when(step == steps - 1)
+        def _():
+            out_ref[...] = (total[...] + terms).astype(BF)
+
+    part = pl.BlockSpec((tall, block), lambda i, j: (i, j))
+    whole = pl.BlockSpec((tall, width), lambda i, j: (i, 0))
+    wide = jax.ShapeDtypeStruct((length, hidden_width), F32)
+    return pl.pallas_call(
+        kernel,
+        grid=(length // tall, steps),
+        out_shape=(
+            wide,
+            wide,
+            jax.ShapeDtypeStruct((length, hidden_width), BF),
+            jax.ShapeDtypeStruct((length, width), BF),
+        ),
+        in_specs=[
+            whole,
+            pl.BlockSpec((width, block), lambda i, j: (0, j)),
+            pl.BlockSpec((width, block), lambda i, j: (0, j + steps)),
+            pl.BlockSpec((block, width), lambda i, j: (j, 0)),
+        ],
+        out_specs=(part, part, part, whole),
+        scratch_shapes=[pltpu.VMEM((tall, width), F32)],
+        compiler_params=pltpu.CompilerParams(vmem_limit_bytes=60 * 2**20),
+        cost_estimate=pl.CostEstimate(
+            flops=6 * length * width * hidden_width,
+            bytes_accessed=6 * width * hidden_width + 4 * length * (width + 3 * hidden_width),
+            transcendentals=length * hidden_width,
+        ),
+    )(rows, gate_up_weight, gate_up_weight, down_full)
+
+
+def rows_back(columns, weight, first=()):
+    inner, length = columns.shape
+    width = weight.shape[0]
+    block = 512
+
+    def kernel(columns_ref, weight_ref, *refs):
+        out_ref, rows_ref = refs[-2:]
+
+        @pl.when(pl.program_id(0) == 0)
+        def _():
+            rows_ref[...] = columns_ref[...].T
+
+        out_ref[...] = against(rows_ref[...], weight_ref[...]).astype(BF)
+
+    return pl.pallas_call(
+        kernel,
+        grid=(width // block,),
+        out_shape=jax.ShapeDtypeStruct((length, width), BF),
+        in_specs=[
+            pl.BlockSpec((inner, length), lambda j: (0, 0)),
+            pl.BlockSpec((block, inner), lambda j: (j, 0)),
+        ]
+        + [pl.BlockSpec(memory_space=pl.ANY)] * len(first),
+        out_specs=pl.BlockSpec((length, block), lambda j: (0, j)),
+        scratch_shapes=[pltpu.VMEM((length, inner), BF)],
+        compiler_params=pltpu.CompilerParams(vmem_limit_bytes=48 * 2**20),
+        cost_estimate=pl.CostEstimate(
+            flops=2 * length * width * inner,
+            bytes_accessed=2 * (length * (width + inner) + width * inner),
+            transcendentals=0,
+        ),
+    )(columns, weight, *first)
+
+
+def flip():
+    return (lax.axis_index("fsdp") if square() else jnp.int32(0)).astype(jnp.int32)[None]
+
+
+def spots(at, width):
+    size = width // 4
+    return [pl.ds(pl.multiple_of((g ^ at[0]) * size, size), size) for g in range(4)]
+
+
+def steadied(values):
+    return lax.rsqrt(jnp.mean(values * values, axis=-1, keepdims=True) + EPSILON)
+
+
+def after_first_sum(summed, tokens, gain, first):
+    rows, width = tokens.shape
+
+    def kernel(at, summed_ref, tokens_ref, gain_ref, attended_ref, normed_ref):
+        values = tokens_ref[...].astype(F32) + summed_ref[...].astype(F32)
+        attended_ref[...] = values
+        normed = (values * steadied(values) * gain_ref[...]).astype(BF)
+        for g, spot in enumerate(spots(at, width)):
+            normed_ref[:, spot] = normed[:, g * (width // 4) : (g + 1) * (width // 4)]
+
+    return move(
+        kernel,
+        (
+            jax.ShapeDtypeStruct((rows, width), F32),
+            jax.ShapeDtypeStruct((rows, width), BF),
+        ),
+        flip(),
+        summed,
+        tokens,
+        gain[None, :],
+        first=first,
+    )
+
+
+def after_second_sum(summed, attended, teacher, mask, weight):
+    rows, width = attended.shape
+
+    def kernel(summed_ref, attended_ref, teacher_ref, mask_ref, weight_ref, *outs):
+        out_ref, grad_ref, low_ref, error_ref = outs
+        result = attended_ref[...] + summed_ref[...].astype(F32)
+        difference = result - teacher_ref[...].astype(F32)
+        out_ref[...] = result.astype(BF)
+        grad = weight_ref[...] * difference
+        grad_ref[...] = grad
+        low_ref[...] = grad.astype(BF)
+        terms = jnp.sum(mask_ref[...] * difference * difference, axis=0, keepdims=True)
+        error_ref[...] = jnp.broadcast_to(jnp.sum(terms, axis=1, keepdims=True), (1, 128))
+
+    narrow = jax.ShapeDtypeStruct((rows, width), BF)
+    wide = jax.ShapeDtypeStruct((rows, width), F32)
+    return move(
+        kernel,
+        (narrow, wide, narrow, jax.ShapeDtypeStruct((1, 128), F32)),
+        summed,
+        attended,
+        teacher,
+        mask,
+        weight,
+    )
+
+
+def after_third_sum(summed, attended, gain, grad_result, first):
+    rows, width = attended.shape
+
+    def kernel(at, summed_ref, attended_ref, gain_ref, result_ref, wide_ref, low_ref, gain_out):
+        grads = jnp.concatenate([summed_ref[:, spot] for spot in spots(at, width)], axis=1)
+        grads = grads.astype(F32)
+        values = attended_ref[...]
+        steady = steadied(values)
+        gain_out[...] = jnp.sum(grads * values * steady, axis=0, keepdims=True)
+        scaled = grads * gain_ref[...]
+        inner = jnp.mean(scaled * values, axis=-1, keepdims=True)
+        total = result_ref[...] + steady * scaled - values * (steady * steady * steady * inner)
+        wide_ref[...] = total
+        low_ref[...] = total.astype(BF)
+
+    return move(
+        kernel,
+        (
+            jax.ShapeDtypeStruct((rows, width), F32),
+            jax.ShapeDtypeStruct((rows, width), BF),
+            jax.ShapeDtypeStruct((1, width), F32),
+        ),
+        flip(),
+        summed,
+        attended,
+        gain[None, :],
+        grad_result,
+        first=first,
+    )
+
+
+def after_last_sum(summed, tokens, gain, grad_after):
+    rows, width = tokens.shape
+
+    def kernel(at, summed_ref, tokens_ref, gain_ref, after_ref, out_ref):
+        grads = jnp.concatenate([summed_ref[:, spot] for spot in spots(at, width)], axis=1)
+        values = tokens_ref[...].astype(F32)
+        steady = steadied(values)
+        scaled = grads.astype(F32) * gain_ref[...]
+        inner = jnp.mean(scaled * values, axis=-1, keepdims=True)
+        out_ref[...] = (
+            after_ref[...] + steady * scaled - values * (steady * steady * steady * inner)
+        )
+
+    return move(
+        kernel,
+        jax.ShapeDtypeStruct((rows, width), F32),
+        flip(),
+        summed,
+        tokens,
+        gain[None, :],
+        grad_after,
+    )
+
+
+def sum_over_chips(values):
+    chip, core, chips = place()
+    shards, width = lax.axis_size("fsdp"), values.shape[1]
+    own = lax.axis_index("fsdp")
+
+    def share(values, at):
+        return lax.dynamic_index_in_dim(values, at, 0, keepdims=False)
+
+    values = values.reshape(shards, chips, 2, width)
+    total = share(values, own)
+    for step in range(1, shards):
+        total += lax.ppermute(
+            share(values, (own + step) % shards),
+            "fsdp",
+            [(f, (f + step) % shards) for f in range(shards)],
+        )
+    total = jnp.moveaxis(total, 1, 0)
+    return share(total, core) + swap(share(total, 1 - core))
+
+
+def sum_to_owners(values, first):
+    chip, core, chips = place()
+    values = tie(values, *first)
+
+    def share(step):
+        return lax.dynamic_index_in_dim(values, (chip + step) % chips, 0, keepdims=False)
+
+    total = share(0)
+    for step in order(chips):
+        total += turn(share(step), -step)
+    return total
 
 
 def body(
@@ -516,7 +871,7 @@
     head_blocks = shards if aligned else 1
     hw = heads * HD
 
-    inputs = tokens.reshape(local_rows, width).astype(F32)
+    own_tokens = tokens.reshape(local_rows, width)
     keep_mask = valid.reshape(local_rows).astype(F32)
     lane_pad = lambda row: jnp.pad(row, ((0, 0), (0, 128 - row.shape[1])))
     own_gains = jnp.concatenate([attention_gain, mlp_gain])[None, :]
@@ -527,23 +882,24 @@
         jnp.broadcast_to(jnp.sum(keep_mask), (1, 128)),
     )
     attention_shares = exchange(
-        columns_of([query_weight, key_weight, value_weight], head_blocks, extra_rows)
+        pairs_of(
+            *columns_of([query_weight, key_weight, value_weight], head_blocks, extra_rows)
+        )
     )
     if aligned:
-        out_weight, out_steps = gather_square(output_weight, ordered=True)
+        out_weight = lax.all_gather(output_weight, "fsdp", axis=0, tiled=True)
     else:
         out_weight = lax.dynamic_slice_in_dim(
             lax.all_gather(output_weight, ALL, axis=0, tiled=True), own * hw, hw, 0
         )
-        out_steps = ((), ())
     down_full, down_steps = gather_square(down_weight, ordered=True)
-    tokens_all = gather_rows(relative_blocks(tokens.reshape(local_rows, width)))
-    attention_in, unused = gather_square(
-        rows_of(attention_shares, first=down_steps[0])
+    tokens_all = gather_rows(
+        tie(relative_blocks(own_tokens), *attention_shares[1:], out_weight, *down_steps[0])
     )
     gate_up_shares = exchange(
-        columns_of([gate_weight, up_weight], shards), (attention_shares[chips // 2],)
-    )
+        pairs_of(*columns_of([gate_weight, up_weight], shards), first=attention_shares[1:])
+    )
+    attention_in = gather_square(rows_of(attention_shares))[0]
     gate_up_weight, gate_up_steps = gather_square(rows_of(gate_up_shares))
 
     qkv_weight = attention_in[:, : 3 * hw]
@@ -560,103 +916,137 @@
     segment = (table[:, 1, :local_rows] * 256 + table[:, 2, :local_rows]).reshape(length)
     cosine, sine = rope_tables(length)
 
-    normed = rms_norm(
-        tokens_all.astype(F32), normed_gain
-    ).astype(BF)
+    wide_tokens = tokens_all.astype(F32)
+    steady = lax.rsqrt(jnp.mean(wide_tokens * wide_tokens, axis=-1, keepdims=True) + EPSILON)
+    normed = (wide_tokens * steady * normed_gain).astype(BF)
     qkv = lax.dot_general(
         qkv_weight, normed, (((0,), (1,)), ((), ())), preferred_element_type=F32
     )
     mixed, query, key, value, logs = attend(
-        qkv, cosine, sine, segment, 2 * local_rows, heads
-    )
-    mixed = tie(mixed, *gate_up_shares[1:], *out_steps[1], *down_steps[1])
-    after_attention = inputs + tie(
-        scatter_rows(transposed(mixed, out_weight)), *gate_up_steps[0]
-    )
-    normed_two = gather_rows(
-        relative_blocks(rms_norm(after_attention, second_gain).astype(BF))
-    )
-    gate_up = matmul(normed_two, gate_up_weight)
-    hidden_width = gate_up.shape[1] // 2
-    gate_value, up_value = gate_up[:, :hidden_width], gate_up[:, hidden_width:]
-    hidden = gated(gate_value, up_value).astype(BF)
-    result = after_attention + scatter_rows(matmul(hidden, down_full))
-    difference = result - teacher.reshape(local_rows, width).astype(F32)
-    error_sum = jnp.sum(keep_mask[:, None] * difference * difference)
-    grad_result = 2.0 / count * keep_mask[:, None] * difference
-    grad_branch = gather_rows(grad_result.astype(BF))
+        qkv, cosine, sine, segment, 2 * local_rows, heads, first=(gate_up_shares[-1],)
+    )
+    mixed = tie(mixed, *gate_up_shares[1:], *down_steps[1])
+    after_attention, normed_two = after_first_sum(
+        scatter_rows(transposed(mixed, out_weight).astype(BF)),
+        own_tokens,
+        second_gain,
+        gate_up_steps[0],
+    )
+    normed_two = gather_rows(normed_two)
+    gate_value, up_value, hidden, partial = mlp(normed_two, gate_up_weight, down_full)
+    hidden_width = hidden.shape[1]
+    output, grad_result, grad_branch, error_sum = after_second_sum(
+        scatter_rows(partial),
+        after_attention,
+        teacher.reshape(local_rows, width),
+        keep_mask[:, None],
+        (2.0 / count * keep_mask)[:, None],
+    )
+    grad_branch = gather_rows(grad_branch)
     unused, gate_pull = jax.vjp(gated, gate_value, up_value)
     grad_gate, grad_upward = gate_pull(against(grad_branch, down_full))
-    gate_up_grad = jnp.concatenate([grad_gate.astype(BF), grad_upward.astype(BF)], axis=1)
-    grad_normed_sum = against(gate_up_grad, gate_up_weight).astype(BF)
-    grad_normed_two = scatter_rows(grad_normed_sum)
-    gate_up_weight_grad = transposed(normed_two, tie(gate_up_grad, grad_normed_sum)).astype(BF)
-    gate_up_back = begin_square(gate_up_weight_grad)
-    down_grad = transposed(hidden, tie(grad_branch, gate_up_weight_grad)).astype(BF)
-    grad_normed_two = relative_blocks(tie(grad_normed_two, down_grad))
-    unused, second_pull = jax.vjp(rms_norm, after_attention, second_gain)
-    grad_after, second_gain_grad = second_pull(grad_normed_two)
-    grad_after = grad_after + grad_result
-
-    grad_out = tie(gather_rows(grad_after.astype(BF)), *gate_up_back[1:])
-    gate_up_back = second_square(*gate_up_back)
+    grad_gate, grad_upward = grad_gate.astype(BF), grad_upward.astype(BF)
+    grad_normed_sum = against(
+        jnp.concatenate([grad_gate, grad_upward], axis=1), gate_up_weight
+    ).astype(BF)
+    gate_back, unused = begin_square(normed_two, grad_gate, first=(grad_normed_sum,))
+    up_back, unused = begin_square(
+        normed_two, grad_upward, first=(gate_back[0],), last=gate_back[1:]
+    )
+    grad_after, grad_out, second_gain_grad = after_third_sum(
+        scatter_rows(grad_normed_sum),
+        after_attention,
+        second_gain,
+        grad_result,
+        up_back,
+    )
+    gate_back = second_square(*gate_back)
+
+    grad_out = gather_rows(grad_out)
+    up_back = second_square(*up_back)
+    down_back, down_sent = begin_square(
+        hidden, grad_branch, ordered=True, first=(gate_back[0],), last=up_back[3:]
+    )
+    gate_up_pairs = pairs_of(
+        *rows_to(
+            jnp.concatenate(
+                [
+                    finish_square(*gate_back, first=down_sent),
+                    finish_square(*up_back),
+                ],
+                axis=1,
+            )
+        )
+    )
+    gate_up_shares = exchange(gate_up_pairs)
     grad_mixed = against(out_weight, grad_out).astype(BF)
-    output_grad = matmul(mixed, grad_out)
-    qkv_grad = jnp.concatenate(
-        attend_back(
-            grad_mixed, query, key, value, logs, cosine, sine, segment, 2 * local_rows, heads
-        ),
-        axis=0,
-    )
-    gate_up_back = finish_square(*gate_up_back[:-1], tie(gate_up_back[-1], qkv_grad))
-    gate_up_shares = exchange(rows_to(gate_up_back))
-    gate_sum, up_sum = columns_to(gate_up_shares, shards, [hidden_width, hidden_width])
-    down_back = second_square(*begin_square(tie(down_grad, grad_mixed), ordered=True))
-    down_sum = finish_square(*down_back).astype(F32)
-    if aligned:
-        output_back = second_square(*begin_square(output_grad, ordered=True))
-        output_sum = finish_square(*output_back).astype(F32)
+    qkv_grad = attend_back(
+        grad_mixed,
+        query,
+        key,
+        value,
+        logs,
+        cosine,
+        sine,
+        segment,
+        2 * local_rows,
+        heads,
+        first=gate_up_pairs,
+    ).reshape(3 * hw, length)
+    down_back = second_square(*down_back, first=gate_up_pairs)
+    grad_normed_sum = rows_back(
+        qkv_grad, attention_in, (*gate_up_shares[1:], *down_back[3:])
+    )
+    qkv_begun, unused = begin_square(
+        normed, qkv_grad, turned=(False, True), first=(grad_normed_sum,)
+    )
+    first_gain_grad = gain_terms(grad_normed_sum, tokens_all, steady, qkv_begun[:1])
+    output_grad = matmul(mixed, grad_out).astype(BF)
+    if aligned and square():
+        output_begun = begin_square_of(output_grad, first=qkv_begun[:1])
+        qkv_back = second_square(*qkv_begun, first=(*output_begun, first_gain_grad))
+        output_back = second_square(*output_begun)
+        output_sum = finish_square(*output_back, kind=F32)
     else:
+        qkv_back = second_square(*qkv_begun, first=(first_gain_grad,))
+        output_back = ()
         output_sum = lax.psum_scatter(
             lax.dynamic_update_slice_in_dim(
-                jnp.zeros((width, width), BF), output_grad.astype(BF), own * hw, 0
+                jnp.zeros((width, width), BF), output_grad, own * hw, 0
             ),
             ALL,
             scatter_dimension=0,
             tiled=True,
         ).astype(F32)
-    qkv_back = begin_square(
-        lax.dot_general(normed, qkv_grad, (((0,), (1,)), ((), ())), preferred_element_type=F32)
-    )
-    qkv_back = finish_square(*second_square(*qkv_back))
-    query_sum, key_sum, value_sum = columns_to(
-        exchange(rows_to(qkv_back)), head_blocks, [hw, hw, hw]
-    )
-
-    grad_normed = relative_blocks(
-        scatter_rows(
-            lax.dot_general(
-                qkv_grad, qkv_weight, (((0,), (1,)), ((), ())), preferred_element_type=F32
-            )
-        )
-    )
-    unused, first_pull = jax.vjp(rms_norm, inputs, first_gain)
-    grad_inputs, first_gain_grad = first_pull(grad_normed)
-    grad_inputs = grad_inputs + grad_after
     devices = shards * groups
-    sums = sum_to_owners(
+    sums = sum_over_chips(
         jnp.concatenate(
             [
-                first_gain_grad.reshape(devices, weight_rows),
+                relative_blocks(first_gain_grad).reshape(devices, weight_rows),
                 second_gain_grad.reshape(devices, weight_rows),
-                jnp.full((devices, 128), error_sum),
+                jnp.broadcast_to(error_sum, (devices, 128)),
             ],
             axis=1,
         )
     )
+    qkv_pairs = pairs_of(
+        *rows_to(finish_square(*qkv_back)), first=(sums, *output_back[3:])
+    )
+    qkv_shares = exchange(qkv_pairs)
+    query_sum, key_sum, value_sum = columns_to(qkv_shares, head_blocks, [hw, hw, hw])
+    gate_sum, up_sum = columns_to(
+        gate_up_shares, shards, [hidden_width, hidden_width], first=qkv_pairs[:1]
+    )
+    down_sum = finish_square(*down_back, kind=F32, first=qkv_pairs[:1])
+    grad_inputs = after_last_sum(
+        scatter_rows(grad_normed_sum), own_tokens, first_gain, grad_after
+    )
+    sums = sum_to_owners(
+        sums, (*qkv_shares[1:], gate_sum, down_sum, grad_inputs, output_sum)
+    )
     output_shape = (sequences, local_rows, width)
     return (
-        result.reshape(output_shape).astype(BF),
+        output.reshape(output_shape),
         sums[2 * weight_rows] / count,
         grad_inputs.reshape(output_shape),
         query_sum,

time: 696 us -> 670 us (0.963)
  Pallas kernels: 41.7 us -> 168 us
  matrix products: 92.2 us -> 36.9 us
  other arithmetic: 70.3 us -> 18.9 us
  waiting for transfers between devices: 325 us -> 290 us
    pallas_call x2 -> x17, Pallas kernels: 26.4 us -> 116 us  [the longest x12 52.4 us: weight_terms(): pl.pallas_call(kernel, grid_spec=pltpu.PrefetchScalarGridSpec(num_scalar_...]
    reduce_scatter x4, waiting for transfers between devices: 109 us -> 45.9 us  [scatter_rows(): return lax.psum_scatter(partial, 'seq', scatter_dimension=0, tiled=True)]
    pallas_call x12 -> x30, Pallas kernels: 15.3 us -> 52.1 us  [move(): pl.pallas_call(lambda *refs: kernel(*refs[:given], *refs[given + len(firs...]
    ppermute x32, waiting for transfers between devices: 108 us -> 136 us  [beside(): lax.ppermute(value, 'fsdp', [(f, f ^ bit) for f in range(lax.axis_size('f...]
    another operation x28 -> x2, other arithmetic: 23.7 us -> 0.15 us  [terms(): jnp.stack([2 * (jnp.int32(r) ^ flip) + h for r, h in which])]
    dot_general x3 -> x1, matrix products: 28.2 us -> 4.79 us  [transposed(): lax.dot_general(left_side, right_side, (((0,), (0,)), ((), ())), preferre...]
    dot_general x3 -> x1, matrix products: 19.8 us -> 1.25 us  [matmul(): return jnp.dot(left_side, right_side, preferred_element_type=F32)]
    all_gather x4, waiting for transfers between devices: 57.4 us -> 75 us  [gather_rows(): return lax.all_gather(local, 'seq', axis=0, tiled=True)]
  transfers between devices with their start and end apart: 61 -> 64, of which waited for: 29 -> 29; matrix products, arithmetic and copies ran while one was open for 22% -> 5% of each run, Pallas kernels for 6% -> 20%
where the time goes in v4:
time: 670 us; the launch traced here: 664 us
  waiting for transfers between devices  290 us (43%)
  Pallas kernels  168 us (25%)
  local copies, waits for them, and re-layouts  67.7 us (10%)
  starting transfers between devices  63.8 us (10%)
  matrix products  36.9 us (6%)
  other arithmetic  18.9 us (3%)
  between operations  18.2 us (3%)
    ppermute x32, waiting for transfers between devices, beside(): lax.ppermute(value, 'fsdp', [(f, f ^ bit) for f in range(lax.axis_size('f...  136 us
    all_gather x4, waiting for transfers between devices, gather_rows(): return lax.all_gather(local, 'seq', axis=0, tiled=True)  75 us
    unnamed x216, local copies, waits for them, and re-layouts  56.8 us
    pallas_call x12, Pallas kernels, weight_terms(): pl.pallas_call(kernel, grid_spec=pltpu.PrefetchScalarGridSpec(num_scalar_...  52.4 us
    pallas_call x30, Pallas kernels, move(): pl.pallas_call(lambda *refs: kernel(*refs[:given], *refs[given + len(firs...  52.1 us
    reduce_scatter x4, waiting for transfers between devices, scatter_rows(): return lax.psum_scatter(partial, 'seq', scatter_dimension=0, tiled=True)  45.9 us
    ppermute x32, starting transfers between devices, beside(): lax.ppermute(value, 'fsdp', [(f, f ^ bit) for f in range(lax.axis_size('f...  35.7 us
    ppermute x15, waiting for transfers between devices, turn(): lax.ppermute(value, 'seq', [(s, (s - 2 * steps) % size) for s in range(si...  31.7 us
  transfers between devices with their start and end apart: 64, of which 29 were waited for; matrix products, arithmetic and copies ran while one was open for 5% of the time, Pallas kernels for 20%

profile of v4, /device:TPU:0, one launch (start us, length us, event | category | flops | bytes accessed | tf_op | source)
XLA Modules:
  0.0 664.2 jit_solution(3321890842495437202)
XLA Ops:
  31.2 13.7 %collective-permute-done.2.refs_3_.refs_2_ = bf16[2,64,896]{2,1,0:T(8,128)(2,1)S(1)} collective-permute-done((bf16[2,64,896]{2,1,0:T(8,128)(2,1)S(1)}, bf16[2,64,896]{2,1,0:T(8,128)(2,1)S(1)}, u32[]{:S(2)}, u32[]{:S(2)}) %collective-permute-start.2) | collective-permute-done | bytes 229408 | tf_op jit(solution)/shard_map/ppermute | solution.py:55
  55.6 17.1 %collective-permute-done.5.refs_3_ = bf16[512,896]{1,0:T(8,128)(2,1)S(1)} collective-permute-done((bf16[512,896]{1,0:T(8,128)(2,1)S(1)}, bf16[512,896]{1,0:T(8,128)(2,1)S(1)}, u32[]{:S(2)}, u32[]{:S(2)}) %collective-permute-start.5) | collective-permute-done | bytes 917536 | tf_op jit(solution)/shard_map/ppermute | solution.py:63
  92.5 19.2 %all-gather.8.cloned.1.call-done.row_ref = bf16[1024,2048]{1,0:T(8,128)(2,1)} async-done(((bf16[128,2048]{1,0:T(8,128)(2,1)}), bf16[1024,2048]{1,0:T(8,128)(2,1)}) %all-gather.8.cloned.1.call-update) | async-done | bytes 4194320 | tf_op jit(solution)/shard_map/all_gather | solution.py:93
  117.2 5.2 fusion.13.refs_0_.refs_1_.refs_2_
  123.1 12.2 %shard_map.227 = (bf16[256,1024]{1,0:T(8,128)(2,1)}, bf16[256,1024]{1,0:T(8,128)(2,1)}, bf16[256,1024]{1,0:T(8,128)(2,1)}, bf16[256,1024]{1,0:T(8,128)(2,1)}, f32[4,1,1024]{2,1,0:T(1,128)}) custom-call(f32[768,1024]{1,0:T(8,128)} %fusion.13.refs_0_.refs_1_.refs_2_, f32[768,1024]{1,0:T(8,128)} %fusion.13.refs_0_.refs_1_.refs_2_, ...), custom_call_target="tpu_custom_call" | custom-call | flops 1073741824 | bytes 6291456 | tf_op jit(solution)/shard_map/pallas_call | solution.py:479
  138.4 4.8 convolution_convert_fusion
  149.2 44.3 %collective-permute-done.17.refs_5_.refs_3_ = bf16[512,2048]{1,0:T(8,128)(2,1)} collective-permute-done((bf16[512,2048]{1,0:T(8,128)(2,1)}, bf16[512,2048]{1,0:T(8,128)(2,1)}, u32[]{:S(2)}, u32[]{:S(2)}) %collective-permute-start.17) | collective-permute-done | bytes 2097184 | tf_op jit(solution)/shard_map/ppermute | solution.py:63
  206.7 18.3 %collective-permute-done.18.refs_4_ = bf16[256,2048]{1,0:T(8,128)(2,1)S(1)} collective-permute-done((bf16[256,2048]{1,0:T(8,128)(2,1)S(1)}, bf16[256,2048]{1,0:T(8,128)(2,1)S(1)}, u32[]{:S(2)}, u32[]{:S(2)}) %collective-permute-start.18) | collective-permute-done | bytes 1048608 | tf_op jit(solution)/shard_map/ppermute | solution.py:63
  226.4 6.9 %shard_map.231 = bf16[4,512,2048]{2,1,0:T(8,128)(2,1)} custom-call(s32[1]{0:T(128)} %constant.175.clone.1.refs_0_, bf16[512,2048]{1,0:T(8,128)(2,1)} %bitcast.12.refs_1_, bf16[512,2048]{1,0:T(8,128)(2,1)} %copy-done.12, bf16[512,2048]{1,0:T(8,128)(2,1)} %collective-permute-done.17.refs_5_.refs_3_, bf16[256,2048]{1,0:T(8,128)(2,1)S(1)} %collective-permute-done.18.refs_4_, ...), custom_call_target="tpu_custom_call" | custom-call | bytes 25165836 | tf_op jit(solution)/shard_map/pallas_call | solution.py:105
  233.2 10.8 %all-gather.10.cloned.1.call-done.x_ref.rows_ref = bf16[1024,2048]{1,0:T(8,128)(2,1)} async-done(((bf16[128,2048]{1,0:T(8,128)(2,1)}), bf16[1024,2048]{1,0:T(8,128)(2,1)}) %all-gather.10.cloned.1.call-update) | async-done | bytes 4194320 | tf_op jit(solution)/shard_map/all_gather | solution.py:93
  244.0 23.1 %shard_map.233 = (f32[1024,1024]{1,0:T(8,128)}, f32[1024,1024]{1,0:T(8,128)}, bf16[1024,1024]{1,0:T(8,128)(2,1)}, bf16[1024,2048]{1,0:T(8,128)(2,1)}) custom-call(bf16[1024,2048]{1,0:T(8,128)(2,1)} %all-gather.10.cloned.1.call-done.x_ref.rows_ref, bf16[2048,2048]{1,0:T(8,128)(2,1)} %bitcast.102, bf16[2048,2048]{1,0:T(8,128)(2,1)} %bitcast.103, ...), custom_call_target="tpu_custom_call" | custom-call | flops 12884901888 | bytes 33554432 | tf_op jit(solution)/shard_map/pallas_call | solution.py:635
  270.2 45.9 %reduce-scatter.7.cloned.1.call-done.refs_0_ = bf16[128,2048]{1,0:T(8,128)(2,1)} async-done(((bf16[1024,2048]{1,0:T(8,128)(2,1)}), bf16[128,2048]{1,0:T(8,128)(2,1)}) %reduce-scatter.7.cloned.1.call-update) | async-done | bytes 524304 | tf_op jit(solution)/shard_map/reduce_scatter | solution.py:97
  320.2 45.0 %all-gather.12.cloned.1.call-done.grads_ref = bf16[1024,2048]{1,0:T(8,128)(2,1)} async-done(((bf16[128,2048]{1,0:T(8,128)(2,1)}), bf16[1024,2048]{1,0:T(8,128)(2,1)}) %all-gather.12.cloned.1.call-update) | async-done | bytes 4194320 | tf_op jit(solution)/shard_map/all_gather | solution.py:93
  365.2 7.7 %fusion.32 = f32[1024,1024]{1,0:T(8,128)S(1)} fusion(bf16[1024,2048]{1,0:T(8,128)(2,1)} %all-gather.12.cloned.1.call-done.grads_ref, bf16[1024,2048]{1,0:T(8,128)(2,1)} %bitcast.109), kind=kOutput, calls=%fused_computation.107 | convolution fusion | flops 4294967296 | bytes 12582912 | tf_op jit(solution)/shard_map/dot_general | solution.py:44
  375.5 13.4 %fusion.10.refs_0_ = bf16[1024,2048]{1,0:T(8,128)(2,1)} fusion(bf16[2048,2048]{1,0:T(8,128)(2,1)} %bitcast.104, bf16[1024,1024]{1,0:T(8,128)(2,1)S(1)} %get-tuple-element.139.grads_ref, bf16[1024,1024]{1,0:T(8,128)(2,1)S(1)} %get-tuple-element.138.grads_ref), kind=kOutput, calls=%fused_computation.16 | convolution fusion | flops 8600420352 | bytes 16777216 | tf_op jit(solution)/shard_map/dot_general | solution.py:44
  400.2 5.7 shard_map.237.refs_0_
  413.6 6.5 collective-permute-done.21.refs_3_.refs_2_
  420.1 4.7 collective-permute-done.20.refs_2_.refs_1_
  424.8 6.7 %shard_map.240.refs_5_.refs_0_ = bf16[4,256,1024]{2,1,0:T(8,128)(2,1)} custom-call(s32[4]{0:T(128)S(1)} %copy-done.95, bf16[1024,2048]{1,0:T(8,128)(2,1)} %all-gather.10.cloned.1.call-done.x_ref.rows_ref, bf16[1024,1024]{1,0:T(8,128)(2,1)} %copy-done.4, bf16[2,256,1024]{2,1,0:T(8,128)(2,1)S(1)} %shard_map.238.refs_0_, ...), custom_call_target="tpu_custom_call" | custom-call | flops 2147483648 | bytes 4194304 | tf_op jit(solution)/shard_map/pallas_call | solution.py:323
  431.5 10.3 %collective-permute-done.23.refs_7_.refs_2_ = bf16[2,256,1024]{2,1,0:T(8,128)(2,1)S(1)} collective-permute-done((bf16[2,256,1024]{2,1,0:T(8,128)(2,1)S(1)}, bf16[2,256,1024]{2,1,0:T(8,128)(2,1)S(1)}, u32[]{:S(2)}, u32[]{:S(2)}) %collective-permute-start.23) | collective-permute-done | bytes 1048608 | tf_op jit(solution)/shard_map/ppermute | solution.py:63
  467.0 4.4 shard_map.244.refs_6_.refs_1_
  471.4 4.7 shard_map.243.refs_5_.refs_0_
  478.7 5.9 collective-permute-done.24.refs_3_
  493.0 6.1 shard_map.251.refs_0_
  506.0 9.6 %collective-permute-done.33.refs_2_ = bf16[2,128,2048]{2,1,0:T(8,128)(2,1)S(1)} collective-permute-done((bf16[2,128,2048]{2,1,0:T(8,128)(2,1)S(1)}, bf16[2,128,2048]{2,1,0:T(8,128)(2,1)S(1)}, u32[]{:S(2)}, u32[]{:S(2)}) %collective-permute-start.33) | collective-permute-done | bytes 1048608 | tf_op jit(solution)/shard_map/ppermute | solution.py:63
  521.1 4.6 fusion.15.refs_0_
  525.6 13.9 %shard_map.250 = bf16[3,256,1024]{2,1,0:T(8,128)(2,1)} custom-call(bf16[256,1024]{1,0:T(8,128)(2,1)} %fusion.15.refs_0_, bf16[256,1024]{1,0:T(8,128)(2,1)} %get-tuple-element.94.refs_1_, bf16[256,1024]{1,0:T(8,128)(2,1)} %get-tuple-element.95.refs_2_, bf16[256,1024]{1,0:T(8,128)(2,1)} %get-tuple-element.96.refs_3_, f32[4,1,1024]{2,1,0:T(1,128)} %get-tuple-element.97.refs_4_, ...), custom_call_target="tpu_custom_call" | custom-call | flops 2684354560 | bytes 6291456 | tf_op jit(solution)/shard_map/pallas_call | solution.py:545
  539.6 10.4 %collective-permute-done.30.refs_1_.refs_3_ = bf16[2,64,2048]{2,1,0:T(8,128)(2,1)} collective-permute-done((bf16[2,64,2048]{2,1,0:T(8,128)(2,1)}, bf16[2,64,2048]{2,1,0:T(8,128)(2,1)}, u32[]{:S(2)}, u32[]{:S(2)}) %collective-permute-start.30) | collective-permute-done | bytes 524320 | tf_op jit(solution)/shard_map/ppermute | solution.py:55
  551.4 7.3 %shard_map.253.refs_0_.grad_ref = bf16[1024,2048]{1,0:T(8,128)(2,1)} custom-call(bf16[768,1024]{1,0:T(8,128)(2,1)S(1)} %bitcast.82, bf16[2048,896]{1,0:T(8,128)(2,1)} %bitcast.100, bf16[2,64,2048]{2,1,0:T(8,128)(2,1)} %collective-permute-done.29.refs_0_.refs_2_, bf16[2,64,2048]{2,1,0:T(8,128)(2,1)} %collective-permute-done.30.refs_1_.refs_3_, ...), custom_call_target="tpu_custom_call" | custom-call | flops 3221225472 | bytes 8912896 | tf_op jit(solution)/shard_map/pallas_call | solution.py:675
  568.4 4.9 shard_map.256.refs_0_.refs_2_
  579.7 7.4 %shard_map.257 = f32[1,2048]{1,0:T(1,128)} custom-call(bf16[1024,2048]{1,0:T(8,128)(2,1)} %shard_map.253.refs_0_.grad_ref, bf16[1024,2048]{1,0:T(8,128)(2,1)} %all-gather.8.cloned.1.call-done.row_ref, f32[1024,1]{1,0:T(8,128)} %copy.63.scale_ref, bf16[4,256,768]{2,1,0:T(8,128)(2,1)} %copy-done.1), custom_call_target="tpu_custom_call" | custom-call | flops 8388608 | bytes 8388608 | tf_op jit(solution)/shard_map/pallas_call | solution.py:589
  621.5 4.2 collective-permute-start.50
  (439 shorter events, 241.2 us)
Async XLA Ops:
  7.2 37.9 %all-gather.6.cloned.1.call-start = ((), (), s32[]{:S(2)}) async-start(), calls=%async_computation.4 | async-start | bytes 1310720 | tf_op jit(solution)/shard_map/all_gather | solution.py:890
  7.9 103.8 %all-gather.8.cloned.1.call-start = ((), (), s32[]{:S(2)}) async-start(), calls=%async_computation.5 | async-start | bytes 4718592 | tf_op jit(solution)/shard_map/all_gather | solution.py:93
  8.0 37.0 %collective-permute-start.8 = (bf16[256,2048]{1,0:T(8,128)(2,1)}, bf16[256,2048]{1,0:T(8,128)(2,1)S(1)}, u32[]{:S(2)}, u32[]{:S(2)}) collective-permute-start(bf16[256,2048]{1,0:T(8,128)(2,1)} %refs_1_.5), channel_id=1, source_target_pairs={{0,8},{8,0},{16,24},{24,16},{1,9},{9,1},{17,25},{25,17},{2,10},{10... | collective-permute-start | bytes 3145736 | tf_op jit(solution)/shard_map/ppermute | solution.py:63
  11.0 34.1 %collective-permute-start.9 = (bf16[256,2048]{1,0:T(8,128)(2,1)}, bf16[256,2048]{1,0:T(8,128)(2,1)S(1)}, u32[]{:S(2)}, u32[]{:S(2)}) collective-permute-start(bf16[256,2048]{1,0:T(8,128)(2,1)} %refs_1_.5), channel_id=1, source_target_pairs={{0,16},{8,24},{16,0},{24,8},{1,17},{9,25},{17,1},{25,9},{2,18},{10... | collective-permute-start | bytes 3145736 | tf_op jit(solution)/shard_map/ppermute | solution.py:63
  46.5 148.2 %reduce-scatter.5.cloned.1.call-start = ((), (), s32[]{:S(2)}) async-start(), calls=%async_computation.6 | async-start | bytes 4718592 | tf_op jit(solution)/shard_map/reduce_scatter | solution.py:97
  76.7 45.6 %collective-permute-start.11 = (bf16[2,64,2048]{2,1,0:T(8,128)(2,1)}, bf16[2,64,2048]{2,1,0:T(8,128)(2,1)S(1)}, u32[]{:S(2)}, u32[]{:S(2)}) collective-permute-start(bf16[2,64,2048]{2,1,0:T(8,128)(2,1)} %get-tuple-element.80), channel_id=1, source_target_pairs={{0,2},{1,3},{2,4},{3,5},{4,6},{5,7},{6,0},{7,1},{8,10},{9,11},{10,... | collective-permute-start | bytes 1572872 | tf_op jit(solution)/shard_map/ppermute | solution.py:55
  77.6 57.7 %collective-permute-start.12 = (bf16[2,64,2048]{2,1,0:T(8,128)(2,1)S(1)}, bf16[2,64,2048]{2,1,0:T(8,128)(2,1)}, u32[]{:S(2)}, u32[]{:S(2)}) collective-permute-start(bf16[2,64,2048]{2,1,0:T(8,128)(2,1)S(1)} %get-tuple-element.82), channel_id=1, source_target_pairs={{0,6},{1,7},{2,0},{3,1},{4,2},{5,3},{6,4},{7,5},{8,14},{9,15},{10,... | collective-permute-start | bytes 1572872 | tf_op jit(solution)/shard_map/ppermute | solution.py:55
  81.0 56.6 %collective-permute-start.13 = (bf16[2,64,2048]{2,1,0:T(8,128)(2,1)S(1)}, bf16[2,64,2048]{2,1,0:T(8,128)(2,1)}, u32[]{:S(2)}, u32[]{:S(2)}) collective-permute-start(bf16[2,64,2048]{2,1,0:T(8,128)(2,1)S(1)} %get-tuple-element.83), channel_id=1, source_target_pairs={{0,4},{1,5},{2,6},{3,7},{4,0},{5,1},{6,2},{7,3},{8,12},{9,13},{10,... | collective-permute-start | bytes 1572872 | tf_op jit(solution)/shard_map/ppermute | solution.py:55
  83.7 53.9 %collective-permute-start.14 = (bf16[128,2048]{1,0:T(8,128)(2,1)}, bf16[128,2048]{1,0:T(8,128)(2,1)S(1)}, u32[]{:S(2)}, u32[]{:S(2)}) collective-permute-start(bf16[128,2048]{1,0:T(8,128)(2,1)} %slice.84), channel_id=1, source_target_pairs={{0,8},{8,0},{16,24},{24,16},{1,9},{9,1},{17,25},{25,17},{2,10},{10... | collective-permute-start | bytes 1572872 | tf_op jit(solution)/shard_map/ppermute | solution.py:63
  84.6 53.1 %collective-permute-start.15 = (bf16[128,2048]{1,0:T(8,128)(2,1)}, bf16[128,2048]{1,0:T(8,128)(2,1)}, u32[]{:S(2)}, u32[]{:S(2)}) collective-permute-start(bf16[128,2048]{1,0:T(8,128)(2,1)} %slice.85), channel_id=1, source_target_pairs={{0,16},{8,24},{16,0},{24,8},{1,17},{9,25},{17,1},{25,9},{2,18},{10... | collective-permute-start | bytes 1572872 | tf_op jit(solution)/shard_map/ppermute | solution.py:63
  143.2 100.7 %all-gather.10.cloned.1.call-start = ((), (), s32[]{:S(2)}) async-start(), calls=%async_computation.7 | async-start | bytes 4718592 | tf_op jit(solution)/shard_map/all_gather | solution.py:93
  146.0 47.5 %collective-permute-start.17 = (bf16[512,2048]{1,0:T(8,128)(2,1)}, bf16[512,2048]{1,0:T(8,128)(2,1)}, u32[]{:S(2)}, u32[]{:S(2)}) collective-permute-start(bf16[512,2048]{1,0:T(8,128)(2,1)} %bitcast.12.refs_1_), channel_id=1, source_target_pairs={{0,16},{8,24},{16,0},{24,8},{1,17},{9,25},{17,1},{25,9},{2,18},{10... | collective-permute-start | bytes 6291464 | tf_op jit(solution)/shard_map/ppermute | solution.py:63
  147.5 47.3 %collective-permute-start.16 = (bf16[512,2048]{1,0:T(8,128)(2,1)}, bf16[512,2048]{1,0:T(8,128)(2,1)S(1)}, u32[]{:S(2)}, u32[]{:S(2)}) collective-permute-start(bf16[512,2048]{1,0:T(8,128)(2,1)} %bitcast.12.refs_1_), channel_id=1, source_target_pairs={{0,8},{8,0},{16,24},{24,16},{1,9},{9,1},{17,25},{25,17},{2,10},{10... | collective-permute-start | bytes 6291464 | tf_op jit(solution)/shard_map/ppermute | solution.py:63
  199.4 116.7 %reduce-scatter.7.cloned.1.call-start = ((), (), s32[]{:S(2)}) async-start(), calls=%async_computation.8 | async-start | bytes 4718592 | tf_op jit(solution)/shard_map/reduce_scatter | solution.py:97
  201.1 23.8 %collective-permute-start.18 = (bf16[256,2048]{1,0:T(8,128)(2,1)S(1)}, bf16[256,2048]{1,0:T(8,128)(2,1)S(1)}, u32[]{:S(2)}, u32[]{:S(2)}) collective-permute-start(bf16[256,2048]{1,0:T(8,128)(2,1)S(1)} %slice.88), channel_id=1, source_target_pairs={{0,8},{8,0},{16,24},{24,16},{1,9},{9,1},{17,25},{25,17},{2,10},{10... | collective-permute-start | bytes 3145736 | tf_op jit(solution)/shard_map/ppermute | solution.py:63
  202.8 23.6 %collective-permute-start.19 = (bf16[256,2048]{1,0:T(8,128)(2,1)S(1)}, bf16[256,2048]{1,0:T(8,128)(2,1)S(1)}, u32[]{:S(2)}, u32[]{:S(2)}) collective-permute-start(bf16[256,2048]{1,0:T(8,128)(2,1)S(1)} %slice.89), channel_id=1, source_target_pairs={{0,16},{8,24},{16,0},{24,8},{1,17},{9,25},{17,1},{25,9},{2,18},{10... | collective-permute-start | bytes 3145736 | tf_op jit(solution)/shard_map/ppermute | solution.py:63
  267.2 98.0 %all-gather.12.cloned.1.call-start = ((), (), s32[]{:S(2)}) async-start(), calls=%async_computation.9 | async-start | bytes 4718592 | tf_op jit(solution)/shard_map/all_gather | solution.py:93
  319.7 127.5 %reduce-scatter.9.cloned.1.call-start = ((), (), s32[]{:S(2)}) async-start(), calls=%async_computation.10 | async-start | bytes 4718592 | tf_op jit(solution)/shard_map/reduce_scatter | solution.py:97
  390.2 130.8 %all-gather.14.cloned.1.call-start = ((), (), s32[]{:S(2)}) async-start(), calls=%async_computation.11 | async-start | bytes 4718592 | tf_op jit(solution)/shard_map/all_gather | solution.py:93
  394.0 26.1 %collective-permute-start.21 = (bf16[2,256,1024]{2,1,0:T(8,128)(2,1)S(1)}, bf16[2,256,1024]{2,1,0:T(8,128)(2,1)S(1)}, u32[]{:S(2)}, u32[]{:S(2)}) collective-permute-start(bf16[2,256,1024]{2,1,0:T(8,128)(2,1)S(1)} %shard_map.236.refs_1_), channel_id=1, source_target_pairs={{0,16},{8,24},{16,0},{24,8},{1,17},{9,25},{17,1},{25,9},{2,18},{10... | collective-permute-start | bytes 3145736 | tf_op jit(solution)/shard_map/ppermute | solution.py:63
  398.7 26.1 %collective-permute-start.20 = (bf16[2,256,1024]{2,1,0:T(8,128)(2,1)S(1)}, bf16[2,256,1024]{2,1,0:T(8,128)(2,1)S(1)}, u32[]{:S(2)}, u32[]{:S(2)}) collective-permute-start(bf16[2,256,1024]{2,1,0:T(8,128)(2,1)S(1)} %shard_map.235.refs_0_), channel_id=1, source_target_pairs={{0,8},{8,0},{16,24},{24,16},{1,9},{9,1},{17,25},{25,17},{2,10},{10... | collective-permute-start | bytes 3145736 | tf_op jit(solution)/shard_map/ppermute | solution.py:63
  409.3 32.6 %collective-permute-start.23 = (bf16[2,256,1024]{2,1,0:T(8,128)(2,1)S(1)}, bf16[2,256,1024]{2,1,0:T(8,128)(2,1)S(1)}, u32[]{:S(2)}, u32[]{:S(2)}) collective-permute-start(bf16[2,256,1024]{2,1,0:T(8,128)(2,1)S(1)} %shard_map.239.refs_1_), channel_id=1, source_target_pairs={{0,16},{8,24},{16,0},{24,8},{1,17},{9,25},{17,1},{25,9},{2,18},{10... | collective-permute-start | bytes 3145736 | tf_op jit(solution)/shard_map/ppermute | solution.py:63
  413.0 33.2 %collective-permute-start.22 = (bf16[2,256,1024]{2,1,0:T(8,128)(2,1)S(1)}, bf16[2,256,1024]{2,1,0:T(8,128)(2,1)S(1)}, u32[]{:S(2)}, u32[]{:S(2)}) collective-permute-start(bf16[2,256,1024]{2,1,0:T(8,128)(2,1)S(1)} %shard_map.238.refs_0_), channel_id=1, source_target_pairs={{0,8},{8,0},{16,24},{24,16},{1,9},{9,1},{17,25},{25,17},{2,10},{10... | collective-permute-start | bytes 3145736 | tf_op jit(solution)/shard_map/ppermute | solution.py:63
  454.6 185.8 %reduce-scatter.11.cloned.1.call-start = ((), (), s32[]{:S(2)}) async-start(), calls=%async_computation.12 | async-start | bytes 4718592 | tf_op jit(solution)/shard_map/reduce_scatter | solution.py:97
  490.0 25.6 %collective-permute-start.33 = (bf16[2,128,2048]{2,1,0:T(8,128)(2,1)S(1)}, bf16[2,128,2048]{2,1,0:T(8,128)(2,1)S(1)}, u32[]{:S(2)}, u32[]{:S(2)}) collective-permute-start(bf16[2,128,2048]{2,1,0:T(8,128)(2,1)S(1)} %copy-done.14), channel_id=1, source_target_pairs={{0,16},{8,24},{16,0},{24,8},{1,17},{9,25},{17,1},{25,9},{2,18},{10... | collective-permute-start | bytes 3145736 | tf_op jit(solution)/shard_map/ppermute | solution.py:63
  491.4 25.4 %collective-permute-start.32 = (bf16[2,128,2048]{2,1,0:T(8,128)(2,1)S(1)}, bf16[2,128,2048]{2,1,0:T(8,128)(2,1)}, u32[]{:S(2)}, u32[]{:S(2)}) collective-permute-start(bf16[2,128,2048]{2,1,0:T(8,128)(2,1)S(1)} %shard_map.243.refs_5_.refs_0_), channel_id=1, source_target_pairs={{0,8},{8,0},{16,24},{24,16},{1,9},{9,1},{17,25},{25,17},{2,10},{10... | collective-permute-start | bytes 3145736 | tf_op jit(solution)/shard_map/ppermute | solution.py:63
  502.8 36.8 %collective-permute-start.29 = (bf16[2,64,2048]{2,1,0:T(8,128)(2,1)}, bf16[2,64,2048]{2,1,0:T(8,128)(2,1)}, u32[]{:S(2)}, u32[]{:S(2)}) collective-permute-start(bf16[2,64,2048]{2,1,0:T(8,128)(2,1)} %get-tuple-element.108.refs_12_.refs_6_), channel_id=1, source_target_pairs={{0,6},{1,7},{2,0},{3,1},{4,2},{5,3},{6,4},{7,5},{8,14},{9,15},{10,... | collective-permute-start | bytes 1572872 | tf_op jit(solution)/shard_map/ppermute | solution.py:55
  503.8 46.2 %collective-permute-start.30 = (bf16[2,64,2048]{2,1,0:T(8,128)(2,1)}, bf16[2,64,2048]{2,1,0:T(8,128)(2,1)}, u32[]{:S(2)}, u32[]{:S(2)}) collective-permute-start(bf16[2,64,2048]{2,1,0:T(8,128)(2,1)} %get-tuple-element.107.refs_11_.refs_5_), channel_id=1, source_target_pairs={{0,4},{1,5},{2,6},{3,7},{4,0},{5,1},{6,2},{7,3},{8,12},{9,13},{10,... | collective-permute-start | bytes 1572872 | tf_op jit(solution)/shard_map/ppermute | solution.py:55
  504.1 46.0 %collective-permute-start.31 = (bf16[2,64,2048]{2,1,0:T(8,128)(2,1)}, bf16[2,64,2048]{2,1,0:T(8,128)(2,1)}, u32[]{:S(2)}, u32[]{:S(2)}) collective-permute-start(bf16[2,64,2048]{2,1,0:T(8,128)(2,1)} %get-tuple-element.106.refs_10_.refs_4_), channel_id=1, source_target_pairs={{0,2},{1,3},{2,4},{3,5},{4,6},{5,7},{6,0},{7,1},{8,10},{9,11},{10,... | collective-permute-start | bytes 1572872 | tf_op jit(solution)/shard_map/ppermute | solution.py:55
  563.7 28.2 %collective-permute-start.41 = (bf16[2,256,768]{2,1,0:T(8,128)(2,1)}, bf16[2,256,768]{2,1,0:T(8,128)(2,1)}, u32[]{:S(2)}, u32[]{:S(2)}) collective-permute-start(bf16[2,256,768]{2,1,0:T(8,128)(2,1)} %shard_map.255.refs_1_), channel_id=1, source_target_pairs={{0,16},{8,24},{16,0},{24,8},{1,17},{9,25},{17,1},{25,9},{2,18},{10... | collective-permute-start | bytes 2359304 | tf_op jit(solution)/shard_map/ppermute | solution.py:63
  567.8 24.1 %collective-permute-start.40 = (bf16[2,256,768]{2,1,0:T(8,128)(2,1)}, bf16[2,256,768]{2,1,0:T(8,128)(2,1)}, u32[]{:S(2)}, u32[]{:S(2)}) collective-permute-start(bf16[2,256,768]{2,1,0:T(8,128)(2,1)} %shard_map.254.refs_0_), channel_id=1, source_target_pairs={{0,8},{8,0},{16,24},{24,16},{1,9},{9,1},{17,25},{25,17},{2,10},{10... | collective-permute-start | bytes 2359304 | tf_op jit(solution)/shard_map/ppermute | solution.py:63
  621.5 22.6 %collective-permute-start.50 = (bf16[2,64,768]{2,1,0:T(8,128)(2,1)}, bf16[2,64,768]{2,1,0:T(8,128)(2,1)}, u32[]{:S(2)}, u32[]{:S(2)}) collective-permute-start(bf16[2,64,768]{2,1,0:T(8,128)(2,1)} %get-tuple-element.123), channel_id=1, source_target_pairs={{0,4},{1,5},{2,6},{3,7},{4,0},{5,1},{6,2},{7,3},{8,12},{9,13},{10,... | collective-permute-start | bytes 589832 | tf_op jit(solution)/shard_map/ppermute | solution.py:55
  (140 other events, 1198.4 us)
Sparse Core Ops, SparseCore 0:
  9.9 34.6 all-gather.5
  46.7 64.9 all-gather.7
  143.4 50.2 reduce-scatter.4
  199.5 44.4 all-gather.9
  267.3 48.7 reduce-scatter.6
  319.8 45.2 all-gather.11
  390.4 48.7 reduce-scatter.8
  454.7 44.9 all-gather.13
  558.8 48.3 reduce-scatter.10

commit v5 on v4

--- a/solution.py
+++ b/solution.py
@@ -344,11 +344,12 @@
     )(blocks, rows, grads, *first)
 
 
-def begin_square(rows, grads, ordered=False, turned=(False, False), first=(), last=()):
+def begin_square(rows, grads, ordered=False, turned=(False, False), first=()):
     if not square():
         rows, grads = rows.T if turned[0] else rows, grads.T if turned[1] else grads
         terms = transposed(rows, grads).astype(BF)
-        return (lax.psum_scatter(terms, "fsdp", scatter_dimension=0, tiled=True),), ()
+        summed = lax.psum_scatter(terms, "fsdp", scatter_dimension=0, tiled=True)
+        return lambda *last: (summed,), ()
     half = rows.shape[0 if turned[0] else 1] // 8
     flip = lax.axis_index("fsdp") if ordered else 0
 
@@ -358,8 +359,12 @@
 
     one = terms([(1, 0), (3, 0)], first)
     two = terms([(2, 1), (3, 1)], first)
-    kept = terms([(2, 0), (1, 1), (0, 0), (0, 1)], (one, two, *last))
-    return (kept, beside(one, 1), beside(two, 2)), (one, two)
+
+    def keep(*last):
+        kept = terms([(2, 0), (1, 1), (0, 0), (0, 1)], (one, two, *last))
+        return kept, beside(one, 1), beside(two, 2)
+
+    return keep, (one, two)
 
 
 def begin_square_of(terms, first=()):
@@ -606,56 +611,105 @@
 def mlp(rows, gate_up_weight, down_full):
     length, width = rows.shape
     hidden_width = down_full.shape[0]
-    tall, block = min(1024, length), min(256, hidden_width)
-    steps = hidden_width // block
-
-    def kernel(x_ref, gate_w, up_w, down_w, gate_ref, up_ref, hidden_ref, out_ref, total):
-        x = x_ref[...]
-        gate, up = dot(x, gate_w[...]), dot(x, up_w[...])
-        hidden = gated(gate, up).astype(BF)
-        gate_ref[...], up_ref[...], hidden_ref[...] = gate, up, hidden
-        terms = dot(hidden, down_w[...])
+    tall, block, wide = min(1024, length), min(256, hidden_width), 512
+    steps, ends = hidden_width // block, width // wide
+
+    def kernel(x_ref, gate_w, up_w, down_w, gate_ref, up_ref, hidden_ref, out_ref, kept):
         step = pl.program_id(1)
 
-        @pl.when(step == 0)
+        @pl.when(step < steps)
         def _():
-            total[...] = terms
-
-        @pl.when((step > 0) & (step < steps - 1))
+            x = x_ref[...]
+            gate, up = dot(x, gate_w[...]), dot(x, up_w[...])
+            hidden = gated(gate, up).astype(BF)
+            gate_ref[...], up_ref[...], hidden_ref[...] = gate, up, hidden
+            kept[jnp.minimum(step, steps - 1)] = hidden
+
+        @pl.when(step >= steps)
         def _():
-            total[...] += terms
-
-        @pl.when(step == steps - 1)
-        def _():
-            out_ref[...] = (total[...] + terms).astype(BF)
-
-    part = pl.BlockSpec((tall, block), lambda i, j: (i, j))
-    whole = pl.BlockSpec((tall, width), lambda i, j: (i, 0))
-    wide = jax.ShapeDtypeStruct((length, hidden_width), F32)
+            hidden = jnp.concatenate([kept[i] for i in range(steps)], axis=1)
+            out_ref[...] = dot(hidden, down_w[...]).astype(BF)
+
+    early = lambda j: jnp.minimum(j, steps - 1)
+    late = lambda j: jnp.maximum(j - steps, 0)
+    part = pl.BlockSpec((tall, block), lambda i, j: (i, early(j)))
+    full = jax.ShapeDtypeStruct((length, hidden_width), F32)
     return pl.pallas_call(
         kernel,
-        grid=(length // tall, steps),
+        grid=(length // tall, steps + ends),
         out_shape=(
-            wide,
-            wide,
+            full,
+            full,
             jax.ShapeDtypeStruct((length, hidden_width), BF),
             jax.ShapeDtypeStruct((length, width), BF),
         ),
         in_specs=[
-            whole,
-            pl.BlockSpec((width, block), lambda i, j: (0, j)),
-            pl.BlockSpec((width, block), lambda i, j: (0, j + steps)),
-            pl.BlockSpec((block, width), lambda i, j: (j, 0)),
+            pl.BlockSpec((tall, width), lambda i, j: (i, 0)),
+            pl.BlockSpec((width, block), lambda i, j: (0, early(j))),
+            pl.BlockSpec((width, block), lambda i, j: (0, early(j) + steps)),
+            pl.BlockSpec((hidden_width, wide), lambda i, j: (0, late(j))),
         ],
-        out_specs=(part, part, part, whole),
-        scratch_shapes=[pltpu.VMEM((tall, width), F32)],
-        compiler_params=pltpu.CompilerParams(vmem_limit_bytes=60 * 2**20),
+        out_specs=(part, part, part, pl.BlockSpec((tall, wide), lambda i, j: (i, late(j)))),
+        scratch_shapes=[pltpu.VMEM((steps, tall, block), BF)],
+        compiler_params=pltpu.CompilerParams(vmem_limit_bytes=56 * 2**20),
         cost_estimate=pl.CostEstimate(
             flops=6 * length * width * hidden_width,
             bytes_accessed=6 * width * hidden_width + 4 * length * (width + 3 * hidden_width),
             transcendentals=length * hidden_width,
         ),
     )(rows, gate_up_weight, gate_up_weight, down_full)
+
+
+def mlp_back(grads, gate, up, gate_up_weight, down_full):
+    length, width = grads.shape
+    hidden_width = down_full.shape[0]
+    tall, block, wide = min(1024, length), min(256, hidden_width), 512
+    steps, ends = hidden_width // block, width // wide
+
+    def kernel(g_ref, gate_ref, up_ref, down_w, both_w, dgate, dup, out_ref, kept):
+        step = pl.program_id(1)
+
+        @pl.when(step < steps)
+        def _():
+            gate, up = gate_ref[...], up_ref[...]
+            share = jax.nn.sigmoid(gate)
+            grad_hidden = against(g_ref[...], down_w[...])
+            grad_gate = (grad_hidden * up * (share + gate * share * (1.0 - share))).astype(BF)
+            grad_up = (grad_hidden * (gate * share)).astype(BF)
+            dgate[...], dup[...] = grad_gate, grad_up
+            at = jnp.minimum(step, steps - 1)
+            kept[at] = grad_gate
+            kept[at + steps] = grad_up
+
+        @pl.when(step >= steps)
+        def _():
+            both = jnp.concatenate([kept[i] for i in range(2 * steps)], axis=1)
+            out_ref[...] = against(both, both_w[...]).astype(BF)
+
+    early = lambda j: jnp.minimum(j, steps - 1)
+    late = lambda j: jnp.maximum(j - steps, 0)
+    part = pl.BlockSpec((tall, block), lambda i, j: (i, early(j)))
+    narrow = jax.ShapeDtypeStruct((length, hidden_width), BF)
+    return pl.pallas_call(
+        kernel,
+        grid=(length // tall, steps + ends),
+        out_shape=(narrow, narrow, jax.ShapeDtypeStruct((length, width), BF)),
+        in_specs=[
+            pl.BlockSpec((tall, width), lambda i, j: (i, 0)),
+            part,
+            part,
+            pl.BlockSpec((block, width), lambda i, j: (early(j), 0)),
+            pl.BlockSpec((wide, 2 * hidden_width), lambda i, j: (late(j), 0)),
+        ],
+        out_specs=(part, part, pl.BlockSpec((tall, wide), lambda i, j: (i, late(j)))),
+        scratch_shapes=[pltpu.VMEM((2 * steps, tall, block), BF)],
+        compiler_params=pltpu.CompilerParams(vmem_limit_bytes=56 * 2**20),
+        cost_estimate=pl.CostEstimate(
+            flops=6 * length * width * hidden_width,
+            bytes_accessed=6 * width * hidden_width + 4 * length * (width + 3 * hidden_width),
+            transcendentals=length * hidden_width,
+        ),
+    )(grads, gate, up, down_full, gate_up_weight)
 
 
 def rows_back(columns, weight, first=()):
@@ -811,7 +865,7 @@
     )
 
 
-def sum_over_chips(values):
+def sum_to_owners(values):
     chip, core, chips = place()
     shards, width = lax.axis_size("fsdp"), values.shape[1]
     own = lax.axis_index("fsdp")
@@ -828,19 +882,10 @@
             [(f, (f + step) % shards) for f in range(shards)],
         )
     total = jnp.moveaxis(total, 1, 0)
-    return share(total, core) + swap(share(total, 1 - core))
-
-
-def sum_to_owners(values, first):
-    chip, core, chips = place()
-    values = tie(values, *first)
-
-    def share(step):
-        return lax.dynamic_index_in_dim(values, (chip + step) % chips, 0, keepdims=False)
-
-    total = share(0)
+    values = share(total, core) + swap(share(total, 1 - core))
+    total = share(values, chip)
     for step in order(chips):
-        total += turn(share(step), -step)
+        total += turn(share(values, (chip + step) % chips), -step)
     return total
 
 
@@ -943,16 +988,13 @@
         (2.0 / count * keep_mask)[:, None],
     )
     grad_branch = gather_rows(grad_branch)
-    unused, gate_pull = jax.vjp(gated, gate_value, up_value)
-    grad_gate, grad_upward = gate_pull(against(grad_branch, down_full))
-    grad_gate, grad_upward = grad_gate.astype(BF), grad_upward.astype(BF)
-    grad_normed_sum = against(
-        jnp.concatenate([grad_gate, grad_upward], axis=1), gate_up_weight
-    ).astype(BF)
-    gate_back, unused = begin_square(normed_two, grad_gate, first=(grad_normed_sum,))
-    up_back, unused = begin_square(
-        normed_two, grad_upward, first=(gate_back[0],), last=gate_back[1:]
-    )
+    grad_gate, grad_upward, grad_normed_sum = mlp_back(
+        grad_branch, gate_value, up_value, gate_up_weight, down_full
+    )
+    gate_keep, unused = begin_square(normed_two, grad_gate, first=(grad_normed_sum,))
+    gate_back = gate_keep()
+    up_keep, unused = begin_square(normed_two, grad_upward, first=gate_back[:1])
+    up_back = up_keep(*gate_back[1:])
     grad_after, grad_out, second_gain_grad = after_third_sum(
         scatter_rows(grad_normed_sum),
         after_attention,
@@ -964,15 +1006,14 @@
 
     grad_out = gather_rows(grad_out)
     up_back = second_square(*up_back)
-    down_back, down_sent = begin_square(
-        hidden, grad_branch, ordered=True, first=(gate_back[0],), last=up_back[3:]
-    )
+    down_keep, down_sent = begin_square(hidden, grad_branch, ordered=True, first=gate_back[:1])
+    down_back = down_keep()
     gate_up_pairs = pairs_of(
         *rows_to(
             jnp.concatenate(
                 [
                     finish_square(*gate_back, first=down_sent),
-                    finish_square(*up_back),
+                    finish_square(*up_back, first=down_back[:1]),
                 ],
                 axis=1,
             )
@@ -997,19 +1038,20 @@
     grad_normed_sum = rows_back(
         qkv_grad, attention_in, (*gate_up_shares[1:], *down_back[3:])
     )
-    qkv_begun, unused = begin_square(
+    qkv_keep, qkv_sent = begin_square(
         normed, qkv_grad, turned=(False, True), first=(grad_normed_sum,)
     )
-    first_gain_grad = gain_terms(grad_normed_sum, tokens_all, steady, qkv_begun[:1])
+    first_gain_grad = gain_terms(grad_normed_sum, tokens_all, steady, qkv_sent)
+    qkv_begun = qkv_keep(first_gain_grad)
     output_grad = matmul(mixed, grad_out).astype(BF)
     if aligned and square():
         output_begun = begin_square_of(output_grad, first=qkv_begun[:1])
-        qkv_back = second_square(*qkv_begun, first=(*output_begun, first_gain_grad))
+        qkv_back = second_square(*qkv_begun, first=output_begun[:1])
         output_back = second_square(*output_begun)
         output_sum = finish_square(*output_back, kind=F32)
     else:
-        qkv_back = second_square(*qkv_begun, first=(first_gain_grad,))
-        output_back = ()
+        qkv_back = second_square(*qkv_begun)
+        output_begun = ()
         output_sum = lax.psum_scatter(
             lax.dynamic_update_slice_in_dim(
                 jnp.zeros((width, width), BF), output_grad, own * hw, 0
@@ -1019,7 +1061,7 @@
             tiled=True,
         ).astype(F32)
     devices = shards * groups
-    sums = sum_over_chips(
+    sums = sum_to_owners(
         jnp.concatenate(
             [
                 relative_blocks(first_gain_grad).reshape(devices, weight_rows),
@@ -1030,19 +1072,21 @@
         )
     )
     qkv_pairs = pairs_of(
-        *rows_to(finish_square(*qkv_back)), first=(sums, *output_back[3:])
+        *rows_to(finish_square(*qkv_back)), first=(sums, *output_begun[1:])
     )
     qkv_shares = exchange(qkv_pairs)
-    query_sum, key_sum, value_sum = columns_to(qkv_shares, head_blocks, [hw, hw, hw])
     gate_sum, up_sum = columns_to(
-        gate_up_shares, shards, [hidden_width, hidden_width], first=qkv_pairs[:1]
-    )
-    down_sum = finish_square(*down_back, kind=F32, first=qkv_pairs[:1])
+        gate_up_shares, shards, [hidden_width, hidden_width], first=qkv_back[3:4]
+    )
+    down_sum = finish_square(*down_back, kind=F32, first=qkv_back[3:4])
     grad_inputs = after_last_sum(
         scatter_rows(grad_normed_sum), own_tokens, first_gain, grad_after
     )
-    sums = sum_to_owners(
-        sums, (*qkv_shares[1:], gate_sum, down_sum, grad_inputs, output_sum)
+    query_sum, key_sum, value_sum = columns_to(
+        qkv_shares,
+        head_blocks,
+        [hw, hw, hw],
+        first=(gate_sum, down_sum, grad_inputs, output_sum),
     )
     output_shape = (sequences, local_rows, width)
     return (

time: 670 us -> 655 us (0.978)
  Pallas kernels: 168 us -> 187 us
  matrix products: 36.9 us -> 18.4 us
  local copies, waits for them, and re-layouts: 67.7 us -> 59.6 us
    dot_general x3 -> x1, matrix products: 25.7 us -> 4.56 us  [against(): lax.dot_general(left_side, right_side, (((1,), (1,)), ((), ())), preferre...]
    pallas_call x1 -> x2, Pallas kernels: 23.1 us -> 42.9 us  [the longest x1 22.3 us: mlp_back(): pl.pallas_call(kernel, grid=(length // tall, steps + ends), out_shape=(na...]
    ppermute x32, waiting for transfers between devices: 136 us -> 126 us  [beside(): lax.ppermute(value, 'fsdp', [(f, f ^ bit) for f in range(lax.axis_size('f...]
    unnamed x216 -> x205, local copies, waits for them, and re-layouts: 56.8 us -> 50.2 us
  transfers between devices with their start and end apart: 64 -> 64, of which waited for: 29 -> 26; matrix products, arithmetic and copies ran while one was open for 5% -> 6% of each run, Pallas kernels for 20% -> 20%
where the time goes in v5:
time: 655 us; the launch traced here: 649 us
  waiting for transfers between devices  290 us (44%)
  Pallas kernels  187 us (29%)
  starting transfers between devices  61.3 us (9%)
  local copies, waits for them, and re-layouts  59.6 us (9%)
  matrix products  18.4 us (3%)
  between operations  18.2 us (3%)
  other arithmetic  14.8 us (2%)
    ppermute x32, waiting for transfers between devices, beside(): lax.ppermute(value, 'fsdp', [(f, f ^ bit) for f in range(lax.axis_size('f...  126 us
    all_gather x4, waiting for transfers between devices, gather_rows(): return lax.all_gather(local, 'seq', axis=0, tiled=True)  74.1 us
    pallas_call x30, Pallas kernels, move(): pl.pallas_call(lambda *refs: kernel(*refs[:given], *refs[given + len(firs...  52 us
    pallas_call x12, Pallas kernels, weight_terms(): pl.pallas_call(kernel, grid_spec=pltpu.PrefetchScalarGridSpec(num_scalar_...  51.7 us
    unnamed x205, local copies, waits for them, and re-layouts  50.2 us
    reduce_scatter x4, waiting for transfers between devices, scatter_rows(): return lax.psum_scatter(partial, 'seq', scatter_dimension=0, tiled=True)  45.9 us
    ppermute x32, starting transfers between devices, beside(): lax.ppermute(value, 'fsdp', [(f, f ^ bit) for f in range(lax.axis_size('f...  37.1 us
    ppermute x15, waiting for transfers between devices, turn(): lax.ppermute(value, 'seq', [(s, (s - 2 * steps) % size) for s in range(si...  36.3 us
  transfers between devices with their start and end apart: 64, of which 26 were waited for; matrix products, arithmetic and copies ran while one was open for 6% of the time, Pallas kernels for 20%

profile of v5, /device:TPU:0, one launch (start us, length us, event | category | flops | bytes accessed | tf_op | source)
XLA Modules:
  0.0 649.3 jit_solution(10526075178944867753)
XLA Ops:
  28.0 4.2 collective-permute-done.1.refs_2_.refs_1_
  32.2 13.7 %collective-permute-done.2.refs_3_.refs_2_ = bf16[2,64,896]{2,1,0:T(8,128)(2,1)S(1)} collective-permute-done((bf16[2,64,896]{2,1,0:T(8,128)(2,1)S(1)}, bf16[2,64,896]{2,1,0:T(8,128)(2,1)S(1)}, u32[]{:S(2)}, u32[]{:S(2)}) %collective-permute-start.2) | collective-permute-done | bytes 229408 | tf_op jit(solution)/shard_map/ppermute | solution.py:55
  56.5 17.1 %collective-permute-done.5.refs_3_ = bf16[512,896]{1,0:T(8,128)(2,1)S(1)} collective-permute-done((bf16[512,896]{1,0:T(8,128)(2,1)S(1)}, bf16[512,896]{1,0:T(8,128)(2,1)S(1)}, u32[]{:S(2)}, u32[]{:S(2)}) %collective-permute-start.5) | collective-permute-done | bytes 917536 | tf_op jit(solution)/shard_map/ppermute | solution.py:63
  93.5 17.8 %all-gather.8.cloned.1.call-done.row_ref = bf16[1024,2048]{1,0:T(8,128)(2,1)} async-done(((bf16[128,2048]{1,0:T(8,128)(2,1)}), bf16[1024,2048]{1,0:T(8,128)(2,1)}) %all-gather.8.cloned.1.call-update) | async-done | bytes 4194320 | tf_op jit(solution)/shard_map/all_gather | solution.py:93
  116.8 5.2 fusion.3.refs_0_.refs_1_.refs_2_
  122.8 12.2 %shard_map.227 = (bf16[256,1024]{1,0:T(8,128)(2,1)}, bf16[256,1024]{1,0:T(8,128)(2,1)}, bf16[256,1024]{1,0:T(8,128)(2,1)}, bf16[256,1024]{1,0:T(8,128)(2,1)}, f32[4,1,1024]{2,1,0:T(1,128)}) custom-call(f32[768,1024]{1,0:T(8,128)} %fusion.3.refs_0_.refs_1_.refs_2_, f32[768,1024]{1,0:T(8,128)} %fusion.3.refs_0_.refs_1_.refs_2_, ...), custom_call_target="tpu_custom_call" | custom-call | flops 1073741824 | bytes 6291456 | tf_op jit(solution)/shard_map/pallas_call | solution.py:484
  138.4 4.8 convolution_convert_fusion
  149.2 44.5 %collective-permute-done.17.refs_5_.refs_3_ = bf16[512,2048]{1,0:T(8,128)(2,1)} collective-permute-done((bf16[512,2048]{1,0:T(8,128)(2,1)}, bf16[512,2048]{1,0:T(8,128)(2,1)}, u32[]{:S(2)}, u32[]{:S(2)}) %collective-permute-start.17) | collective-permute-done | bytes 2097184 | tf_op jit(solution)/shard_map/ppermute | solution.py:63
  206.9 18.1 %collective-permute-done.18.refs_4_ = bf16[256,2048]{1,0:T(8,128)(2,1)S(1)} collective-permute-done((bf16[256,2048]{1,0:T(8,128)(2,1)S(1)}, bf16[256,2048]{1,0:T(8,128)(2,1)S(1)}, u32[]{:S(2)}, u32[]{:S(2)}) %collective-permute-start.18) | collective-permute-done | bytes 1048608 | tf_op jit(solution)/shard_map/ppermute | solution.py:63
  226.3 6.9 %shard_map.231 = bf16[4,512,2048]{2,1,0:T(8,128)(2,1)} custom-call(s32[1]{0:T(128)} %constant.170.clone.1.refs_0_, bf16[512,2048]{1,0:T(8,128)(2,1)} %bitcast.12.refs_1_, bf16[512,2048]{1,0:T(8,128)(2,1)} %copy-done.11, bf16[512,2048]{1,0:T(8,128)(2,1)} %collective-permute-done.17.refs_5_.refs_3_, bf16[256,2048]{1,0:T(8,128)(2,1)S(1)} %collective-permute-done.18.refs_4_, ...), custom_call_target="tpu_custom_call" | custom-call | bytes 25165836 | tf_op jit(solution)/shard_map/pallas_call | solution.py:105
  233.2 10.9 %all-gather.10.cloned.1.call-done.x_ref.rows_ref = bf16[1024,2048]{1,0:T(8,128)(2,1)} async-done(((bf16[128,2048]{1,0:T(8,128)(2,1)}), bf16[1024,2048]{1,0:T(8,128)(2,1)}) %all-gather.10.cloned.1.call-update) | async-done | bytes 4194320 | tf_op jit(solution)/shard_map/all_gather | solution.py:93
  244.1 20.7 %shard_map.233 = (f32[1024,1024]{1,0:T(8,128)}, f32[1024,1024]{1,0:T(8,128)}, bf16[1024,1024]{1,0:T(8,128)(2,1)}, bf16[1024,2048]{1,0:T(8,128)(2,1)}) custom-call(bf16[1024,2048]{1,0:T(8,128)(2,1)} %all-gather.10.cloned.1.call-done.x_ref.rows_ref, bf16[2048,2048]{1,0:T(8,128)(2,1)} %bitcast.103, bf16[2048,2048]{1,0:T(8,128)(2,1)} %bitcast.104, ...), custom_call_target="tpu_custom_call" | custom-call | flops 12884901888 | bytes 33554432 | tf_op jit(solution)/shard_map/pallas_call | solution.py:637
  267.8 45.9 %reduce-scatter.7.cloned.1.call-done.refs_0_ = bf16[128,2048]{1,0:T(8,128)(2,1)} async-done(((bf16[1024,2048]{1,0:T(8,128)(2,1)}), bf16[128,2048]{1,0:T(8,128)(2,1)}) %reduce-scatter.7.cloned.1.call-update) | async-done | bytes 524304 | tf_op jit(solution)/shard_map/reduce_scatter | solution.py:97
  317.4 45.4 %all-gather.12.cloned.1.call-done.g_ref.grads_ref = bf16[1024,2048]{1,0:T(8,128)(2,1)} async-done(((bf16[128,2048]{1,0:T(8,128)(2,1)}), bf16[1024,2048]{1,0:T(8,128)(2,1)}) %all-gather.12.cloned.1.call-update) | async-done | bytes 4194320 | tf_op jit(solution)/shard_map/all_gather | solution.py:93
  362.8 22.3 %shard_map.235 = (bf16[1024,1024]{1,0:T(8,128)(2,1)}, bf16[1024,1024]{1,0:T(8,128)(2,1)}, bf16[1024,2048]{1,0:T(8,128)(2,1)}) custom-call(bf16[1024,2048]{1,0:T(8,128)(2,1)} %all-gather.12.cloned.1.call-done.g_ref.grads_ref, f32[1024,1024]{1,0:T(8,128)} %get-tuple-element.93.gate_ref, f32[1024,1024]{1,0:T(8,128)} %get-tuple-element.94.up_ref, ...), custom_call_target="tpu_custom_call" | custom-call | flops 12884901888 | bytes 33554432 | tf_op jit(solution)/shard_map/pallas_call | solution.py:693
  396.0 5.7 shard_map.238.refs_0_
  409.4 6.5 collective-permute-done.21.refs_3_.refs_2_
  415.9 4.7 collective-permute-done.20.refs_2_.refs_1_
  420.5 6.7 %shard_map.241.refs_5_.refs_0_ = bf16[4,256,1024]{2,1,0:T(8,128)(2,1)} custom-call(s32[4]{0:T(128)S(1)} %copy-done.94, bf16[1024,2048]{1,0:T(8,128)(2,1)} %all-gather.10.cloned.1.call-done.x_ref.rows_ref, bf16[1024,1024]{1,0:T(8,128)(2,1)} %get-tuple-element.97.grads_ref, bf16[2,256,1024]{2,1,0:T(8,128)(2,1)S(1)} %shard_map.239.refs_0_, ...), custom_call_target="tpu_custom_call" | custom-call | flops 2147483648 | bytes 4194304 | tf_op jit(solution)/shard_map/pallas_call | solution.py:323
  427.2 10.4 %collective-permute-done.23.refs_7_.refs_2_ = bf16[2,256,1024]{2,1,0:T(8,128)(2,1)S(1)} collective-permute-done((bf16[2,256,1024]{2,1,0:T(8,128)(2,1)S(1)}, bf16[2,256,1024]{2,1,0:T(8,128)(2,1)S(1)}, u32[]{:S(2)}, u32[]{:S(2)}) %collective-permute-start.23) | collective-permute-done | bytes 1048608 | tf_op jit(solution)/shard_map/ppermute | solution.py:63
  459.9 4.4 shard_map.245.refs_6_.refs_1_
  464.3 4.4 shard_map.244.refs_5_.refs_0_
  468.6 6.2 shard_map.248.refs_5_.refs_0_
  489.2 18.2 %collective-permute-done.33.refs_2_ = bf16[2,128,2048]{2,1,0:T(8,128)(2,1)S(1)} collective-permute-done((bf16[2,128,2048]{2,1,0:T(8,128)(2,1)S(1)}, bf16[2,128,2048]{2,1,0:T(8,128)(2,1)S(1)}, u32[]{:S(2)}, u32[]{:S(2)}) %collective-permute-start.33) | collective-permute-done | bytes 1048608 | tf_op jit(solution)/shard_map/ppermute | solution.py:63
  514.7 4.6 fusion.5.refs_0_
  519.3 14.0 %shard_map.252 = bf16[3,256,1024]{2,1,0:T(8,128)(2,1)} custom-call(bf16[256,1024]{1,0:T(8,128)(2,1)} %fusion.5.refs_0_, bf16[256,1024]{1,0:T(8,128)(2,1)} %get-tuple-element.100.refs_1_, bf16[256,1024]{1,0:T(8,128)(2,1)} %get-tuple-element.101.refs_2_, bf16[256,1024]{1,0:T(8,128)(2,1)} %get-tuple-element.102.refs_3_, ...), custom_call_target="tpu_custom_call" | custom-call | flops 2684354560 | bytes 6291456 | tf_op jit(solution)/shard_map/pallas_call | solution.py:550
  533.3 5.8 collective-permute-done.30.refs_1_.refs_3_
  540.7 7.3 %shard_map.254.refs_0_.grad_ref = bf16[1024,2048]{1,0:T(8,128)(2,1)} custom-call(bf16[768,1024]{1,0:T(8,128)(2,1)S(1)} %bitcast.80, bf16[2048,896]{1,0:T(8,128)(2,1)} %bitcast.101, bf16[2,64,2048]{2,1,0:T(8,128)(2,1)S(1)} %collective-permute-done.29.refs_0_.refs_2_, bf16[2,64,2048]{2,1,0:T(8,128)(2,1)S(1)} %collective-permute-done.30.refs_1_.refs_3_, ...), custom_call_target="tpu_custom_call" | custom-call | flops 3221225472 | bytes 8912896 | tf_op jit(solution)/shard_map/pallas_call | solution.py:729
  562.9 7.3 %shard_map.257 = f32[1,2048]{1,0:T(1,128)} custom-call(bf16[1024,2048]{1,0:T(8,128)(2,1)} %shard_map.254.refs_0_.grad_ref, bf16[1024,2048]{1,0:T(8,128)(2,1)} %all-gather.8.cloned.1.call-done.row_ref, f32[1024,1]{1,0:T(8,128)} %copy.52.scale_ref, bf16[2,256,768]{2,1,0:T(8,128)(2,1)} %shard_map.255.refs_0_, bf16[2,256,768]{2,1,0:T(8,128)(2,1)} %shard_map.256.refs_1_), custom_call_target="tpu_custom_call" | custom-call | flops 8388608 | bytes 8388608 | tf_op jit(solution)/shard_map/pallas_call | solution.py:594
  571.0 4.6 shard_map.259.refs_2_.refs_0_
  589.7 5.4 collective-permute-done.36
  609.1 4.5 collective-permute-done.42
  (423 shorter events, 221.1 us)
Async XLA Ops:
  7.2 38.8 %all-gather.6.cloned.1.call-start = ((), (), s32[]{:S(2)}) async-start(), calls=%async_computation.4 | async-start | bytes 1310720 | tf_op jit(solution)/shard_map/all_gather | solution.py:935
  7.9 103.4 %all-gather.8.cloned.1.call-start = ((), (), s32[]{:S(2)}) async-start(), calls=%async_computation.5 | async-start | bytes 4718592 | tf_op jit(solution)/shard_map/all_gather | solution.py:93
  8.0 38.0 %collective-permute-start.8 = (bf16[256,2048]{1,0:T(8,128)(2,1)}, bf16[256,2048]{1,0:T(8,128)(2,1)S(1)}, u32[]{:S(2)}, u32[]{:S(2)}) collective-permute-start(bf16[256,2048]{1,0:T(8,128)(2,1)} %refs_1_.5), channel_id=1, source_target_pairs={{0,8},{8,0},{16,24},{24,16},{1,9},{9,1},{17,25},{25,17},{2,10},{10... | collective-permute-start | bytes 3145736 | tf_op jit(solution)/shard_map/ppermute | solution.py:63
  11.0 35.0 %collective-permute-start.9 = (bf16[256,2048]{1,0:T(8,128)(2,1)}, bf16[256,2048]{1,0:T(8,128)(2,1)S(1)}, u32[]{:S(2)}, u32[]{:S(2)}) collective-permute-start(bf16[256,2048]{1,0:T(8,128)(2,1)} %refs_1_.5), channel_id=1, source_target_pairs={{0,16},{8,24},{16,0},{24,8},{1,17},{9,25},{17,1},{25,9},{2,18},{10... | collective-permute-start | bytes 3145736 | tf_op jit(solution)/shard_map/ppermute | solution.py:63
  47.4 147.3 %reduce-scatter.5.cloned.1.call-start = ((), (), s32[]{:S(2)}) async-start(), calls=%async_computation.6 | async-start | bytes 4718592 | tf_op jit(solution)/shard_map/reduce_scatter | solution.py:97
  78.0 44.0 %collective-permute-start.11 = (bf16[2,64,2048]{2,1,0:T(8,128)(2,1)}, bf16[2,64,2048]{2,1,0:T(8,128)(2,1)S(1)}, u32[]{:S(2)}, u32[]{:S(2)}) collective-permute-start(bf16[2,64,2048]{2,1,0:T(8,128)(2,1)} %get-tuple-element.83), channel_id=1, source_target_pairs={{0,2},{1,3},{2,4},{3,5},{4,6},{5,7},{6,0},{7,1},{8,10},{9,11},{10,... | collective-permute-start | bytes 1572872 | tf_op jit(solution)/shard_map/ppermute | solution.py:55
  78.8 56.2 %collective-permute-start.12 = (bf16[2,64,2048]{2,1,0:T(8,128)(2,1)}, bf16[2,64,2048]{2,1,0:T(8,128)(2,1)}, u32[]{:S(2)}, u32[]{:S(2)}) collective-permute-start(bf16[2,64,2048]{2,1,0:T(8,128)(2,1)} %get-tuple-element.85), channel_id=1, source_target_pairs={{0,6},{1,7},{2,0},{3,1},{4,2},{5,3},{6,4},{7,5},{8,14},{9,15},{10,... | collective-permute-start | bytes 1572872 | tf_op jit(solution)/shard_map/ppermute | solution.py:55
  81.9 55.7 %collective-permute-start.13 = (bf16[2,64,2048]{2,1,0:T(8,128)(2,1)}, bf16[2,64,2048]{2,1,0:T(8,128)(2,1)}, u32[]{:S(2)}, u32[]{:S(2)}) collective-permute-start(bf16[2,64,2048]{2,1,0:T(8,128)(2,1)} %get-tuple-element.86), channel_id=1, source_target_pairs={{0,4},{1,5},{2,6},{3,7},{4,0},{5,1},{6,2},{7,3},{8,12},{9,13},{10,... | collective-permute-start | bytes 1572872 | tf_op jit(solution)/shard_map/ppermute | solution.py:55
  84.6 53.0 %collective-permute-start.14 = (bf16[128,2048]{1,0:T(8,128)(2,1)}, bf16[128,2048]{1,0:T(8,128)(2,1)S(1)}, u32[]{:S(2)}, u32[]{:S(2)}) collective-permute-start(bf16[128,2048]{1,0:T(8,128)(2,1)} %slice.84), channel_id=1, source_target_pairs={{0,8},{8,0},{16,24},{24,16},{1,9},{9,1},{17,25},{25,17},{2,10},{10... | collective-permute-start | bytes 1572872 | tf_op jit(solution)/shard_map/ppermute | solution.py:63
  85.5 52.1 %collective-permute-start.15 = (bf16[128,2048]{1,0:T(8,128)(2,1)}, bf16[128,2048]{1,0:T(8,128)(2,1)}, u32[]{:S(2)}, u32[]{:S(2)}) collective-permute-start(bf16[128,2048]{1,0:T(8,128)(2,1)} %slice.85), channel_id=1, source_target_pairs={{0,16},{8,24},{16,0},{24,8},{1,17},{9,25},{17,1},{25,9},{2,18},{10... | collective-permute-start | bytes 1572872 | tf_op jit(solution)/shard_map/ppermute | solution.py:63
  143.3 100.9 %all-gather.10.cloned.1.call-start = ((), (), s32[]{:S(2)}) async-start(), calls=%async_computation.7 | async-start | bytes 4718592 | tf_op jit(solution)/shard_map/all_gather | solution.py:93
  146.0 47.7 %collective-permute-start.17 = (bf16[512,2048]{1,0:T(8,128)(2,1)}, bf16[512,2048]{1,0:T(8,128)(2,1)}, u32[]{:S(2)}, u32[]{:S(2)}) collective-permute-start(bf16[512,2048]{1,0:T(8,128)(2,1)} %bitcast.12.refs_1_), channel_id=1, source_target_pairs={{0,16},{8,24},{16,0},{24,8},{1,17},{9,25},{17,1},{25,9},{2,18},{10... | collective-permute-start | bytes 6291464 | tf_op jit(solution)/shard_map/ppermute | solution.py:63
  147.5 47.1 %collective-permute-start.16 = (bf16[512,2048]{1,0:T(8,128)(2,1)}, bf16[512,2048]{1,0:T(8,128)(2,1)S(1)}, u32[]{:S(2)}, u32[]{:S(2)}) collective-permute-start(bf16[512,2048]{1,0:T(8,128)(2,1)} %bitcast.12.refs_1_), channel_id=1, source_target_pairs={{0,8},{8,0},{16,24},{24,16},{1,9},{9,1},{17,25},{25,17},{2,10},{10... | collective-permute-start | bytes 6291464 | tf_op jit(solution)/shard_map/ppermute | solution.py:63
  199.3 114.4 %reduce-scatter.7.cloned.1.call-start = ((), (), s32[]{:S(2)}) async-start(), calls=%async_computation.8 | async-start | bytes 4718592 | tf_op jit(solution)/shard_map/reduce_scatter | solution.py:97
  201.3 23.7 %collective-permute-start.18 = (bf16[256,2048]{1,0:T(8,128)(2,1)S(1)}, bf16[256,2048]{1,0:T(8,128)(2,1)S(1)}, u32[]{:S(2)}, u32[]{:S(2)}) collective-permute-start(bf16[256,2048]{1,0:T(8,128)(2,1)S(1)} %slice.88), channel_id=1, source_target_pairs={{0,8},{8,0},{16,24},{24,16},{1,9},{9,1},{17,25},{25,17},{2,10},{10... | collective-permute-start | bytes 3145736 | tf_op jit(solution)/shard_map/ppermute | solution.py:63
  202.9 23.4 %collective-permute-start.19 = (bf16[256,2048]{1,0:T(8,128)(2,1)S(1)}, bf16[256,2048]{1,0:T(8,128)(2,1)S(1)}, u32[]{:S(2)}, u32[]{:S(2)}) collective-permute-start(bf16[256,2048]{1,0:T(8,128)(2,1)S(1)} %slice.89), channel_id=1, source_target_pairs={{0,16},{8,24},{16,0},{24,8},{1,17},{9,25},{17,1},{25,9},{2,18},{10... | collective-permute-start | bytes 3145736 | tf_op jit(solution)/shard_map/ppermute | solution.py:63
  264.9 98.0 %all-gather.12.cloned.1.call-start = ((), (), s32[]{:S(2)}) async-start(), calls=%async_computation.9 | async-start | bytes 4718592 | tf_op jit(solution)/shard_map/all_gather | solution.py:93
  317.4 125.6 %reduce-scatter.9.cloned.1.call-start = ((), (), s32[]{:S(2)}) async-start(), calls=%async_computation.10 | async-start | bytes 4718592 | tf_op jit(solution)/shard_map/reduce_scatter | solution.py:97
  385.1 129.6 %all-gather.14.cloned.1.call-start = ((), (), s32[]{:S(2)}) async-start(), calls=%async_computation.11 | async-start | bytes 4718592 | tf_op jit(solution)/shard_map/all_gather | solution.py:93
  389.8 26.1 %collective-permute-start.21 = (bf16[2,256,1024]{2,1,0:T(8,128)(2,1)S(1)}, bf16[2,256,1024]{2,1,0:T(8,128)(2,1)S(1)}, u32[]{:S(2)}, u32[]{:S(2)}) collective-permute-start(bf16[2,256,1024]{2,1,0:T(8,128)(2,1)S(1)} %shard_map.237.refs_1_), channel_id=1, source_target_pairs={{0,16},{8,24},{16,0},{24,8},{1,17},{9,25},{17,1},{25,9},{2,18},{10... | collective-permute-start | bytes 3145736 | tf_op jit(solution)/shard_map/ppermute | solution.py:63
  394.4 26.1 %collective-permute-start.20 = (bf16[2,256,1024]{2,1,0:T(8,128)(2,1)S(1)}, bf16[2,256,1024]{2,1,0:T(8,128)(2,1)S(1)}, u32[]{:S(2)}, u32[]{:S(2)}) collective-permute-start(bf16[2,256,1024]{2,1,0:T(8,128)(2,1)S(1)} %shard_map.236.refs_0_), channel_id=1, source_target_pairs={{0,8},{8,0},{16,24},{24,16},{1,9},{9,1},{17,25},{25,17},{2,10},{10... | collective-permute-start | bytes 3145736 | tf_op jit(solution)/shard_map/ppermute | solution.py:63
  405.0 32.6 %collective-permute-start.23 = (bf16[2,256,1024]{2,1,0:T(8,128)(2,1)S(1)}, bf16[2,256,1024]{2,1,0:T(8,128)(2,1)S(1)}, u32[]{:S(2)}, u32[]{:S(2)}) collective-permute-start(bf16[2,256,1024]{2,1,0:T(8,128)(2,1)S(1)} %shard_map.240.refs_1_), channel_id=1, source_target_pairs={{0,16},{8,24},{16,0},{24,8},{1,17},{9,25},{17,1},{25,9},{2,18},{10... | collective-permute-start | bytes 3145736 | tf_op jit(solution)/shard_map/ppermute | solution.py:63
  408.8 33.2 %collective-permute-start.22 = (bf16[2,256,1024]{2,1,0:T(8,128)(2,1)S(1)}, bf16[2,256,1024]{2,1,0:T(8,128)(2,1)S(1)}, u32[]{:S(2)}, u32[]{:S(2)}) collective-permute-start(bf16[2,256,1024]{2,1,0:T(8,128)(2,1)S(1)} %shard_map.239.refs_0_), channel_id=1, source_target_pairs={{0,8},{8,0},{16,24},{24,16},{1,9},{9,1},{17,25},{25,17},{2,10},{10... | collective-permute-start | bytes 3145736 | tf_op jit(solution)/shard_map/ppermute | solution.py:63
  450.4 178.5 %reduce-scatter.11.cloned.1.call-start = ((), (), s32[]{:S(2)}) async-start(), calls=%async_computation.12 | async-start | bytes 4718592 | tf_op jit(solution)/shard_map/reduce_scatter | solution.py:97
  452.9 23.3 %collective-permute-start.24 = (bf16[256,1024]{1,0:T(8,128)(2,1)}, bf16[256,1024]{1,0:T(8,128)(2,1)}, u32[]{:S(2)}, u32[]{:S(2)}) collective-permute-start(bf16[256,1024]{1,0:T(8,128)(2,1)} %get-tuple-element.104), channel_id=1, source_target_pairs={{0,16},{8,24},{16,0},{24,8},{1,17},{9,25},{17,1},{25,9},{2,18},{10... | collective-permute-start | bytes 1572872 | tf_op jit(solution)/shard_map/ppermute | solution.py:63
  453.5 22.7 %collective-permute-start.25 = (bf16[256,1024]{1,0:T(8,128)(2,1)}, bf16[256,1024]{1,0:T(8,128)(2,1)}, u32[]{:S(2)}, u32[]{:S(2)}) collective-permute-start(bf16[256,1024]{1,0:T(8,128)(2,1)} %get-tuple-element.105), channel_id=1, source_target_pairs={{0,8},{8,0},{16,24},{24,16},{1,9},{9,1},{17,25},{25,17},{2,10},{10... | collective-permute-start | bytes 1572872 | tf_op jit(solution)/shard_map/ppermute | solution.py:63
  482.1 25.3 %collective-permute-start.33 = (bf16[2,128,2048]{2,1,0:T(8,128)(2,1)S(1)}, bf16[2,128,2048]{2,1,0:T(8,128)(2,1)S(1)}, u32[]{:S(2)}, u32[]{:S(2)}) collective-permute-start(bf16[2,128,2048]{2,1,0:T(8,128)(2,1)S(1)} %copy-done.23), channel_id=1, source_target_pairs={{0,16},{8,24},{16,0},{24,8},{1,17},{9,25},{17,1},{25,9},{2,18},{10... | collective-permute-start | bytes 3145736 | tf_op jit(solution)/shard_map/ppermute | solution.py:63
  483.0 25.0 %collective-permute-start.32 = (bf16[2,128,2048]{2,1,0:T(8,128)(2,1)S(1)}, bf16[2,128,2048]{2,1,0:T(8,128)(2,1)S(1)}, u32[]{:S(2)}, u32[]{:S(2)}) collective-permute-start(bf16[2,128,2048]{2,1,0:T(8,128)(2,1)S(1)} %shard_map.244.refs_5_.refs_0_), channel_id=1, source_target_pairs={{0,8},{8,0},{16,24},{24,16},{1,9},{9,1},{17,25},{25,17},{2,10},{10... | collective-permute-start | bytes 3145736 | tf_op jit(solution)/shard_map/ppermute | solution.py:63
  485.8 47.5 %collective-permute-start.29 = (bf16[2,64,2048]{2,1,0:T(8,128)(2,1)}, bf16[2,64,2048]{2,1,0:T(8,128)(2,1)S(1)}, u32[]{:S(2)}, u32[]{:S(2)}) collective-permute-start(bf16[2,64,2048]{2,1,0:T(8,128)(2,1)} %get-tuple-element.114.refs_12_.refs_6_), channel_id=1, source_target_pairs={{0,6},{1,7},{2,0},{3,1},{4,2},{5,3},{6,4},{7,5},{8,14},{9,15},{10,... | collective-permute-start | bytes 1572872 | tf_op jit(solution)/shard_map/ppermute | solution.py:55
  487.3 51.8 %collective-permute-start.30 = (bf16[2,64,2048]{2,1,0:T(8,128)(2,1)}, bf16[2,64,2048]{2,1,0:T(8,128)(2,1)S(1)}, u32[]{:S(2)}, u32[]{:S(2)}) collective-permute-start(bf16[2,64,2048]{2,1,0:T(8,128)(2,1)} %get-tuple-element.113.refs_11_.refs_5_), channel_id=1, source_target_pairs={{0,4},{1,5},{2,6},{3,7},{4,0},{5,1},{6,2},{7,3},{8,12},{9,13},{10,... | collective-permute-start | bytes 1572872 | tf_op jit(solution)/shard_map/ppermute | solution.py:55
  487.7 51.3 %collective-permute-start.31 = (bf16[2,64,2048]{2,1,0:T(8,128)(2,1)}, bf16[2,64,2048]{2,1,0:T(8,128)(2,1)S(1)}, u32[]{:S(2)}, u32[]{:S(2)}) collective-permute-start(bf16[2,64,2048]{2,1,0:T(8,128)(2,1)} %get-tuple-element.112.refs_10_.refs_4_), channel_id=1, source_target_pairs={{0,2},{1,3},{2,4},{3,5},{4,6},{5,7},{6,0},{7,1},{8,10},{9,11},{10,... | collective-permute-start | bytes 1572872 | tf_op jit(solution)/shard_map/ppermute | solution.py:55
  556.4 24.3 %collective-permute-start.44 = (bf16[2,256,768]{2,1,0:T(8,128)(2,1)}, bf16[2,256,768]{2,1,0:T(8,128)(2,1)}, u32[]{:S(2)}, u32[]{:S(2)}) collective-permute-start(bf16[2,256,768]{2,1,0:T(8,128)(2,1)} %shard_map.256.refs_1_), channel_id=1, source_target_pairs={{0,16},{8,24},{16,0},{24,8},{1,17},{9,25},{17,1},{25,9},{2,18},{10... | collective-permute-start | bytes 2359304 | tf_op jit(solution)/shard_map/ppermute | solution.py:63
  (134 other events, 1139.4 us)
Sparse Core Ops, SparseCore 0:
  9.9 34.6 all-gather.5
  47.5 63.7 all-gather.7
  143.4 50.1 reduce-scatter.4
  199.4 44.6 all-gather.9
  265.0 48.7 reduce-scatter.6
  317.5 45.2 all-gather.11
  385.2 48.7 reduce-scatter.8
  450.6 47.7 all-gather.13
  550.5 49.1 reduce-scatter.10

commit v6 on v5

--- a/solution.py
+++ b/solution.py
@@ -714,36 +714,30 @@
 
 def rows_back(columns, weight, first=()):
     inner, length = columns.shape
+    rows = columns.T
     width = weight.shape[0]
     block = 512
 
-    def kernel(columns_ref, weight_ref, *refs):
-        out_ref, rows_ref = refs[-2:]
-
-        @pl.when(pl.program_id(0) == 0)
-        def _():
-            rows_ref[...] = columns_ref[...].T
-
-        out_ref[...] = against(rows_ref[...], weight_ref[...]).astype(BF)
+    def kernel(rows_ref, weight_ref, *refs):
+        refs[-1][...] = against(rows_ref[...], weight_ref[...]).astype(BF)
 
     return pl.pallas_call(
         kernel,
         grid=(width // block,),
         out_shape=jax.ShapeDtypeStruct((length, width), BF),
         in_specs=[
-            pl.BlockSpec((inner, length), lambda j: (0, 0)),
+            pl.BlockSpec((length, inner), lambda j: (0, 0)),
             pl.BlockSpec((block, inner), lambda j: (j, 0)),
         ]
         + [pl.BlockSpec(memory_space=pl.ANY)] * len(first),
         out_specs=pl.BlockSpec((length, block), lambda j: (0, j)),
-        scratch_shapes=[pltpu.VMEM((length, inner), BF)],
         compiler_params=pltpu.CompilerParams(vmem_limit_bytes=48 * 2**20),
         cost_estimate=pl.CostEstimate(
             flops=2 * length * width * inner,
             bytes_accessed=2 * (length * (width + inner) + width * inner),
             transcendentals=0,
         ),
-    )(columns, weight, *first)
+    )(rows, weight, *first)
 
 
 def flip():

time: 655 us -> 654 us (level)
    unnamed x205 -> x197, local copies, waits for them, and re-layouts: 50.2 us -> 48.9 us
where the time goes in v6:
time: 654 us; the launch traced here: 649 us
  waiting for transfers between devices  288 us (44%)
  Pallas kernels  188 us (29%)
  starting transfers between devices  61.3 us (9%)
  local copies, waits for them, and re-layouts  60.1 us (9%)
  between operations  18.2 us (3%)
  matrix products  18.1 us (3%)
  other arithmetic  14.8 us (2%)
    ppermute x32, waiting for transfers between devices, beside(): lax.ppermute(value, 'fsdp', [(f, f ^ bit) for f in range(lax.axis_size('f...  126 us
    all_gather x4, waiting for transfers between devices, gather_rows(): return lax.all_gather(local, 'seq', axis=0, tiled=True)  74.2 us
    pallas_call x30, Pallas kernels, move(): pl.pallas_call(lambda *refs: kernel(*refs[:given], *refs[given + len(firs...  53.3 us
    pallas_call x12, Pallas kernels, weight_terms(): pl.pallas_call(kernel, grid_spec=pltpu.PrefetchScalarGridSpec(num_scalar_...  51.7 us
    unnamed x197, local copies, waits for them, and re-layouts  48.9 us
    reduce_scatter x4, waiting for transfers between devices, scatter_rows(): return lax.psum_scatter(partial, 'seq', scatter_dimension=0, tiled=True)  45.9 us
    ppermute x32, starting transfers between devices, beside(): lax.ppermute(value, 'fsdp', [(f, f ^ bit) for f in range(lax.axis_size('f...  37.1 us
    ppermute x15, waiting for transfers between devices, turn(): lax.ppermute(value, 'seq', [(s, (s - 2 * steps) % size) for s in range(si...  34.8 us
  transfers between devices with their start and end apart: 64, of which 26 were waited for; matrix products, arithmetic and copies ran while one was open for 6% of the time, Pallas kernels for 20%

profile of v6, /device:TPU:0, one launch (start us, length us, event | category | flops | bytes accessed | tf_op | source)
XLA Modules:
  0.0 648.9 jit_solution(267140170566051302)
XLA Ops:
  28.0 4.2 collective-permute-done.1.refs_2_.refs_1_
  32.2 13.7 %collective-permute-done.2.refs_3_.refs_2_ = bf16[2,64,896]{2,1,0:T(8,128)(2,1)S(1)} collective-permute-done((bf16[2,64,896]{2,1,0:T(8,128)(2,1)S(1)}, bf16[2,64,896]{2,1,0:T(8,128)(2,1)S(1)}, u32[]{:S(2)}, u32[]{:S(2)}) %collective-permute-start.2) | collective-permute-done | bytes 229408 | tf_op jit(solution)/shard_map/ppermute | solution.py:55
  56.5 17.1 %collective-permute-done.5.refs_3_ = bf16[512,896]{1,0:T(8,128)(2,1)S(1)} collective-permute-done((bf16[512,896]{1,0:T(8,128)(2,1)S(1)}, bf16[512,896]{1,0:T(8,128)(2,1)S(1)}, u32[]{:S(2)}, u32[]{:S(2)}) %collective-permute-start.5) | collective-permute-done | bytes 917536 | tf_op jit(solution)/shard_map/ppermute | solution.py:63
  93.5 17.8 %all-gather.8.cloned.1.call-done.row_ref = bf16[1024,2048]{1,0:T(8,128)(2,1)} async-done(((bf16[128,2048]{1,0:T(8,128)(2,1)}), bf16[1024,2048]{1,0:T(8,128)(2,1)}) %all-gather.8.cloned.1.call-update) | async-done | bytes 4194320 | tf_op jit(solution)/shard_map/all_gather | solution.py:93
  116.8 5.2 fusion.3.refs_0_.refs_1_.refs_2_
  122.8 12.2 %shard_map.227 = (bf16[256,1024]{1,0:T(8,128)(2,1)}, bf16[256,1024]{1,0:T(8,128)(2,1)}, bf16[256,1024]{1,0:T(8,128)(2,1)}, bf16[256,1024]{1,0:T(8,128)(2,1)}, f32[4,1,1024]{2,1,0:T(1,128)}) custom-call(f32[768,1024]{1,0:T(8,128)} %fusion.3.refs_0_.refs_1_.refs_2_, f32[768,1024]{1,0:T(8,128)} %fusion.3.refs_0_.refs_1_.refs_2_, ...), custom_call_target="tpu_custom_call" | custom-call | flops 1073741824 | bytes 6291456 | tf_op jit(solution)/shard_map/pallas_call | solution.py:484
  138.4 4.8 convolution_convert_fusion
  149.2 44.5 %collective-permute-done.17.refs_5_.refs_3_ = bf16[512,2048]{1,0:T(8,128)(2,1)} collective-permute-done((bf16[512,2048]{1,0:T(8,128)(2,1)}, bf16[512,2048]{1,0:T(8,128)(2,1)}, u32[]{:S(2)}, u32[]{:S(2)}) %collective-permute-start.17) | collective-permute-done | bytes 2097184 | tf_op jit(solution)/shard_map/ppermute | solution.py:63
  206.9 18.0 %collective-permute-done.18.refs_4_ = bf16[256,2048]{1,0:T(8,128)(2,1)S(1)} collective-permute-done((bf16[256,2048]{1,0:T(8,128)(2,1)S(1)}, bf16[256,2048]{1,0:T(8,128)(2,1)S(1)}, u32[]{:S(2)}, u32[]{:S(2)}) %collective-permute-start.18) | collective-permute-done | bytes 1048608 | tf_op jit(solution)/shard_map/ppermute | solution.py:63
  226.3 6.9 %shard_map.231 = bf16[4,512,2048]{2,1,0:T(8,128)(2,1)} custom-call(s32[1]{0:T(128)} %constant.170.clone.1.refs_0_, bf16[512,2048]{1,0:T(8,128)(2,1)} %bitcast.12.refs_1_, bf16[512,2048]{1,0:T(8,128)(2,1)} %copy-done.10, bf16[512,2048]{1,0:T(8,128)(2,1)} %collective-permute-done.17.refs_5_.refs_3_, bf16[256,2048]{1,0:T(8,128)(2,1)S(1)} %collective-permute-done.18.refs_4_, ...), custom_call_target="tpu_custom_call" | custom-call | bytes 25165836 | tf_op jit(solution)/shard_map/pallas_call | solution.py:105
  233.2 10.9 %all-gather.10.cloned.1.call-done.x_ref.rows_ref = bf16[1024,2048]{1,0:T(8,128)(2,1)} async-done(((bf16[128,2048]{1,0:T(8,128)(2,1)}), bf16[1024,2048]{1,0:T(8,128)(2,1)}) %all-gather.10.cloned.1.call-update) | async-done | bytes 4194320 | tf_op jit(solution)/shard_map/all_gather | solution.py:93
  244.1 20.7 %shard_map.233 = (f32[1024,1024]{1,0:T(8,128)}, f32[1024,1024]{1,0:T(8,128)}, bf16[1024,1024]{1,0:T(8,128)(2,1)}, bf16[1024,2048]{1,0:T(8,128)(2,1)}) custom-call(bf16[1024,2048]{1,0:T(8,128)(2,1)} %all-gather.10.cloned.1.call-done.x_ref.rows_ref, bf16[2048,2048]{1,0:T(8,128)(2,1)} %bitcast.105, bf16[2048,2048]{1,0:T(8,128)(2,1)} %bitcast.106, ...), custom_call_target="tpu_custom_call" | custom-call | flops 12884901888 | bytes 33554432 | tf_op jit(solution)/shard_map/pallas_call | solution.py:637
  267.8 45.9 %reduce-scatter.7.cloned.1.call-done.refs_0_ = bf16[128,2048]{1,0:T(8,128)(2,1)} async-done(((bf16[1024,2048]{1,0:T(8,128)(2,1)}), bf16[128,2048]{1,0:T(8,128)(2,1)}) %reduce-scatter.7.cloned.1.call-update) | async-done | bytes 524304 | tf_op jit(solution)/shard_map/reduce_scatter | solution.py:97
  317.4 45.4 %all-gather.12.cloned.1.call-done.g_ref.grads_ref = bf16[1024,2048]{1,0:T(8,128)(2,1)} async-done(((bf16[128,2048]{1,0:T(8,128)(2,1)}), bf16[1024,2048]{1,0:T(8,128)(2,1)}) %all-gather.12.cloned.1.call-update) | async-done | bytes 4194320 | tf_op jit(solution)/shard_map/all_gather | solution.py:93
  362.8 22.3 %shard_map.235 = (bf16[1024,1024]{1,0:T(8,128)(2,1)}, bf16[1024,1024]{1,0:T(8,128)(2,1)}, bf16[1024,2048]{1,0:T(8,128)(2,1)}) custom-call(bf16[1024,2048]{1,0:T(8,128)(2,1)} %all-gather.12.cloned.1.call-done.g_ref.grads_ref, f32[1024,1024]{1,0:T(8,128)} %get-tuple-element.93.gate_ref, f32[1024,1024]{1,0:T(8,128)} %get-tuple-element.94.up_ref, ...), custom_call_target="tpu_custom_call" | custom-call | flops 12884901888 | bytes 33554432 | tf_op jit(solution)/shard_map/pallas_call | solution.py:693
  396.0 5.7 shard_map.238.refs_0_
  409.4 6.4 collective-permute-done.21.refs_3_.refs_2_
  415.8 4.7 collective-permute-done.20.refs_2_.refs_1_
  420.5 6.7 %shard_map.241.refs_5_.refs_0_ = bf16[4,256,1024]{2,1,0:T(8,128)(2,1)} custom-call(s32[4]{0:T(128)S(1)} %copy-done.89, bf16[1024,2048]{1,0:T(8,128)(2,1)} %all-gather.10.cloned.1.call-done.x_ref.rows_ref, bf16[1024,1024]{1,0:T(8,128)(2,1)} %get-tuple-element.97.grads_ref, bf16[2,256,1024]{2,1,0:T(8,128)(2,1)S(1)} %shard_map.239.refs_0_, ...), custom_call_target="tpu_custom_call" | custom-call | flops 2147483648 | bytes 4194304 | tf_op jit(solution)/shard_map/pallas_call | solution.py:323
  427.2 10.4 %collective-permute-done.23.refs_7_.refs_2_ = bf16[2,256,1024]{2,1,0:T(8,128)(2,1)S(1)} collective-permute-done((bf16[2,256,1024]{2,1,0:T(8,128)(2,1)S(1)}, bf16[2,256,1024]{2,1,0:T(8,128)(2,1)S(1)}, u32[]{:S(2)}, u32[]{:S(2)}) %collective-permute-start.23) | collective-permute-done | bytes 1048608 | tf_op jit(solution)/shard_map/ppermute | solution.py:63
  459.9 4.4 shard_map.245.refs_6_.refs_1_
  464.3 4.3 shard_map.244.refs_5_.refs_0_
  468.6 6.2 shard_map.248.refs_5_.refs_0_
  489.1 18.3 %collective-permute-done.33.refs_2_ = bf16[2,128,2048]{2,1,0:T(8,128)(2,1)S(1)} collective-permute-done((bf16[2,128,2048]{2,1,0:T(8,128)(2,1)S(1)}, bf16[2,128,2048]{2,1,0:T(8,128)(2,1)S(1)}, u32[]{:S(2)}, u32[]{:S(2)}) %collective-permute-start.33) | collective-permute-done | bytes 1048608 | tf_op jit(solution)/shard_map/ppermute | solution.py:63
  514.7 4.3 fusion.5.refs_0_
  518.9 13.9 %shard_map.252 = bf16[3,256,1024]{2,1,0:T(8,128)(2,1)} custom-call(bf16[256,1024]{1,0:T(8,128)(2,1)} %fusion.5.refs_0_, bf16[256,1024]{1,0:T(8,128)(2,1)} %get-tuple-element.100.refs_1_, bf16[256,1024]{1,0:T(8,128)(2,1)} %get-tuple-element.101.refs_2_, bf16[256,1024]{1,0:T(8,128)(2,1)} %get-tuple-element.102.refs_3_, ...), custom_call_target="tpu_custom_call" | custom-call | flops 2684354560 | bytes 6291456 | tf_op jit(solution)/shard_map/pallas_call | solution.py:550
  534.6 4.4 collective-permute-done.30.refs_1_.refs_3_
  539.0 6.8 %shard_map.254.refs_0_.grad_ref = bf16[1024,2048]{1,0:T(8,128)(2,1)} custom-call(bf16[1024,768]{1,0:T(8,128)(2,1)S(1)} %copy.54.rows_ref, bf16[2048,896]{1,0:T(8,128)(2,1)} %bitcast.103, bf16[2,64,2048]{2,1,0:T(8,128)(2,1)S(1)} %collective-permute-done.29.refs_0_.refs_2_, bf16[2,64,2048]{2,1,0:T(8,128)(2,1)S(1)} %collective-permute-done.30.refs_1_.refs_3_, ...), custom_call_target="tpu_custom_call" | custom-call | flops 3221225472 | bytes 8912896 | tf_op jit(solution)/shard_map/pallas_call | solution.py:724
  560.8 7.3 %shard_map.257 = f32[1,2048]{1,0:T(1,128)} custom-call(bf16[1024,2048]{1,0:T(8,128)(2,1)} %shard_map.254.refs_0_.grad_ref, bf16[1024,2048]{1,0:T(8,128)(2,1)} %all-gather.8.cloned.1.call-done.row_ref, f32[1024,1]{1,0:T(8,128)} %copy.55.scale_ref, bf16[2,256,768]{2,1,0:T(8,128)(2,1)} %shard_map.255.refs_0_, bf16[2,256,768]{2,1,0:T(8,128)(2,1)} %shard_map.256.refs_1_), custom_call_target="tpu_custom_call" | custom-call | flops 8388608 | bytes 8388608 | tf_op jit(solution)/shard_map/pallas_call | solution.py:594
  568.9 4.6 shard_map.259.refs_2_.refs_0_
  587.6 5.4 collective-permute-done.36
  607.1 4.5 collective-permute-done.42
  (416 shorter events, 222.7 us)
Async XLA Ops:
  7.2 38.8 %all-gather.6.cloned.1.call-start = ((), (), s32[]{:S(2)}) async-start(), calls=%async_computation.4 | async-start | bytes 1310720 | tf_op jit(solution)/shard_map/all_gather | solution.py:929
  7.9 103.4 %all-gather.8.cloned.1.call-start = ((), (), s32[]{:S(2)}) async-start(), calls=%async_computation.5 | async-start | bytes 4718592 | tf_op jit(solution)/shard_map/all_gather | solution.py:93
  8.0 38.0 %collective-permute-start.8 = (bf16[256,2048]{1,0:T(8,128)(2,1)}, bf16[256,2048]{1,0:T(8,128)(2,1)S(1)}, u32[]{:S(2)}, u32[]{:S(2)}) collective-permute-start(bf16[256,2048]{1,0:T(8,128)(2,1)} %refs_1_.5), channel_id=1, source_target_pairs={{0,8},{8,0},{16,24},{24,16},{1,9},{9,1},{17,25},{25,17},{2,10},{10... | collective-permute-start | bytes 3145736 | tf_op jit(solution)/shard_map/ppermute | solution.py:63
  11.0 35.0 %collective-permute-start.9 = (bf16[256,2048]{1,0:T(8,128)(2,1)}, bf16[256,2048]{1,0:T(8,128)(2,1)S(1)}, u32[]{:S(2)}, u32[]{:S(2)}) collective-permute-start(bf16[256,2048]{1,0:T(8,128)(2,1)} %refs_1_.5), channel_id=1, source_target_pairs={{0,16},{8,24},{16,0},{24,8},{1,17},{9,25},{17,1},{25,9},{2,18},{10... | collective-permute-start | bytes 3145736 | tf_op jit(solution)/shard_map/ppermute | solution.py:63
  47.4 147.2 %reduce-scatter.5.cloned.1.call-start = ((), (), s32[]{:S(2)}) async-start(), calls=%async_computation.6 | async-start | bytes 4718592 | tf_op jit(solution)/shard_map/reduce_scatter | solution.py:97
  78.0 44.0 %collective-permute-start.11 = (bf16[2,64,2048]{2,1,0:T(8,128)(2,1)}, bf16[2,64,2048]{2,1,0:T(8,128)(2,1)S(1)}, u32[]{:S(2)}, u32[]{:S(2)}) collective-permute-start(bf16[2,64,2048]{2,1,0:T(8,128)(2,1)} %get-tuple-element.83), channel_id=1, source_target_pairs={{0,2},{1,3},{2,4},{3,5},{4,6},{5,7},{6,0},{7,1},{8,10},{9,11},{10,... | collective-permute-start | bytes 1572872 | tf_op jit(solution)/shard_map/ppermute | solution.py:55
  78.7 56.2 %collective-permute-start.12 = (bf16[2,64,2048]{2,1,0:T(8,128)(2,1)}, bf16[2,64,2048]{2,1,0:T(8,128)(2,1)}, u32[]{:S(2)}, u32[]{:S(2)}) collective-permute-start(bf16[2,64,2048]{2,1,0:T(8,128)(2,1)} %get-tuple-element.85), channel_id=1, source_target_pairs={{0,6},{1,7},{2,0},{3,1},{4,2},{5,3},{6,4},{7,5},{8,14},{9,15},{10,... | collective-permute-start | bytes 1572872 | tf_op jit(solution)/shard_map/ppermute | solution.py:55
  81.9 55.7 %collective-permute-start.13 = (bf16[2,64,2048]{2,1,0:T(8,128)(2,1)}, bf16[2,64,2048]{2,1,0:T(8,128)(2,1)}, u32[]{:S(2)}, u32[]{:S(2)}) collective-permute-start(bf16[2,64,2048]{2,1,0:T(8,128)(2,1)} %get-tuple-element.86), channel_id=1, source_target_pairs={{0,4},{1,5},{2,6},{3,7},{4,0},{5,1},{6,2},{7,3},{8,12},{9,13},{10,... | collective-permute-start | bytes 1572872 | tf_op jit(solution)/shard_map/ppermute | solution.py:55
  84.6 53.0 %collective-permute-start.14 = (bf16[128,2048]{1,0:T(8,128)(2,1)}, bf16[128,2048]{1,0:T(8,128)(2,1)S(1)}, u32[]{:S(2)}, u32[]{:S(2)}) collective-permute-start(bf16[128,2048]{1,0:T(8,128)(2,1)} %slice.84), channel_id=1, source_target_pairs={{0,8},{8,0},{16,24},{24,16},{1,9},{9,1},{17,25},{25,17},{2,10},{10... | collective-permute-start | bytes 1572872 | tf_op jit(solution)/shard_map/ppermute | solution.py:63
  85.5 52.1 %collective-permute-start.15 = (bf16[128,2048]{1,0:T(8,128)(2,1)}, bf16[128,2048]{1,0:T(8,128)(2,1)}, u32[]{:S(2)}, u32[]{:S(2)}) collective-permute-start(bf16[128,2048]{1,0:T(8,128)(2,1)} %slice.85), channel_id=1, source_target_pairs={{0,16},{8,24},{16,0},{24,8},{1,17},{9,25},{17,1},{25,9},{2,18},{10... | collective-permute-start | bytes 1572872 | tf_op jit(solution)/shard_map/ppermute | solution.py:63
  143.3 100.9 %all-gather.10.cloned.1.call-start = ((), (), s32[]{:S(2)}) async-start(), calls=%async_computation.7 | async-start | bytes 4718592 | tf_op jit(solution)/shard_map/all_gather | solution.py:93
  146.0 47.7 %collective-permute-start.17 = (bf16[512,2048]{1,0:T(8,128)(2,1)}, bf16[512,2048]{1,0:T(8,128)(2,1)}, u32[]{:S(2)}, u32[]{:S(2)}) collective-permute-start(bf16[512,2048]{1,0:T(8,128)(2,1)} %bitcast.12.refs_1_), channel_id=1, source_target_pairs={{0,16},{8,24},{16,0},{24,8},{1,17},{9,25},{17,1},{25,9},{2,18},{10... | collective-permute-start | bytes 6291464 | tf_op jit(solution)/shard_map/ppermute | solution.py:63
  147.5 47.1 %collective-permute-start.16 = (bf16[512,2048]{1,0:T(8,128)(2,1)}, bf16[512,2048]{1,0:T(8,128)(2,1)S(1)}, u32[]{:S(2)}, u32[]{:S(2)}) collective-permute-start(bf16[512,2048]{1,0:T(8,128)(2,1)} %bitcast.12.refs_1_), channel_id=1, source_target_pairs={{0,8},{8,0},{16,24},{24,16},{1,9},{9,1},{17,25},{25,17},{2,10},{10... | collective-permute-start | bytes 6291464 | tf_op jit(solution)/shard_map/ppermute | solution.py:63
  199.3 114.4 %reduce-scatter.7.cloned.1.call-start = ((), (), s32[]{:S(2)}) async-start(), calls=%async_computation.8 | async-start | bytes 4718592 | tf_op jit(solution)/shard_map/reduce_scatter | solution.py:97
  201.3 23.7 %collective-permute-start.18 = (bf16[256,2048]{1,0:T(8,128)(2,1)S(1)}, bf16[256,2048]{1,0:T(8,128)(2,1)S(1)}, u32[]{:S(2)}, u32[]{:S(2)}) collective-permute-start(bf16[256,2048]{1,0:T(8,128)(2,1)S(1)} %slice.88), channel_id=1, source_target_pairs={{0,8},{8,0},{16,24},{24,16},{1,9},{9,1},{17,25},{25,17},{2,10},{10... | collective-permute-start | bytes 3145736 | tf_op jit(solution)/shard_map/ppermute | solution.py:63
  202.9 23.4 %collective-permute-start.19 = (bf16[256,2048]{1,0:T(8,128)(2,1)S(1)}, bf16[256,2048]{1,0:T(8,128)(2,1)S(1)}, u32[]{:S(2)}, u32[]{:S(2)}) collective-permute-start(bf16[256,2048]{1,0:T(8,128)(2,1)S(1)} %slice.89), channel_id=1, source_target_pairs={{0,16},{8,24},{16,0},{24,8},{1,17},{9,25},{17,1},{25,9},{2,18},{10... | collective-permute-start | bytes 3145736 | tf_op jit(solution)/shard_map/ppermute | solution.py:63
  264.8 98.0 %all-gather.12.cloned.1.call-start = ((), (), s32[]{:S(2)}) async-start(), calls=%async_computation.9 | async-start | bytes 4718592 | tf_op jit(solution)/shard_map/all_gather | solution.py:93
  317.4 125.6 %reduce-scatter.9.cloned.1.call-start = ((), (), s32[]{:S(2)}) async-start(), calls=%async_computation.10 | async-start | bytes 4718592 | tf_op jit(solution)/shard_map/reduce_scatter | solution.py:97
  385.1 129.6 %all-gather.14.cloned.1.call-start = ((), (), s32[]{:S(2)}) async-start(), calls=%async_computation.11 | async-start | bytes 4718592 | tf_op jit(solution)/shard_map/all_gather | solution.py:93
  389.8 26.1 %collective-permute-start.21 = (bf16[2,256,1024]{2,1,0:T(8,128)(2,1)S(1)}, bf16[2,256,1024]{2,1,0:T(8,128)(2,1)S(1)}, u32[]{:S(2)}, u32[]{:S(2)}) collective-permute-start(bf16[2,256,1024]{2,1,0:T(8,128)(2,1)S(1)} %shard_map.237.refs_1_), channel_id=1, source_target_pairs={{0,16},{8,24},{16,0},{24,8},{1,17},{9,25},{17,1},{25,9},{2,18},{10... | collective-permute-start | bytes 3145736 | tf_op jit(solution)/shard_map/ppermute | solution.py:63
  394.4 26.1 %collective-permute-start.20 = (bf16[2,256,1024]{2,1,0:T(8,128)(2,1)S(1)}, bf16[2,256,1024]{2,1,0:T(8,128)(2,1)S(1)}, u32[]{:S(2)}, u32[]{:S(2)}) collective-permute-start(bf16[2,256,1024]{2,1,0:T(8,128)(2,1)S(1)} %shard_map.236.refs_0_), channel_id=1, source_target_pairs={{0,8},{8,0},{16,24},{24,16},{1,9},{9,1},{17,25},{25,17},{2,10},{10... | collective-permute-start | bytes 3145736 | tf_op jit(solution)/shard_map/ppermute | solution.py:63
  405.0 32.6 %collective-permute-start.23 = (bf16[2,256,1024]{2,1,0:T(8,128)(2,1)S(1)}, bf16[2,256,1024]{2,1,0:T(8,128)(2,1)S(1)}, u32[]{:S(2)}, u32[]{:S(2)}) collective-permute-start(bf16[2,256,1024]{2,1,0:T(8,128)(2,1)S(1)} %shard_map.240.refs_1_), channel_id=1, source_target_pairs={{0,16},{8,24},{16,0},{24,8},{1,17},{9,25},{17,1},{25,9},{2,18},{10... | collective-permute-start | bytes 3145736 | tf_op jit(solution)/shard_map/ppermute | solution.py:63
  408.8 33.2 %collective-permute-start.22 = (bf16[2,256,1024]{2,1,0:T(8,128)(2,1)S(1)}, bf16[2,256,1024]{2,1,0:T(8,128)(2,1)S(1)}, u32[]{:S(2)}, u32[]{:S(2)}) collective-permute-start(bf16[2,256,1024]{2,1,0:T(8,128)(2,1)S(1)} %shard_map.239.refs_0_), channel_id=1, source_target_pairs={{0,8},{8,0},{16,24},{24,16},{1,9},{9,1},{17,25},{25,17},{2,10},{10... | collective-permute-start | bytes 3145736 | tf_op jit(solution)/shard_map/ppermute | solution.py:63
  450.4 178.2 %reduce-scatter.11.cloned.1.call-start = ((), (), s32[]{:S(2)}) async-start(), calls=%async_computation.12 | async-start | bytes 4718592 | tf_op jit(solution)/shard_map/reduce_scatter | solution.py:97
  452.9 23.3 %collective-permute-start.24 = (bf16[256,1024]{1,0:T(8,128)(2,1)}, bf16[256,1024]{1,0:T(8,128)(2,1)}, u32[]{:S(2)}, u32[]{:S(2)}) collective-permute-start(bf16[256,1024]{1,0:T(8,128)(2,1)} %get-tuple-element.104), channel_id=1, source_target_pairs={{0,16},{8,24},{16,0},{24,8},{1,17},{9,25},{17,1},{25,9},{2,18},{10... | collective-permute-start | bytes 1572872 | tf_op jit(solution)/shard_map/ppermute | solution.py:63
  453.4 22.7 %collective-permute-start.25 = (bf16[256,1024]{1,0:T(8,128)(2,1)}, bf16[256,1024]{1,0:T(8,128)(2,1)}, u32[]{:S(2)}, u32[]{:S(2)}) collective-permute-start(bf16[256,1024]{1,0:T(8,128)(2,1)} %get-tuple-element.105), channel_id=1, source_target_pairs={{0,8},{8,0},{16,24},{24,16},{1,9},{9,1},{17,25},{25,17},{2,10},{10... | collective-permute-start | bytes 1572872 | tf_op jit(solution)/shard_map/ppermute | solution.py:63
  482.1 25.3 %collective-permute-start.33 = (bf16[2,128,2048]{2,1,0:T(8,128)(2,1)S(1)}, bf16[2,128,2048]{2,1,0:T(8,128)(2,1)S(1)}, u32[]{:S(2)}, u32[]{:S(2)}) collective-permute-start(bf16[2,128,2048]{2,1,0:T(8,128)(2,1)S(1)} %copy-done.22), channel_id=1, source_target_pairs={{0,16},{8,24},{16,0},{24,8},{1,17},{9,25},{17,1},{25,9},{2,18},{10... | collective-permute-start | bytes 3145736 | tf_op jit(solution)/shard_map/ppermute | solution.py:63
  483.0 25.0 %collective-permute-start.32 = (bf16[2,128,2048]{2,1,0:T(8,128)(2,1)S(1)}, bf16[2,128,2048]{2,1,0:T(8,128)(2,1)S(1)}, u32[]{:S(2)}, u32[]{:S(2)}) collective-permute-start(bf16[2,128,2048]{2,1,0:T(8,128)(2,1)S(1)} %shard_map.244.refs_5_.refs_0_), channel_id=1, source_target_pairs={{0,8},{8,0},{16,24},{24,16},{1,9},{9,1},{17,25},{25,17},{2,10},{10... | collective-permute-start | bytes 3145736 | tf_op jit(solution)/shard_map/ppermute | solution.py:63
  485.7 48.9 %collective-permute-start.29 = (bf16[2,64,2048]{2,1,0:T(8,128)(2,1)}, bf16[2,64,2048]{2,1,0:T(8,128)(2,1)S(1)}, u32[]{:S(2)}, u32[]{:S(2)}) collective-permute-start(bf16[2,64,2048]{2,1,0:T(8,128)(2,1)} %get-tuple-element.114.refs_12_.refs_6_), channel_id=1, source_target_pairs={{0,6},{1,7},{2,0},{3,1},{4,2},{5,3},{6,4},{7,5},{8,14},{9,15},{10,... | collective-permute-start | bytes 1572872 | tf_op jit(solution)/shard_map/ppermute | solution.py:55
  487.2 51.8 %collective-permute-start.30 = (bf16[2,64,2048]{2,1,0:T(8,128)(2,1)}, bf16[2,64,2048]{2,1,0:T(8,128)(2,1)S(1)}, u32[]{:S(2)}, u32[]{:S(2)}) collective-permute-start(bf16[2,64,2048]{2,1,0:T(8,128)(2,1)} %get-tuple-element.113.refs_11_.refs_5_), channel_id=1, source_target_pairs={{0,4},{1,5},{2,6},{3,7},{4,0},{5,1},{6,2},{7,3},{8,12},{9,13},{10,... | collective-permute-start | bytes 1572872 | tf_op jit(solution)/shard_map/ppermute | solution.py:55
  487.7 51.4 %collective-permute-start.31 = (bf16[2,64,2048]{2,1,0:T(8,128)(2,1)}, bf16[2,64,2048]{2,1,0:T(8,128)(2,1)S(1)}, u32[]{:S(2)}, u32[]{:S(2)}) collective-permute-start(bf16[2,64,2048]{2,1,0:T(8,128)(2,1)} %get-tuple-element.112.refs_10_.refs_4_), channel_id=1, source_target_pairs={{0,2},{1,3},{2,4},{3,5},{4,6},{5,7},{6,0},{7,1},{8,10},{9,11},{10,... | collective-permute-start | bytes 1572872 | tf_op jit(solution)/shard_map/ppermute | solution.py:55
  554.3 24.3 %collective-permute-start.44 = (bf16[2,256,768]{2,1,0:T(8,128)(2,1)}, bf16[2,256,768]{2,1,0:T(8,128)(2,1)}, u32[]{:S(2)}, u32[]{:S(2)}) collective-permute-start(bf16[2,256,768]{2,1,0:T(8,128)(2,1)} %shard_map.256.refs_1_), channel_id=1, source_target_pairs={{0,16},{8,24},{16,0},{24,8},{1,17},{9,25},{17,1},{25,9},{2,18},{10... | collective-permute-start | bytes 2359304 | tf_op jit(solution)/shard_map/ppermute | solution.py:63
  (130 other events, 1134.6 us)
Sparse Core Ops, SparseCore 0:
  9.9 34.6 all-gather.5
  47.5 63.7 all-gather.7
  143.4 50.1 reduce-scatter.4
  199.4 44.6 all-gather.9
  265.0 48.7 reduce-scatter.6
  317.5 45.2 all-gather.11
  385.2 48.7 reduce-scatter.8
  450.6 47.7 all-gather.13
  548.4 50.3 reduce-scatter.10
